TPU v7x, 32 devices: a whole 2x2x4 slice. The times are simulated.
32 devices in a mesh: dp: 8 (over z, x), mp: 4 (over y, core).
Axes of the slice: x: 2, y: 2, z: 4, core: 2. Of those that a mesh axis runs over, the one named last changes fastest.
Arguments:
- block_input: bfloat16 [1024, 1152], P('dp'), may hold values from -6 to 6
- cotangent: bfloat16 [1024, 1152], P('dp'), may hold values from -6 to 6
- segments: int32 [8, 128], P('dp'), may hold values from 0 to 7, never falling along the last dimension, each value on 1 to 64 neighbouring positions
- mixer_gain: float32 [1152], replicated, may hold values from 0.5 to 1.5
- feed_gain: float32 [1152], replicated, may hold values from 0.5 to 1.5
- query_matrix: bfloat16 [1152, 1024], P(None, 'mp'), may hold values from -0.1875 to 0.1875
- key_value_weight: bfloat16 [1152, 512], replicated, may hold values from -0.1875 to 0.1875
- output_matrix: bfloat16 [1024, 1152], P('mp'), may hold values from -0.75 to 0.75
- gate_up_weight: bfloat16 [1152, 2, 6912], P(None, None, 'mp'), may hold values from -0.1875 to 0.1875
- down_matrix: bfloat16 [6912, 1152], P('mp'), may hold values from -0.078125 to 0.078125
- query_adapter_inner: bfloat16 [2, 1152, 256], replicated, may hold values from -0.1875 to 0.1875
- query_adapter_outer: bfloat16 [2, 256, 1024], P(None, None, 'mp'), may hold values from -0.375 to 0.375
- key_value_inner: bfloat16 [2, 1152, 2, 256], replicated, may hold values from -0.1875 to 0.1875
- key_value_outer: bfloat16 [2, 2, 256, 256], replicated, may hold values from -0.375 to 0.375
- output_adapter_inner: bfloat16 [2, 1024, 256], P(None, 'mp'), may hold values from -0.75 to 0.75
- output_adapter_outer: bfloat16 [2, 256, 1152], replicated, may hold values from -0.375 to 0.375
- widen_inner_adapter: bfloat16 [2, 1152, 2, 256], replicated, may hold values from -0.1875 to 0.1875
- widen_outer_adapter: bfloat16 [2, 2, 256, 6912], P(None, None, None, 'mp'), may hold values from -0.375 to 0.375
- down_adapter_inner: bfloat16 [2, 6912, 256], P(None, 'mp'), may hold values from -0.078125 to 0.078125
- down_adapter_outer: bfloat16 [2, 256, 1152], replicated, may hold values from -0.375 to 0.375
Outputs:
- block_output: bfloat16 [1024, 1152], P('dp')
- input_grad: float32 [1024, 1152], P('dp')
- mixer_gain_grad: float32 [1152], P('dp')
- feed_gain_grad: float32 [1152], P('dp')
- query_weight_grad: float32 [1152, 1024], P('dp', 'mp')
- pair_weight_grad: float32 [1152, 512], P(('dp', 'mp'))
- output_weight_grad: float32 [1024, 1152], P('mp', 'dp')
- expand_weight_grad: float32 [1152, 2, 6912], P('dp', None, 'mp')
- shrink_weight_grad: float32 [6912, 1152], P('mp', 'dp')
- query_inner_grad: float32 [2, 1152, 256], P(None, ('dp', 'mp'))
- query_outer_grad: float32 [2, 256, 1024], P(None, 'dp', 'mp')
- pair_inner_grad: float32 [2, 1152, 2, 256], P(None, ('dp', 'mp'))
- pair_outer_grad: float32 [2, 2, 256, 256], P(None, None, ('dp', 'mp'))
- output_inner_grad: float32 [2, 1024, 256], P(None, 'mp', 'dp')
- output_outer_grad: float32 [2, 256, 1152], P(None, None, 'dp')
- expand_inner_grad: float32 [2, 1152, 2, 256], P(None, ('dp', 'mp'))
- expand_outer_grad: float32 [2, 2, 256, 6912], P(None, None, 'dp', 'mp')
- shrink_inner_grad: float32 [2, 6912, 256], P(None, 'mp', 'dp')
- shrink_outer_grad: float32 [2, 256, 1152], P(None, None, 'dp')
Inputs may be any that keep to these rules, and one draw needn't show every extreme that they name: `segments`: in each row ids never fall; each of the 8 documents has 1 to 64 tokens, one exactly 64.
All inputs are finite; a program needn't handle non-finite values.
Results may differ from a plain program's by a relative error of at most 0.04.
Values sent between devices are 32-bit elements; how exact they have to be, the bound alone decides.
A program may use at most 256 MiB of HBM per device.

v0:
```python
import math

import jax
import jax.numpy as jnp
from jax import lax
from jax.sharding import PartitionSpec as P

EPSILON = 1e-06
MASKED = -1e30


def product(left, right):
    return jnp.dot(left, right, preferred_element_type=jnp.float32)


def product_t(left, right):
    return lax.dot_general(
        left, right, (((1,), (1,)), ((), ())), preferred_element_type=jnp.float32
    )


def product_tn(left, right):
    return lax.dot_general(
        left, right, (((0,), (0,)), ((), ())), preferred_element_type=jnp.float32
    )


def exact_product(left, right):
    return jnp.dot(left, right, precision=lax.Precision.HIGHEST, preferred_element_type=jnp.float32)


def exact_tn(left, right):
    return lax.dot_general(
        left,
        right,
        (((0,), (0,)), ((), ())),
        precision=lax.Precision.HIGHEST,
        preferred_element_type=jnp.float32,
    )


def normalize(hidden_state, gain):
    factor = lax.rsqrt(jnp.mean(hidden_state * hidden_state, axis=-1, keepdims=True) + EPSILON)
    return (hidden_state * factor * gain, factor)


def normalize_back(hidden_state, factor, gain, upstream_gradient):
    unit = hidden_state * factor
    scaled = upstream_gradient * gain
    downstream = factor * (scaled - unit * jnp.mean(scaled * unit, axis=-1, keepdims=True))
    return (downstream, jnp.sum(upstream_gradient * unit, axis=0))


def rotate(values, cosine_table, sine_table):
    half_width = values.shape[-1] // 2
    first = values[..., :half_width]
    second = values[..., half_width:]
    return jnp.concatenate(
        [first * cosine_table - second * sine_table, second * cosine_table + first * sine_table],
        axis=-1,
    )


def rotary_tables(segment_row, head_size):
    length_value = segment_row.shape[0]
    earlier = jnp.sum((segment_row[None, :] < segment_row[:, None]).astype(jnp.int32), axis=1)
    position = (jnp.arange(length_value, dtype=jnp.int32) - earlier).astype(jnp.float32)
    steps_half = jnp.arange(head_size // 2, dtype=jnp.float32)
    frequency = 10000.0 ** (-2.0 * steps_half / head_size)
    angles = position[:, None] * frequency[None, :]
    same_segment = segment_row[:, None] == segment_row[None, :]
    ordinal = jnp.arange(length_value, dtype=jnp.int32)
    allowed_mask = same_segment & (ordinal[:, None] >= ordinal[None, :])
    return (jnp.cos(angles), jnp.sin(angles), allowed_mask)


def gelu_tanh(values):
    return jax.nn.gelu(values, approximate=True)


def attention_probs(queries, keys, allowed_mask, score_scale):
    scores = (
        jnp.einsum("ihd,jd->hij", queries, keys, preferred_element_type=jnp.float32) * score_scale
    )
    return jnp.where(allowed_mask[None], scores, MASKED)


def forward_loop_pass(hidden_state, shared_weights, low_rank_adapter, rotary_table_pair):
    (
        mixer_gain,
        feed_gain,
        query_matrix,
        key_value_weight,
        output_matrix,
        gate_up_weight,
        down_matrix,
    ) = shared_weights
    (
        query_adapter_inner,
        query_adapter_outer,
        key_value_inner,
        key_value_outer,
        output_adapter_inner,
        output_adapter_outer,
        widen_inner_adapter,
        widen_outer_adapter,
        down_adapter_inner,
        down_adapter_outer,
    ) = low_rank_adapter
    cosine_table, sine_table, allowed_mask = rotary_table_pair
    tokens_here, width = hidden_state.shape
    head_size = key_value_weight.shape[1] // 2
    local_heads = query_matrix.shape[1] // head_size
    rank_size = query_adapter_inner.shape[1]
    hidden_local = down_matrix.shape[0]
    score_scale = 1.0 / math.sqrt(head_size)
    normalized_state, mixer_factor = normalize(hidden_state, mixer_gain)
    normed_low = normalized_state.astype(jnp.bfloat16)
    query_rank_value = product(normed_low, query_adapter_inner).astype(jnp.bfloat16)
    query_projected = product(normed_low, query_matrix) + product(
        query_rank_value, query_adapter_outer
    )
    key_value_rank_value = (
        product(normed_low, key_value_inner.reshape(width, 2 * rank_size))
        .astype(jnp.bfloat16)
        .reshape(tokens_here, 2, rank_size)
    )
    key_value_linear = product(normed_low, key_value_weight) + jnp.einsum(
        "tjr,jrh->tjh", key_value_rank_value, key_value_outer, preferred_element_type=jnp.float32
    ).reshape(tokens_here, 2 * head_size)
    queries = rotate(
        query_projected.reshape(tokens_here, local_heads, head_size),
        cosine_table[:, None],
        sine_table[:, None],
    ).astype(jnp.bfloat16)
    keys = rotate(key_value_linear[:, :head_size], cosine_table, sine_table).astype(jnp.bfloat16)
    values = key_value_linear[:, head_size:].astype(jnp.bfloat16)
    masked = attention_probs(queries, keys, allowed_mask, score_scale)
    highest = jnp.max(masked, axis=-1, keepdims=True)
    expo = jnp.exp(masked - highest)
    totals = jnp.sum(expo, axis=-1, keepdims=True)
    probs = expo / totals
    logsum = highest + jnp.log(totals)
    attention_mixed = jnp.einsum(
        "hij,jd->ihd", probs.astype(jnp.bfloat16), values, preferred_element_type=jnp.float32
    )
    attention_mixed = attention_mixed.reshape(tokens_here, local_heads * head_size).astype(
        jnp.bfloat16
    )
    head_part = product(attention_mixed, output_matrix)
    rank_part = product(attention_mixed, output_adapter_inner)
    summed, output_rank = lax.psum((head_part, rank_part), "mp")
    middle = (
        hidden_state + summed + exact_product(output_rank, output_adapter_outer.astype(jnp.float32))
    )
    feed_result, feed_factor = normalize(middle, feed_gain)
    fed_low = feed_result.astype(jnp.bfloat16)
    widen_rank_value = (
        product(fed_low, widen_inner_adapter.reshape(width, 2 * rank_size))
        .astype(jnp.bfloat16)
        .reshape(tokens_here, 2, rank_size)
    )
    widened_hidden = product(fed_low, gate_up_weight.reshape(width, 2 * hidden_local)).reshape(
        tokens_here, 2, hidden_local
    )
    widened_hidden = widened_hidden + jnp.einsum(
        "tjr,jrf->tjf", widen_rank_value, widen_outer_adapter, preferred_element_type=jnp.float32
    )
    gated_hidden = (gelu_tanh(widened_hidden[:, 0]) * widened_hidden[:, 1]).astype(jnp.bfloat16)
    shrink_part = product(gated_hidden, down_matrix)
    shrink_rank_part = product(gated_hidden, down_adapter_inner)
    shrunk, shrink_rank = lax.psum((shrink_part, shrink_rank_part), "mp")
    result = middle + shrunk + exact_product(shrink_rank, down_adapter_outer.astype(jnp.float32))
    kept_state = (
        hidden_state,
        mixer_factor,
        normed_low,
        query_rank_value,
        key_value_rank_value,
        queries,
        keys,
        values,
        logsum,
        attention_mixed,
        output_rank,
        middle,
        feed_factor,
        fed_low,
        widen_rank_value,
        widened_hidden,
        gated_hidden,
        shrink_rank,
    )
    return (result, kept_state)


def reverse_loop_pass(
    upstream_gradient, kept_state, shared_weights, low_rank_adapter, rotary_table_pair
):
    (
        mixer_gain,
        feed_gain,
        query_matrix,
        key_value_weight,
        output_matrix,
        gate_up_weight,
        down_matrix,
    ) = shared_weights
    (
        query_adapter_inner,
        query_adapter_outer,
        key_value_inner,
        key_value_outer,
        output_adapter_inner,
        output_adapter_outer,
        widen_inner_adapter,
        widen_outer_adapter,
        down_adapter_inner,
        down_adapter_outer,
    ) = low_rank_adapter
    cosine_table, sine_table, allowed_mask = rotary_table_pair
    (
        hidden_state,
        mixer_factor,
        normed_low,
        query_rank_value,
        key_value_rank_value,
        queries,
        keys,
        values,
        logsum,
        attention_mixed,
        output_rank,
        middle,
        feed_factor,
        fed_low,
        widen_rank_value,
        widened_hidden,
        gated_hidden,
        shrink_rank,
    ) = kept_state
    tokens_here, width = hidden_state.shape
    head_size = key_value_weight.shape[1] // 2
    local_heads = query_matrix.shape[1] // head_size
    rank_size = query_adapter_inner.shape[1]
    hidden_local = down_matrix.shape[0]
    score_scale = 1.0 / math.sqrt(head_size)
    grad_feed = upstream_gradient.astype(jnp.bfloat16)
    grad_shrink_rank = product_t(grad_feed, down_adapter_outer).astype(jnp.bfloat16)
    shrink_outer_grad = exact_tn(shrink_rank, grad_feed.astype(jnp.float32))
    shrink_weight_grad = product_tn(gated_hidden, grad_feed)
    shrink_inner_grad = product_tn(gated_hidden, grad_shrink_rank)
    grad_activated = product_t(grad_feed, down_matrix) + product_t(
        grad_shrink_rank, down_adapter_inner
    )
    gelu_value, gelu_pullback = jax.vjp(gelu_tanh, widened_hidden[:, 0])
    grad_gate = gelu_pullback(grad_activated * widened_hidden[:, 1])[0]
    grad_up = grad_activated * gelu_value
    grad_expand = jnp.stack([grad_gate, grad_up], axis=1).astype(jnp.bfloat16)
    grad_expand_flat = grad_expand.reshape(tokens_here, 2 * hidden_local)
    expand_weight_grad = product_tn(fed_low, grad_expand_flat).reshape(width, 2, hidden_local)
    expand_outer_grad = jnp.einsum(
        "tjr,tjf->jrf", widen_rank_value, grad_expand, preferred_element_type=jnp.float32
    )
    grad_expand_rank = (
        jnp.einsum(
            "tjf,jrf->tjr", grad_expand, widen_outer_adapter, preferred_element_type=jnp.float32
        )
        .reshape(tokens_here, 2 * rank_size)
        .astype(jnp.bfloat16)
    )
    expand_inner_grad = product_tn(fed_low, grad_expand_rank).reshape(width, 2, rank_size)
    grad_fed = product_t(
        grad_expand_flat, gate_up_weight.reshape(width, 2 * hidden_local)
    ) + product_t(grad_expand_rank, widen_inner_adapter.reshape(width, 2 * rank_size))
    grad_fed = lax.psum(grad_fed, "mp")
    grad_middle_norm, feed_gain_grad = normalize_back(middle, feed_factor, feed_gain, grad_fed)
    grad_middle = upstream_gradient + grad_middle_norm
    grad_attend = grad_middle.astype(jnp.bfloat16)
    grad_output_rank = product_t(grad_attend, output_adapter_outer).astype(jnp.bfloat16)
    output_outer_grad = exact_tn(output_rank, grad_attend.astype(jnp.float32))
    output_weight_grad = product_tn(attention_mixed, grad_attend)
    output_inner_grad = product_tn(attention_mixed, grad_output_rank)
    grad_mixed = product_t(grad_attend, output_matrix) + product_t(
        grad_output_rank, output_adapter_inner
    )
    grad_mixed = grad_mixed.astype(jnp.bfloat16).reshape(tokens_here, local_heads, head_size)
    masked = attention_probs(queries, keys, allowed_mask, score_scale)
    probs = jnp.exp(masked - logsum)
    grad_probs = jnp.einsum("ihd,jd->hij", grad_mixed, values, preferred_element_type=jnp.float32)
    delta = jnp.sum(grad_probs * probs, axis=-1, keepdims=True)
    grad_scores = (probs * (grad_probs - delta)).astype(jnp.bfloat16)
    grad_queries = (
        jnp.einsum("hij,jd->ihd", grad_scores, keys, preferred_element_type=jnp.float32)
        * score_scale
    )
    grad_keys = (
        jnp.einsum("hij,ihd->jd", grad_scores, queries, preferred_element_type=jnp.float32)
        * score_scale
    )
    grad_values = jnp.einsum(
        "hij,ihd->jd", probs.astype(jnp.bfloat16), grad_mixed, preferred_element_type=jnp.float32
    )
    grad_query_linear = (
        rotate(grad_queries, cosine_table[:, None], -sine_table[:, None])
        .reshape(tokens_here, local_heads * head_size)
        .astype(jnp.bfloat16)
    )
    grad_pair = jnp.concatenate(
        [rotate(grad_keys, cosine_table, -sine_table), grad_values], axis=-1
    ).astype(jnp.bfloat16)
    query_weight_grad = product_tn(normed_low, grad_query_linear)
    query_outer_grad = product_tn(query_rank_value, grad_query_linear)
    grad_query_rank = product_t(grad_query_linear, query_adapter_outer).astype(jnp.bfloat16)
    query_inner_grad = product_tn(normed_low, grad_query_rank)
    pair_weight_grad = product_tn(normed_low, grad_pair)
    grad_pair_split = grad_pair.reshape(tokens_here, 2, head_size)
    pair_outer_grad = jnp.einsum(
        "tjr,tjh->jrh", key_value_rank_value, grad_pair_split, preferred_element_type=jnp.float32
    )
    grad_pair_rank = (
        jnp.einsum(
            "tjh,jrh->tjr", grad_pair_split, key_value_outer, preferred_element_type=jnp.float32
        )
        .reshape(tokens_here, 2 * rank_size)
        .astype(jnp.bfloat16)
    )
    pair_inner_grad = product_tn(normed_low, grad_pair_rank).reshape(width, 2, rank_size)
    grad_normed = product_t(grad_query_linear, query_matrix) + product_t(
        grad_query_rank, query_adapter_inner
    )
    grad_normed = (
        grad_normed
        + product_t(grad_pair, key_value_weight)
        + product_t(grad_pair_rank, key_value_inner.reshape(width, 2 * rank_size))
    )
    grad_normed = lax.psum(grad_normed, "mp")
    grad_hidden_norm, mixer_gain_grad = normalize_back(
        hidden_state, mixer_factor, mixer_gain, grad_normed
    )
    hidden_gradient = grad_middle + grad_hidden_norm
    shared_gradients = (
        mixer_gain_grad,
        feed_gain_grad,
        query_weight_grad,
        pair_weight_grad,
        output_weight_grad,
        expand_weight_grad,
        shrink_weight_grad,
    )
    adapter_gradients = (
        query_inner_grad,
        query_outer_grad,
        pair_inner_grad,
        pair_outer_grad,
        output_inner_grad,
        output_outer_grad,
        expand_inner_grad,
        expand_outer_grad,
        shrink_inner_grad,
        shrink_outer_grad,
    )
    return (hidden_gradient, shared_gradients, adapter_gradients)


def per_device(
    block_input,
    cotangent,
    segments,
    mixer_gain,
    feed_gain,
    query_matrix,
    key_value_weight,
    output_matrix,
    gate_up_weight,
    down_matrix,
    query_adapter_inner,
    query_adapter_outer,
    key_value_inner,
    key_value_outer,
    output_adapter_inner,
    output_adapter_outer,
    widen_inner_adapter,
    widen_outer_adapter,
    down_adapter_inner,
    down_adapter_outer,
):
    shared_weights = (
        mixer_gain,
        feed_gain,
        query_matrix,
        key_value_weight,
        output_matrix,
        gate_up_weight,
        down_matrix,
    )
    adapter_stacked = (
        query_adapter_inner,
        query_adapter_outer,
        key_value_inner,
        key_value_outer,
        output_adapter_inner,
        output_adapter_outer,
        widen_inner_adapter,
        widen_outer_adapter,
        down_adapter_inner,
        down_adapter_outer,
    )
    repeat_count = query_adapter_inner.shape[0]
    head_size = key_value_weight.shape[1] // 2
    rotary_table_pair = rotary_tables(segments[0], head_size)
    hidden_state = block_input.astype(jnp.float32)
    kept_state_list = []
    for repeat_index in range(repeat_count):
        low_rank_adapter = tuple((entry_value[repeat_index] for entry_value in adapter_stacked))
        hidden_state, kept_state = forward_loop_pass(
            hidden_state, shared_weights, low_rank_adapter, rotary_table_pair
        )
        kept_state_list.append(kept_state)
    block_output = hidden_state.astype(jnp.bfloat16)
    upstream_gradient = cotangent.astype(jnp.float32)
    shared_total = shared_weights
    adapter_pieces = [adapter_stacked] * repeat_count
    for repeat_index in reversed(range(repeat_count)):
        low_rank_adapter = tuple((entry_value[repeat_index] for entry_value in adapter_stacked))
        upstream_gradient, shared_piece, adapter_piece = reverse_loop_pass(
            upstream_gradient,
            kept_state_list[repeat_index],
            shared_weights,
            low_rank_adapter,
            rotary_table_pair,
        )
        if repeat_index == repeat_count - 1:
            shared_total = shared_piece
        else:
            shared_total = tuple(
                (first + second for first, second in zip(shared_total, shared_piece))
            )
        adapter_pieces[repeat_index] = adapter_piece
    stacked = tuple(
        (
            jnp.stack(
                [
                    adapter_pieces[repeat_index][member_entry]
                    for repeat_index in range(repeat_count)
                ],
                axis=0,
            )
            for member_entry in range(10)
        )
    )
    both = (
        lax.psum_scatter(shared_total[3], ("dp", "mp"), scatter_dimension=0, tiled=True),
        lax.psum_scatter(stacked[0], ("dp", "mp"), scatter_dimension=1, tiled=True),
        lax.psum_scatter(stacked[2], ("dp", "mp"), scatter_dimension=1, tiled=True),
        lax.psum_scatter(stacked[3], ("dp", "mp"), scatter_dimension=2, tiled=True),
        lax.psum_scatter(stacked[6], ("dp", "mp"), scatter_dimension=1, tiled=True),
    )
    alone = (
        lax.psum_scatter(shared_total[0], "dp", scatter_dimension=0, tiled=True),
        lax.psum_scatter(shared_total[1], "dp", scatter_dimension=0, tiled=True),
        lax.psum_scatter(shared_total[2], "dp", scatter_dimension=0, tiled=True),
        lax.psum_scatter(shared_total[4], "dp", scatter_dimension=1, tiled=True),
        lax.psum_scatter(shared_total[5], "dp", scatter_dimension=0, tiled=True),
        lax.psum_scatter(shared_total[6], "dp", scatter_dimension=1, tiled=True),
        lax.psum_scatter(stacked[1], "dp", scatter_dimension=1, tiled=True),
        lax.psum_scatter(stacked[4], "dp", scatter_dimension=2, tiled=True),
        lax.psum_scatter(stacked[5], "dp", scatter_dimension=2, tiled=True),
        lax.psum_scatter(stacked[7], "dp", scatter_dimension=2, tiled=True),
        lax.psum_scatter(stacked[8], "dp", scatter_dimension=2, tiled=True),
        lax.psum_scatter(stacked[9], "dp", scatter_dimension=2, tiled=True),
    )
    pair_weight_grad = both[0]
    shared_rest = (alone[0], alone[1], alone[2], alone[3], alone[4], alone[5])
    adapter_output = (
        both[1],
        alone[6],
        both[2],
        both[3],
        alone[7],
        alone[8],
        both[4],
        alone[9],
        alone[10],
        alone[11],
    )
    return (
        block_output,
        upstream_gradient,
        shared_rest[0],
        shared_rest[1],
        shared_rest[2],
        pair_weight_grad,
        shared_rest[3],
        shared_rest[4],
        shared_rest[5],
        adapter_output[0],
        adapter_output[1],
        adapter_output[2],
        adapter_output[3],
        adapter_output[4],
        adapter_output[5],
        adapter_output[6],
        adapter_output[7],
        adapter_output[8],
        adapter_output[9],
    )


def solution(mesh):
    in_specs = (
        P("dp", None),
        P("dp", None),
        P("dp", None),
        P(),
        P(),
        P(None, "mp"),
        P(),
        P("mp", None),
        P(None, None, "mp"),
        P("mp", None),
        P(),
        P(None, None, "mp"),
        P(),
        P(),
        P(None, "mp", None),
        P(),
        P(),
        P(None, None, None, "mp"),
        P(None, "mp", None),
        P(),
    )
    out_specs = (
        P("dp", None),
        P("dp", None),
        P("dp"),
        P("dp"),
        P("dp", "mp"),
        P(("dp", "mp"), None),
        P("mp", "dp"),
        P("dp", None, "mp"),
        P("mp", "dp"),
        P(None, ("dp", "mp"), None),
        P(None, "dp", "mp"),
        P(None, ("dp", "mp"), None, None),
        P(None, None, ("dp", "mp"), None),
        P(None, "mp", "dp"),
        P(None, None, "dp"),
        P(None, ("dp", "mp"), None, None),
        P(None, None, "dp", "mp"),
        P(None, "mp", "dp"),
        P(None, None, "dp"),
    )
    return jax.shard_map(
        per_device, mesh=mesh, in_specs=in_specs, out_specs=out_specs, check_vma=False
    )
```

profile of v0, /device:TPU:0, one launch (start us, length us, event | category | flops | bytes accessed | tf_op | source)
XLA Modules:
  0.0 1882.0 jit_solution(13436863261936621976)
XLA Ops:
  9.4 3.7 fusion.326
  21.4 3.7 fusion.325
  26.4 32.2 %all-reduce.45.cloned.1.call-done = (f32[128,256]{1,0:T(8,128)}, f32[128,1152]{1,0:T(8,128)}) async-done(((f32[128,256]{1,0:T(8,128)}, f32[128,1152]{1,0:T(8,128)}), (f32[128,256]{1,0:T(8,128)}, f32[128,1152]{1,0:T(8,128)})) %all-reduce.45.cloned.1.call-update) | async-done | bytes 720912 | tf_op jit(solution)/shard_map/psum | solution.py:152
  60.7 5.7 fusion.3
  80.7 26.1 %all-reduce.43.cloned.1.call-done = (f32[128,256]{1,0:T(8,128)}, f32[128,1152]{1,0:T(8,128)}) async-done(((f32[128,256]{1,0:T(8,128)}, f32[128,1152]{1,0:T(8,128)}), (f32[128,256]{1,0:T(8,128)}, f32[128,1152]{1,0:T(8,128)})) %all-reduce.43.cloned.1.call-update) | async-done | bytes 720912 | tf_op jit(solution)/shard_map/psum | solution.py:172
  121.5 32.1 %all-reduce.41.cloned.1.call-done = (f32[128,256]{1,0:T(8,128)}, f32[128,1152]{1,0:T(8,128)}) async-done(((f32[128,256]{1,0:T(8,128)}, f32[128,1152]{1,0:T(8,128)}), (f32[128,256]{1,0:T(8,128)}, f32[128,1152]{1,0:T(8,128)})) %all-reduce.41.cloned.1.call-update) | async-done | bytes 720912 | tf_op jit(solution)/shard_map/psum | solution.py:152
  156.1 5.7 fusion.1
  176.0 4.0 fusion.337
  181.2 27.9 %all-reduce.29.cloned.1.call-done = f32[128,1152]{1,0:T(8,128)} async-done(((f32[128,1152]{1,0:T(8,128)}), f32[128,1152]{1,0:T(8,128)}) %all-reduce.29.cloned.1.call-update) | async-done | bytes 589840 | tf_op jit(solution)/shard_map/psum | solution.py:276
  230.0 27.4 %all-reduce.31.cloned.1.call-done = f32[128,1152]{1,0:T(8,128)} async-done(((f32[128,1152]{1,0:T(8,128)}), f32[128,1152]{1,0:T(8,128)}) %all-reduce.31.cloned.1.call-update) | async-done | bytes 589840 | tf_op jit(solution)/shard_map/psum | solution.py:337
  276.4 10.0 copy.175
  286.5 20.6 %all-reduce.33.cloned.1.call-done = f32[128,1152]{1,0:T(8,128)} async-done(((f32[128,1152]{1,0:T(8,128)}), f32[128,1152]{1,0:T(8,128)}) %all-reduce.33.cloned.1.call-update) | async-done | bytes 589840 | tf_op jit(solution)/shard_map/psum | solution.py:276
  323.3 7.7 copy.163
  332.9 10.1 copy.166
  353.1 12.0 copy.178
  368.6 6.8 copy.179
  382.1 5.0 copy.172
  390.3 5.0 copy.180
  399.9 8.9 convolution_add_fusion
  421.0 4.6 convolution_add_fusion.1
  429.3 85.7 %fusion = f32[40,512]{1,0:T(8,128)S(1)} fusion(f32[1152,512]{1,0:T(8,128)} %convolution_add_fusion.2), kind=kCustom, calls=%all-reduce-scatter | all-reduce-scatter fusion | flops 655361 | bytes 2441216
  523.0 6.3 concatenate.84
  531.9 38.2 %all-reduce.13 = (f32[1152]{0:T(1024)S(1)}, f32[1152]{0:T(1024)S(1)}) all-reduce(f32[1152]{0:T(1024)S(1)} %add.323, f32[1152]{0:T(1024)} %add.324), channel_id=2, replica_groups=mesh['dp'=8,'mp'=4] {'dp'}, use_global_device_ids=true, to_apply=%region_29.30.clone | all-reduce | flops 2304 | bytes 18432
  574.7 30.6 %all-reduce.35.cloned.1.call-done = (f32[2,1152,256]{2,0,1:T(2,128)}, f32[2,1152,2,256]{3,2,0,1:T(2,128)}, f32[2,1152,2,256]{3,2,0,1:T(2,128)}) async-done(((f32[2,1152,256]{2,0,1:T(2,128)}, f32[2,1152,2,256]{3,2,0,1:T(2,128)}, f32[2,1152,2,256]{3,2,0,1:T(2,128)}), (f32[2,1152,256]{2,0,1:T(2,128)}, f32[2,1152,2,256]{3,2,0,1:T(2,128)}, f32[2,1152,2,256]{3,2,0,1:T(2,128)})) %all-reduce.35.cloned.1.call-update) | async-done | bytes 11796496
  609.3 501.1 %all-reduce.37.cloned.1.call-done = (f32[2,256,256]{1,0,2:T(2,128)}, f32[2,256,1152]{1,0,2:T(2,128)}, f32[2,2,256,1728]{3,1,0,2:T(2,128)}, f32[2,1728,256]{1,0,2:T(2,128)}, f32[2,256,1152]{1,0,2:T(2,128)}) async-done(((f32[2,256,256]{1,0,2:T(2,128)}, f32[2,256,1152]{1,0,2:T(2,128)}, f32[2,2,256,1728]{3,1,0,2:T(2,128)}, f32[2,1728,256]{1,0,2:T(2,128)}, f32[2,256,1152]{1,0,2:T(2,128)}), ...) | async-done | bytes 15859728
  1118.8 272.4 %reduce-scatter.13.cloned.1.call-done = f32[144,2,1728]{2,0,1:T(8,128)} async-done(((f32[1152,2,1728]{2,0,1:T(8,128)}), f32[144,2,1728]{2,0,1:T(8,128)}) %reduce-scatter.13.cloned.1.call-update) | async-done | bytes 1990672 | tf_op jit(solution)/shard_map/reduce_scatter | solution.py:464
  1391.2 4.5 copy.181
  1395.7 60.7 %reduce-scatter.17.cloned.1.call-done = f32[2,32,256]{2,1,0:T(8,128)} async-done(((f32[2,256,256]{2,1,0:T(8,128)}), f32[2,32,256]{2,1,0:T(8,128)}) %reduce-scatter.17.cloned.1.call-update) | async-done | bytes 65552 | tf_op jit(solution)/shard_map/reduce_scatter | solution.py:466
  1456.4 136.5 %reduce-scatter.19.cloned.1.call-done = f32[2,2,8,256]{3,2,1,0:T(8,128)} async-done(((f32[2,2,256,256]{3,2,1,0:T(8,128)}), f32[2,2,8,256]{3,2,1,0:T(8,128)}) %reduce-scatter.19.cloned.1.call-update) | async-done | bytes 32784 | tf_op jit(solution)/shard_map/reduce_scatter | solution.py:456
  1592.9 64.5 %reduce-scatter.9.cloned.1.call-done = f32[144,256]{1,0:T(8,128)} async-done(((f32[1152,256]{1,0:T(8,128)}), f32[144,256]{1,0:T(8,128)}) %reduce-scatter.9.cloned.1.call-update) | async-done | bytes 147472 | tf_op jit(solution)/shard_map/reduce_scatter | solution.py:462
  1657.3 67.3 %reduce-scatter.11.cloned.1.call-done = f32[256,144]{0,1:T(8,128)} async-done(((f32[256,1152]{0,1:T(8,128)}), f32[256,144]{0,1:T(8,128)}) %reduce-scatter.11.cloned.1.call-update) | async-done | bytes 147472 | tf_op jit(solution)/shard_map/reduce_scatter | solution.py:463
  1724.7 150.3 %reduce-scatter.15.cloned.1.call-done = f32[1728,144]{0,1:T(8,128)} async-done(((f32[1728,1152]{0,1:T(8,128)}), f32[1728,144]{0,1:T(8,128)}) %reduce-scatter.15.cloned.1.call-update) | async-done | bytes 995344 | tf_op jit(solution)/shard_map/reduce_scatter | solution.py:465
  (620 shorter events, 186.2 us)
Async XLA Ops:
  7.2 51.4 %all-reduce.45.cloned.1.call-start = ((), (), s32[]{:S(2)}) async-start(), calls=%async_computation.20 | async-start | bytes 1441792 | tf_op jit(solution)/shard_map/psum | solution.py:152
  7.3 10.6 copy-start.167
  21.3 85.5 %all-reduce.43.cloned.1.call-start = ((), (), s32[]{:S(2)}) async-start(), calls=%async_computation.19 | async-start | bytes 1441792 | tf_op jit(solution)/shard_map/psum | solution.py:172
  25.1 35.4 %copy-start.131 = (f32[1152]{0:T(1024)S(1)}, f32[1152]{0:T(1024)}, u32[]{:S(2)}) copy-start(f32[1152]{0:T(1024)} %param.24) | copy-start | bytes 13828
  72.2 81.4 %all-reduce.41.cloned.1.call-start = ((), (), s32[]{:S(2)}) async-start(), calls=%async_computation.18 | async-start | bytes 1441792 | tf_op jit(solution)/shard_map/psum | solution.py:152
  119.0 90.1 %all-reduce.29.cloned.1.call-start = ((), (), s32[]{:S(2)}) async-start(), calls=%async_computation.6 | async-start | bytes 1179648 | tf_op jit(solution)/shard_map/psum | solution.py:276
  175.5 82.0 %all-reduce.31.cloned.1.call-start = ((), (), s32[]{:S(2)}) async-start(), calls=%async_computation.7 | async-start | bytes 1179648 | tf_op jit(solution)/shard_map/psum | solution.py:337
  223.8 83.3 %all-reduce.33.cloned.1.call-start = ((), (), s32[]{:S(2)}) async-start(), calls=%async_computation.8 | async-start | bytes 1179648 | tf_op jit(solution)/shard_map/psum | solution.py:276
  273.5 113.6 %all-reduce.39.cloned.1.call-start = ((), (), s32[]{:S(2)}) async-start(), calls=%async_computation.17 | async-start | bytes 2621440 | tf_op jit(solution)/shard_map/psum | solution.py:172
  276.4 32.7 %copy-start.62 = (f32[128,1152]{1,0:T(8,128)S(1)}, f32[128,1152]{1,0:T(8,128)}, u32[]{:S(2)}) copy-start(f32[128,1152]{1,0:T(8,128)} %get-tuple-element.125) | copy-start | bytes 1769476
  321.9 283.5 %all-reduce.35.cloned.1.call-start = ((), (), s32[]{:S(2)}) async-start(), calls=%async_computation.15 | async-start | bytes 23592960
  343.0 767.3 %all-reduce.37.cloned.1.call-start = ((), (), s32[]{:S(2)}) async-start(), calls=%async_computation.16 | async-start | bytes 32505856
  353.1 12.0 copy-start.29
  353.1 12.0 copy-start.164
  395.4 995.8 %reduce-scatter.13.cloned.1.call-start = ((), (), s32[]{:S(2)}) async-start(), calls=%async_computation.11 | async-start | bytes 18579456 | tf_op jit(solution)/shard_map/reduce_scatter | solution.py:464
  408.9 1047.5 %reduce-scatter.17.cloned.1.call-start = ((), (), s32[]{:S(2)}) async-start(), calls=%async_computation.13 | async-start | bytes 589824 | tf_op jit(solution)/shard_map/reduce_scatter | solution.py:466
  411.9 1181.0 %reduce-scatter.19.cloned.1.call-start = ((), (), s32[]{:S(2)}) async-start(), calls=%async_computation.14 | async-start | bytes 1081344 | tf_op jit(solution)/shard_map/reduce_scatter | solution.py:456
  415.3 1242.0 %reduce-scatter.9.cloned.1.call-start = ((), (), s32[]{:S(2)}) async-start(), calls=%async_computation.9 | async-start | bytes 1327104 | tf_op jit(solution)/shard_map/reduce_scatter | solution.py:462
  417.5 1307.2 %reduce-scatter.11.cloned.1.call-start = ((), (), s32[]{:S(2)}) async-start(), calls=%async_computation.10 | async-start | bytes 1327104 | tf_op jit(solution)/shard_map/reduce_scatter | solution.py:463
  419.6 1455.4 %reduce-scatter.15.cloned.1.call-start = ((), (), s32[]{:S(2)}) async-start(), calls=%async_computation.12 | async-start | bytes 9289728 | tf_op jit(solution)/shard_map/reduce_scatter | solution.py:465
  429.3 91.0 %copy-start.194 = (u32[32]{0:T(128)S(1)}, u32[32]{0:T(128)}, u32[]{:S(2)}) copy-start(u32[32]{0:T(128)} %constant.47) | copy-start | bytes 388
  429.3 92.9 %copy-start.177 = (f32[1152]{0:T(1024)S(1)}, f32[1152]{0:T(1024)}, u32[]{:S(2)}) copy-start(f32[1152]{0:T(1024)} %get-tuple-element.97) | copy-start | bytes 13828
  429.3 92.9 %copy-start.178 = (f32[1152]{0:T(1024)S(1)}, f32[1152]{0:T(1024)}, u32[]{:S(2)}) copy-start(f32[1152]{0:T(1024)} %get-tuple-element.95) | copy-start | bytes 13828
  429.3 101.7 %copy-start.60 = (f32[128,1152]{1,0:T(8,128)S(1)}, f32[128,1152]{1,0:T(8,128)}, u32[]{:S(2)}) copy-start(f32[128,1152]{1,0:T(8,128)} %get-tuple-element.115) | copy-start | bytes 1769476
  429.3 142.2 %copy-start.80 = (bf16[2,256,1152]{2,1,0:T(8,128)(2,1)S(1)}, bf16[2,256,1152]{2,1,0:T(8,128)(2,1)}, u32[]{:S(2)}) copy-start(bf16[2,256,1152]{2,1,0:T(8,128)(2,1)} %param.39) | copy-start | bytes 3538948
  429.3 142.2 %copy-start.117 = (f32[128,256]{1,0:T(8,128)S(1)}, f32[128,256]{1,0:T(8,128)}, u32[]{:S(2)}) copy-start(f32[128,256]{1,0:T(8,128)} %get-tuple-element.113) | copy-start | bytes 393220
  515.1 7.8 collective-permute-start.2
  516.4 6.7 collective-permute-start.1
  517.7 5.4 collective-permute-start
  519.0 3.8 collective-permute-start.3
  529.3 44.3 %copy-start.61 = (f32[128,1152]{1,0:T(8,128)S(1)}, f32[128,1152]{1,0:T(8,128)}, u32[]{:S(2)}) copy-start(f32[128,1152]{1,0:T(8,128)} %get-tuple-element.123) | copy-start | bytes 1769476
  1118.1 757.0 %copy-start.1 = (bf16[1152,512]{1,0:T(8,128)(2,1)S(1)}, bf16[1152,512]{1,0:T(8,128)(2,1)}, u32[]{:S(2)}) copy-start(bf16[1152,512]{1,0:T(8,128)(2,1)} %param.26) | copy-start | bytes 3538948
  (186 other events, 478.3 us)
Sparse Core Ops, SparseCore 0:
  21.4 37.1 all-reduce.44
  72.3 34.4 all-reduce.42
  119.1 34.4 all-reduce.40
  175.6 33.4 all-reduce.28
  223.9 33.4 all-reduce.30
  273.6 33.4 all-reduce.32
  322.0 39.3 all-reduce.38
  367.8 237.5 all-reduce.34
  610.7 499.6 all-reduce.36
  1114.7 276.4 reduce-scatter.12
  1395.5 60.8 reduce-scatter.16
  1459.1 133.7 reduce-scatter.18
  1597.2 60.0 reduce-scatter.8
  1661.5 63.0 reduce-scatter.10
  1729.3 145.7 reduce-scatter.14
where the time goes:
time: 1890 us; the launch traced here: 1880 us
  waiting for transfers between devices  1450 us (77%)
  blocking collectives  124 us (7%)
  local copies, waits for them, and re-layouts  122 us (6%)
  matrix products  121 us (6%)
  other arithmetic  39.8 us (2%)
    unnamed x21, waiting for transfers between devices  532 us
    reduce_scatter x1, waiting for transfers between devices, per_device(): lax.psum_scatter(shared_total[5], 'dp', scatter_dimension=0, tiled=True)  272 us
    reduce_scatter x1, waiting for transfers between devices, per_device(): lax.psum_scatter(shared_total[6], 'dp', scatter_dimension=1, tiled=True)  150 us
    reduce_scatter x1, waiting for transfers between devices, per_device(): lax.psum_scatter(stacked[3], ('dp', 'mp'), scatter_dimension=2, tiled=True)  136 us
    unnamed x2, blocking collectives  124 us
    reduce_scatter x1, waiting for transfers between devices, per_device(): lax.psum_scatter(shared_total[4], 'dp', scatter_dimension=1, tiled=True)  67.3 us
    reduce_scatter x1, waiting for transfers between devices, per_device(): lax.psum_scatter(shared_total[2], 'dp', scatter_dimension=0, tiled=True)  64.5 us
    psum x2, waiting for transfers between devices, forward_loop_pass(): summed, output_rank = lax.psum((head_part, rank_part), 'mp')  64.3 us
  transfers between devices with their start and end apart: 19, of which 15 were waited for; matrix products, arithmetic and copies ran while one was open for 14% of the time, Pallas kernels for 0%

commit v1 on v0

v1 whole, which is shorter than its diff:
```python
import functools
import math
from types import SimpleNamespace

import jax
import jax.numpy as jnp
from jax import lax
from jax.experimental import pallas as pl
from jax.experimental.pallas import tpu as pltpu
from jax.sharding import PartitionSpec as P

EPSILON = 1e-06
MASKED = -1e30
MESH = pl.DeviceIdType.MESH


def product(left, right):
    return jnp.dot(left, right, preferred_element_type=jnp.float32)


def product_t(left, right):
    return lax.dot_general(
        left, right, (((1,), (1,)), ((), ())), preferred_element_type=jnp.float32
    )


def product_tn(left, right):
    return lax.dot_general(
        left, right, (((0,), (0,)), ((), ())), preferred_element_type=jnp.float32
    )


def exact_product(left, right):
    return jnp.dot(left, right, precision=lax.Precision.HIGHEST, preferred_element_type=jnp.float32)


def exact_tn(left, right):
    return lax.dot_general(
        left,
        right,
        (((0,), (0,)), ((), ())),
        precision=lax.Precision.HIGHEST,
        preferred_element_type=jnp.float32,
    )


def normalize(hidden_state, gain):
    factor = lax.rsqrt(jnp.mean(hidden_state * hidden_state, axis=-1, keepdims=True) + EPSILON)
    return (hidden_state * factor * gain, factor)


def normalize_back(hidden_state, factor, gain, upstream_gradient):
    unit = hidden_state * factor
    scaled = upstream_gradient * gain
    downstream = factor * (scaled - unit * jnp.mean(scaled * unit, axis=-1, keepdims=True))
    return (downstream, jnp.sum(upstream_gradient * unit, axis=0))


def rotate(values, cosine_table, sine_table):
    half_width = values.shape[-1] // 2
    first = values[..., :half_width]
    second = values[..., half_width:]
    return jnp.concatenate(
        [first * cosine_table - second * sine_table, second * cosine_table + first * sine_table],
        axis=-1,
    )


def rotary_tables(segment_row, head_size):
    length_value = segment_row.shape[0]
    earlier = jnp.sum((segment_row[None, :] < segment_row[:, None]).astype(jnp.int32), axis=1)
    position = (jnp.arange(length_value, dtype=jnp.int32) - earlier).astype(jnp.float32)
    steps_half = jnp.arange(head_size // 2, dtype=jnp.float32)
    frequency = 10000.0 ** (-2.0 * steps_half / head_size)
    angles = position[:, None] * frequency[None, :]
    same_segment = segment_row[:, None] == segment_row[None, :]
    ordinal = jnp.arange(length_value, dtype=jnp.int32)
    allowed_mask = same_segment & (ordinal[:, None] >= ordinal[None, :])
    return (jnp.cos(angles), jnp.sin(angles), allowed_mask)


def gelu_tanh(values):
    return jax.nn.gelu(values, approximate=True)


def attention_probs(queries, keys, allowed_mask, score_scale):
    scores = (
        jnp.einsum("ihd,jd->hij", queries, keys, preferred_element_type=jnp.float32) * score_scale
    )
    return jnp.where(allowed_mask[None], scores, MASKED)


def mp_total(size):
    def kernel(part, out, near, mine, far, core_send, core_recv, y_send, y_recv, back_send, back_recv):
        dp, mp = lax.axis_index("dp"), lax.axis_index("mp")
        side = lax.rem(mp, 2)
        core = (dp, mp + 1 - 2 * side)
        other = (dp, lax.rem(mp + 2, 4))
        half = part.shape[0] // 2
        pieces = near.shape[0]
        width = part.shape[1] // pieces
        own = pl.ds(pl.multiple_of(side * half, half), half)
        theirs = pl.ds(pl.multiple_of((1 - side) * half, half), half)

        def columns(i):
            return pl.ds(i * width, width)

        barrier = pltpu.get_barrier_semaphore()
        for device in (core, other):
            pl.semaphore_signal(barrier, inc=1, device_id=device, device_id_type=MESH)
        pl.semaphore_wait(barrier, 2)
        first = [
            pltpu.make_async_remote_copy(
                part.at[theirs, columns(i)], near.at[i], core_send.at[i], core_recv.at[i],
                device_id=core, device_id_type=MESH,
            )
            for i in range(pieces)
        ]
        second = [
            pltpu.make_async_remote_copy(
                mine.at[i], far.at[i], y_send.at[i], y_recv.at[i],
                device_id=other, device_id_type=MESH,
            )
            for i in range(pieces)
        ]
        third = [
            pltpu.make_async_remote_copy(
                out.at[own, columns(i)], out.at[own, columns(i)], back_send.at[i], back_recv.at[i],
                device_id=core, device_id_type=MESH,
            )
            for i in range(pieces)
        ]
        for copy in first:
            copy.start()
        for i in range(pieces):
            first[i].wait_recv()
            mine[i] = part[own, columns(i)] + near[i]
            second[i].start()
        for i in range(pieces):
            second[i].wait_recv()
            out[own, columns(i)] = mine[i] + far[i]
            third[i].start()
        for copy in third:
            copy.wait_recv()
        for copy in first + second + third:
            copy.wait_send()

    def total(identity, *parts):
        if size != 4:
            return lax.psum(parts, "mp")
        joined = jnp.concatenate(parts, axis=1)
        tokens_here, columns_here = joined.shape
        pieces = 1
        for count in (5, 4, 3, 2):
            if columns_here % (128 * count) == 0:
                pieces = count
                break
        half = (pieces, tokens_here // 2, columns_here // pieces)
        summed = pl.pallas_call(
            kernel,
            out_shape=jax.ShapeDtypeStruct(joined.shape, jnp.float32),
            in_specs=[pl.BlockSpec(memory_space=pltpu.VMEM)],
            out_specs=pl.BlockSpec(memory_space=pltpu.VMEM),
            scratch_shapes=[pltpu.VMEM(half, jnp.float32)] * 3
            + [pltpu.SemaphoreType.DMA((pieces,))] * 6,
            compiler_params=pltpu.CompilerParams(
                collective_id=identity, has_side_effects=True, vmem_limit_bytes=16 << 20
            ),
        )(joined)
        edges, start = [], 0
        for part in parts:
            edges.append(summed[:, start : start + part.shape[1]])
            start += part.shape[1]
        return tuple(edges)

    return total


def forward_loop(hidden_state, shared, adapters, tables, total, identity):
    (mixer_gain, feed_gain, query_matrix, pair_matrix, output_matrix, widen_matrix, down_matrix) = shared
    (q_in, q_out, kv_in, kv_out, o_in, o_out, w_in, w_out, d_in, d_out) = adapters
    cosine, sine, allowed = tables
    tokens_here, width = hidden_state.shape
    head = pair_matrix.shape[1] // 2
    heads = query_matrix.shape[1] // head
    rank = q_in.shape[1]
    hidden = down_matrix.shape[0]
    kept = SimpleNamespace(h=hidden_state)
    normed, kept.mixer_factor = normalize(hidden_state, mixer_gain)
    normed = normed.astype(jnp.bfloat16)
    query_rank = product(normed, q_in).astype(jnp.bfloat16)
    query_linear = product(normed, query_matrix) + product(query_rank, q_out)
    pair_rank = product(normed, kv_in.reshape(width, 2 * rank)).astype(jnp.bfloat16)
    pair_linear = product(normed, pair_matrix) + jnp.concatenate(
        [product(pair_rank[:, :rank], kv_out[0]), product(pair_rank[:, rank:], kv_out[1])], axis=1
    )
    queries = rotate(
        query_linear.reshape(tokens_here, heads, head), cosine[:, None], sine[:, None]
    ).astype(jnp.bfloat16)
    keys = rotate(pair_linear[:, :head], cosine, sine).astype(jnp.bfloat16)
    values = pair_linear[:, head:].astype(jnp.bfloat16)
    masked = attention_probs(queries, keys, allowed, 1.0 / math.sqrt(head))
    expo = jnp.exp(masked - jnp.max(masked, axis=-1, keepdims=True))
    probs = expo / jnp.sum(expo, axis=-1, keepdims=True)
    mixed = jnp.einsum(
        "hij,jd->ihd", probs.astype(jnp.bfloat16), values, preferred_element_type=jnp.float32
    )
    mixed = mixed.reshape(tokens_here, heads * head).astype(jnp.bfloat16)
    summed, output_rank = total(identity, product(mixed, output_matrix), product(mixed, o_in))
    middle = hidden_state + summed + exact_product(output_rank, o_out.astype(jnp.float32))
    fed, kept.feed_factor = normalize(middle, feed_gain)
    fed = fed.astype(jnp.bfloat16)
    widen_rank = product(fed, w_in.reshape(width, 2 * rank)).astype(jnp.bfloat16)
    gate = product(fed, widen_matrix[:, 0]) + product(widen_rank[:, :rank], w_out[0])
    up = product(fed, widen_matrix[:, 1]) + product(widen_rank[:, rank:], w_out[1])
    activated = (gelu_tanh(gate) * up).astype(jnp.bfloat16)
    shrunk, shrink_rank = total(identity + 1, product(activated, down_matrix), product(activated, d_in))
    result = middle + shrunk + exact_product(shrink_rank, d_out.astype(jnp.float32))
    vars(kept).update(
        normed=normed, query_rank=query_rank, pair_rank=pair_rank, queries=queries, keys=keys,
        values=values, probs=probs, mixed=mixed, output_rank=output_rank, middle=middle, fed=fed,
        widen_rank=widen_rank, gate=gate, up=up, activated=activated, shrink_rank=shrink_rank,
    )
    return result, kept


def reverse_loop(upstream, kept, shared, adapters, tables, total, identity):
    (mixer_gain, feed_gain, query_matrix, pair_matrix, output_matrix, widen_matrix, down_matrix) = shared
    (q_in, q_out, kv_in, kv_out, o_in, o_out, w_in, w_out, d_in, d_out) = adapters
    cosine, sine, allowed = tables
    tokens_here, width = upstream.shape
    head = pair_matrix.shape[1] // 2
    heads = query_matrix.shape[1] // head
    rank = q_in.shape[1]
    scale = 1.0 / math.sqrt(head)
    grad_feed = upstream.astype(jnp.bfloat16)
    grad_shrink_rank = product_t(grad_feed, d_out).astype(jnp.bfloat16)
    grad_activated = product_t(grad_feed, down_matrix) + product_t(grad_shrink_rank, d_in)
    gelu_value, gelu_pullback = jax.vjp(gelu_tanh, kept.gate)
    grad_gate = gelu_pullback(grad_activated * kept.up)[0].astype(jnp.bfloat16)
    grad_up = (grad_activated * gelu_value).astype(jnp.bfloat16)
    grad_fed, grad_widen_rank = total(
        identity,
        product_t(grad_gate, widen_matrix[:, 0]) + product_t(grad_up, widen_matrix[:, 1]),
        jnp.concatenate([product_t(grad_gate, w_out[0]), product_t(grad_up, w_out[1])], axis=1),
    )
    grad_widen_rank = grad_widen_rank.astype(jnp.bfloat16)
    grad_fed = grad_fed + product_t(grad_widen_rank, w_in.reshape(width, 2 * rank))
    grad_norm, feed_gain_grad = normalize_back(kept.middle, kept.feed_factor, feed_gain, grad_fed)
    grad_middle = upstream + grad_norm
    grad_attend = grad_middle.astype(jnp.bfloat16)
    grad_output_rank = product_t(grad_attend, o_out).astype(jnp.bfloat16)
    grad_mixed = product_t(grad_attend, output_matrix) + product_t(grad_output_rank, o_in)
    grad_mixed = grad_mixed.astype(jnp.bfloat16).reshape(tokens_here, heads, head)
    queries, keys, values, probs = kept.queries, kept.keys, kept.values, kept.probs
    grad_probs = jnp.einsum("ihd,jd->hij", grad_mixed, values, preferred_element_type=jnp.float32)
    delta = jnp.sum(grad_probs * probs, axis=-1, keepdims=True)
    grad_scores = (probs * (grad_probs - delta)).astype(jnp.bfloat16)
    grad_queries = scale * jnp.einsum(
        "hij,jd->ihd", grad_scores, keys, preferred_element_type=jnp.float32
    )
    grad_keys = scale * jnp.einsum(
        "hij,ihd->jd", grad_scores, queries, preferred_element_type=jnp.float32
    )
    grad_values = jnp.einsum(
        "hij,ihd->jd", probs.astype(jnp.bfloat16), grad_mixed, preferred_element_type=jnp.float32
    )
    grad_query = rotate(grad_queries, cosine[:, None], -sine[:, None])
    grad_query = grad_query.reshape(tokens_here, heads * head).astype(jnp.bfloat16)
    grad_normed, grad_query_rank, grad_pair = total(
        identity + 1,
        product_t(grad_query, query_matrix),
        product_t(grad_query, q_out),
        jnp.concatenate([rotate(grad_keys, cosine, -sine), grad_values], axis=1),
    )
    grad_query_rank = grad_query_rank.astype(jnp.bfloat16)
    grad_pair = grad_pair.astype(jnp.bfloat16)
    grad_pair_rank = jnp.concatenate(
        [product_t(grad_pair[:, :head], kv_out[0]), product_t(grad_pair[:, head:], kv_out[1])], axis=1
    ).astype(jnp.bfloat16)
    grad_normed = (
        grad_normed
        + product_t(grad_query_rank, q_in)
        + product_t(grad_pair, pair_matrix)
        + product_t(grad_pair_rank, kv_in.reshape(width, 2 * rank))
    )
    grad_norm, mixer_gain_grad = normalize_back(
        kept.h, kept.mixer_factor, mixer_gain, grad_normed
    )
    vars(kept).update(
        grad_feed=grad_feed, grad_shrink_rank=grad_shrink_rank, grad_gate=grad_gate, grad_up=grad_up,
        grad_widen_rank=grad_widen_rank, grad_attend=grad_attend, grad_output_rank=grad_output_rank,
        grad_query=grad_query, grad_query_rank=grad_query_rank, grad_pair=grad_pair,
        grad_pair_rank=grad_pair_rank, feed_gain_grad=feed_gain_grad, mixer_gain_grad=mixer_gain_grad,
    )
    return grad_middle + grad_norm


def scattered_gradients(kept, dp_size, mp_size):
    def scatter(value, axis):
        return lax.psum_scatter(value, "dp", scatter_dimension=axis, tiled=True)

    def shared_of(factors):
        return sum(product_tn(*factors(k)) for k in kept)

    def each(function):
        return jnp.stack([function(k) for k in kept], axis=0)

    def quarter(value, axis):
        block = scatter(value, axis)
        size = block.shape[axis] // mp_size
        return lax.dynamic_slice_in_dim(block, lax.axis_index("mp") * size, size, axis)

    width = kept[0].normed.shape[1]
    rank = kept[0].query_rank.shape[1]
    head = kept[0].grad_pair.shape[1] // 2

    def pair_outer(k):
        left, right = k.pair_rank, k.grad_pair
        return jnp.stack(
            [product_tn(left[:, :rank], right[:, :head]), product_tn(left[:, rank:], right[:, head:])]
        )

    def expand_outer(k):
        left = k.widen_rank
        return jnp.stack(
            [product_tn(left[:, :rank], k.grad_gate), product_tn(left[:, rank:], k.grad_up)]
        )

    return (
        scatter(sum(k.mixer_gain_grad for k in kept), 0),
        scatter(sum(k.feed_gain_grad for k in kept), 0),
        scatter(shared_of(lambda k: (k.normed, k.grad_query)), 0),
        quarter(shared_of(lambda k: (k.normed, k.grad_pair)), 0),
        scatter(shared_of(lambda k: (k.mixed, k.grad_attend)), 1),
        scatter(jnp.stack([shared_of(lambda k: (k.fed, k.grad_gate)), shared_of(lambda k: (k.fed, k.grad_up))], axis=1), 0),
        scatter(shared_of(lambda k: (k.activated, k.grad_feed)), 1),
        quarter(each(lambda k: product_tn(k.normed, k.grad_query_rank)), 1),
        scatter(each(lambda k: product_tn(k.query_rank, k.grad_query)), 1),
        quarter(
            each(lambda k: product_tn(k.normed, k.grad_pair_rank).reshape(width, 2, rank)), 1
        ),
        quarter(each(pair_outer), 2),
        scatter(each(lambda k: product_tn(k.mixed, k.grad_output_rank)), 2),
        scatter(
            each(lambda k: exact_tn(k.output_rank, k.grad_attend.astype(jnp.float32))), 2
        ),
        quarter(
            each(lambda k: product_tn(k.fed, k.grad_widen_rank).reshape(width, 2, rank)), 1
        ),
        scatter(each(expand_outer), 2),
        scatter(each(lambda k: product_tn(k.activated, k.grad_shrink_rank)), 2),
        scatter(each(lambda k: exact_tn(k.shrink_rank, k.grad_feed.astype(jnp.float32))), 2),
    )


WIDE = 896


def split3(value):
    high = value.astype(jnp.bfloat16)
    rest = value - high.astype(jnp.float32)
    middle = rest.astype(jnp.bfloat16)
    low = (rest - middle.astype(jnp.float32)).astype(jnp.bfloat16)
    return high, middle, low


WEIGHTS = (
    "q_in", "query", "q_out", "kv_in", "pair", "kv_out", "output", "o_in", "o_out",
    "w_in", "gate", "up", "w_out", "down", "d_in", "d_out",
)
SUM_STEP = 384


def block_kernel(*refs):
    (h_in, cot, cosine_ref, sine_ref, mask_ref, mixer_gain, feed_gain), refs = refs[:7], refs[7:]
    count = len(WEIGHTS)
    sources, refs = refs[:count], refs[count:]
    (out_ref, grad_ref, xt_ref, rt_ref, b_ref, q_ref, raw_ref), refs = refs[:7], refs[7:]
    weights, refs = refs[:count], refs[count:]
    (
        h_s, mid_s, normed_s, qr_s, kvr_s, q_s, k_s, v_s, probs_s, mixed_s, or_s, fed_s, er_s,
        gate_s, up_s, act_s, sr_s, gg_s, gu_s, g_s, gain_s, select,
        part, total, near, mine, far,
        load_sems, c_s, c_r, y_s, y_r, e_s, e_r,
    ) = refs
    W = SimpleNamespace(**dict(zip(WEIGHTS, weights)))
    dp, mp = lax.axis_index("dp"), lax.axis_index("mp")
    side = lax.rem(mp, 2)
    core = (dp, mp + 1 - 2 * side)
    other = (dp, lax.rem(mp + 2, 4))
    loads = [
        pltpu.make_async_copy(source, target, load_sems.at[i])
        for i, (source, target) in enumerate(zip(sources, weights))
    ]
    load = SimpleNamespace(**dict(zip(WEIGHTS, loads)))
    for copy in loads:
        copy.start()
    barrier = pltpu.get_barrier_semaphore()
    for device in (core, other):
        pl.semaphore_signal(barrier, inc=1, device_id=device, device_id_type=MESH)
    pl.semaphore_wait(barrier, 2)

    tokens, width = h_in.shape
    half = tokens // 2
    head = W.query.shape[1]
    rank = W.q_in.shape[2]
    hidden = W.down.shape[0]
    scale = 1.0 / math.sqrt(head)
    own = pl.ds(pl.multiple_of(side * half, half), half)
    theirs = pl.ds(pl.multiple_of((1 - side) * half, half), half)
    blocks = xt_ref.shape[1] * xt_ref.shape[2]
    block = width // blocks
    quarter = block // 4
    rank_quarter = rank // (4 * blocks)
    chunks = [(0, WIDE), (WIDE, hidden - WIDE)]

    def columns_of(size):
        return [(at, min(SUM_STEP, size - at)) for at in range(0, size, SUM_STEP)]

    def sum_over_mp(size, fill, turn):
        def pieces_of(make):
            return [make(i, pl.ds(at, n)) for i, (at, n) in enumerate(columns_of(size))]

        def remote(source, target, send, recv, device):
            return pltpu.make_async_remote_copy(
                source, target, send, recv, device_id=device, device_id_type=MESH
            )

        first = pieces_of(
            lambda i, c: remote(part.at[theirs, c], near.at[:, c], c_s.at[i], c_r.at[i], core)
        )
        second = pieces_of(
            lambda i, c: remote(
                mine.at[:, c], far.at[turn, :, c], y_s.at[turn, i], y_r.at[turn, i], other
            )
        )
        third = pieces_of(
            lambda i, c: remote(total.at[own, c], total.at[own, c], e_s.at[i], e_r.at[i], core)
        )

        def middle(i):
            at, n = columns_of(size)[i]
            first[i].wait_recv()
            mine[:, at : at + n] = part[own, at : at + n] + near[:, at : at + n]
            second[i].start()

        for i, (at, n) in enumerate(columns_of(size)):
            fill(at, n)
            first[i].start()
            if i:
                middle(i - 1)
        middle(len(first) - 1)
        for i, (at, n) in enumerate(columns_of(size)):
            second[i].wait_recv()
            total[own, at : at + n] = mine[:, at : at + n] + far[turn, :, at : at + n]
            third[i].start()
        for copy in third:
            copy.wait_recv()
        for copy in first + second + third:
            copy.wait_send()

    def dot(left, right):
        return jnp.dot(left, right, preferred_element_type=jnp.float32)

    def low(value):
        return value.astype(jnp.bfloat16)

    def spin(value, sign):
        a, b = value[:, : head // 2], value[:, head // 2 :]
        cosine, sine = cosine_ref[...], sign * sine_ref[...]
        return jnp.concatenate([a * cosine - b * sine, b * cosine + a * sine], axis=1)

    def factor_of(value):
        return lax.rsqrt(jnp.mean(value * value, axis=-1, keepdims=True) + EPSILON)

    def gelu_parts(value):
        c = math.sqrt(2.0 / math.pi)
        square = value * value
        t = jnp.tanh(c * value * (1.0 + 0.044715 * square))
        gelu = 0.5 * value * (1.0 + t)
        slope = 0.5 * (1.0 + t) + 0.5 * value * (1.0 - t * t) * c * (1.0 + 3 * 0.044715 * square)
        return gelu, slope

    h_s[0] = h_in[...].astype(jnp.float32)
    mixer, feed = mixer_gain[...], feed_gain[...]

    def forward(l, carry):
        def need(*copies):
            @pl.when(l == 0)
            def _():
                for copy in copies:
                    copy.wait()

        h = h_s[l]
        normed = low(h * factor_of(h) * mixer)
        normed_s[l] = normed
        need(load.q_in, load.query, load.q_out, load.kv_in, load.pair, load.kv_out)
        query_rank = low(dot(normed, W.q_in[l]))
        qr_s[l] = query_rank
        queries = dot(normed, W.query[...]) + dot(query_rank, W.q_out[l])
        q_s[l] = low(spin(queries, 1.0))
        pair_rank = low(dot(normed, W.kv_in[l]))
        kvr_s[l] = pair_rank
        keys = dot(normed, W.pair[:, :head]) + dot(pair_rank[:, :rank], W.kv_out[l, 0])
        k_s[l] = low(spin(keys, 1.0))
        values = dot(normed, W.pair[:, head:]) + dot(pair_rank[:, rank:], W.kv_out[l, 1])
        v_s[l] = low(values)
        scores = product_t(q_s[l], k_s[l]) * scale
        scores = jnp.where(mask_ref[...] > 0, scores, MASKED)
        expo = jnp.exp(scores - jnp.max(scores, axis=-1, keepdims=True))
        probs = expo / jnp.sum(expo, axis=-1, keepdims=True)
        probs_s[l] = probs
        mixed = low(dot(low(probs), v_s[l]))
        mixed_s[l] = mixed
        need(load.output, load.o_in, load.o_out)

        def fill_attend(at, n):
            cut = min(n, max(0, width - at))
            if cut:
                part[:, at : at + cut] = dot(mixed, W.output[:, at : at + cut])
            if cut < n:
                start = at + cut - width
                part[:, at + cut : at + n] = dot(mixed, W.o_in[l, :, start : start + n - cut])

        sum_over_mp(width + rank, fill_attend, 0)
        output_rank = total[:, width : width + rank]
        or_s[l] = output_rank
        middle = h_s[l] + total[:, :width]
        for piece in split3(output_rank):
            middle = middle + dot(piece, W.o_out[l])
        mid_s[l] = middle
        fed = low(middle * factor_of(middle) * feed)
        fed_s[l] = fed
        need(load.w_in, load.gate, load.up, load.w_out)
        widen_rank = low(dot(fed, W.w_in[l]))
        er_s[l] = widen_rank
        for at, n in chunks:
            gate = dot(fed, W.gate[:, at : at + n]) + dot(
                widen_rank[:, :rank], W.w_out[l, 0, :, at : at + n]
            )
            gate_s[l, :, at : at + n] = gate
            up = dot(fed, W.up[:, at : at + n]) + dot(
                widen_rank[:, rank:], W.w_out[l, 1, :, at : at + n]
            )
            up_s[l, :, at : at + n] = up
            act_s[:, at : at + n] = low(gelu_parts(gate)[0] * up)
        rows = pl.ds(pl.multiple_of(l * tokens, tokens), tokens)
        for i, (at, n) in enumerate(chunks):
            b_ref[4 + i, rows, :n] = act_s[:, at : at + n]
            if n < WIDE:
                b_ref[4 + i, rows, n:] = jnp.zeros((tokens, WIDE - n), jnp.bfloat16)
        need(load.down, load.d_in, load.d_out)

        def fill_feed(at, n):
            cut = min(n, max(0, width - at))
            if cut:
                part[:, at : at + cut] = dot(act_s[...], W.down[:, at : at + cut])
            if cut < n:
                start = at + cut - width
                part[:, at + cut : at + n] = dot(act_s[...], W.d_in[l, :, start : start + n - cut])

        sum_over_mp(width + rank, fill_feed, 1)
        shrink_rank = total[:, width : width + rank]
        sr_s[l] = shrink_rank
        result = mid_s[l] + total[:, :width]
        for piece in split3(shrink_rank):
            result = result + dot(piece, W.d_out[l])
        h_s[l + 1] = result
        return carry

    loops = W.q_in.shape[0]
    lax.fori_loop(0, loops, forward, 0)
    out_ref[...] = low(h_s[loops])

    g_s[...] = cot[...].astype(jnp.float32)
    gain_s[...] = jnp.zeros_like(gain_s)
    padded_quarter = select.shape[0] // blocks
    row = lax.broadcasted_iota(jnp.int32, (padded_quarter, width), 0)
    column = lax.broadcasted_iota(jnp.int32, (padded_quarter, width), 1)
    for b in range(blocks):
        hit = jnp.logical_and(column == row + (b * 4 + mp) * quarter, row < quarter)
        select[b * padded_quarter : (b + 1) * padded_quarter] = low(
            jnp.where(hit, 1.0, 0.0)
        )
    small_row = lax.broadcasted_iota(jnp.int32, (rank_quarter, rank), 0)
    small_column = lax.broadcasted_iota(jnp.int32, (rank_quarter, rank), 1)
    rank_select = low(
        jnp.concatenate(
            [
                jnp.where(small_column == small_row + (b * 4 + mp) * rank_quarter, 1.0, 0.0)
                for b in range(blocks)
            ],
            axis=0,
        )
    )
    raw_rows = raw_layout(quarter, rank_quarter, loops)

    def back(step, carry):
        l = loops - 1 - step
        lanes = pl.ds(pl.multiple_of(l * tokens, tokens), tokens)
        rows = lanes

        def keep_t(i, value):
            turned = low(value.astype(jnp.float32).T)
            for b in range(blocks):
                xt_ref[i, b % 2, b // 2, :, lanes] = turned[b * block : (b + 1) * block]

        def keep_rank(i, value):
            turned = low(value.astype(jnp.float32).T)
            size = rank // blocks
            for b in range(blocks):
                rt_ref[i, b % 2, b // 2, :, lanes] = turned[b * size : (b + 1) * size]

        upstream = g_s[...]
        grad_feed = low(upstream)
        grad_shrink = low(product_t(grad_feed, W.d_out[l]))
        for i, (at, n) in enumerate(chunks):
            grad_act = product_t(grad_feed, W.down[at : at + n]) + product_t(
                grad_shrink, W.d_in[l, at : at + n]
            )
            gelu, slope = gelu_parts(gate_s[l, :, at : at + n])
            grad_gate = low(grad_act * up_s[l, :, at : at + n] * slope)
            grad_up = low(grad_act * gelu)
            gg_s[:, at : at + n] = grad_gate
            gu_s[:, at : at + n] = grad_up
            b_ref[i, rows, :n] = grad_gate
            b_ref[2 + i, rows, :n] = grad_up
            if n < WIDE:
                b_ref[i, rows, n:] = jnp.zeros((tokens, WIDE - n), jnp.bfloat16)
                b_ref[2 + i, rows, n:] = jnp.zeros((tokens, WIDE - n), jnp.bfloat16)

        def fill_fed(at, n):
            cut = min(n, max(0, width - at))
            if cut:
                part[:, at : at + cut] = product_t(
                    gg_s[...], W.gate[at : at + cut]
                ) + product_t(gu_s[...], W.up[at : at + cut])
            while cut < n:
                start = at + cut - width
                j, offset = divmod(start, rank)
                size = min(n - cut, rank - offset)
                value = (gg_s, gu_s)[j][...]
                part[:, at + cut : at + cut + size] = product_t(
                    value, W.w_out[l, j, offset : offset + size]
                )
                cut += size

        sum_over_mp(width + 2 * rank, fill_fed, 0)
        grad_widen = low(total[:, width : width + 2 * rank])
        grad_fed = total[:, :width] + product_t(grad_widen, W.w_in[l])
        middle = mid_s[l]
        factor = factor_of(middle)
        unit = middle * factor
        scaled = grad_fed * feed
        grad_middle = upstream + factor * (
            scaled - unit * jnp.mean(scaled * unit, axis=-1, keepdims=True)
        )
        gain_s[1:2] += jnp.sum(grad_fed * unit, axis=0, keepdims=True)
        g_s[...] = grad_middle
        grad_attend = low(grad_middle)
        grad_output = low(product_t(grad_attend, W.o_out[l]))
        grad_mixed = low(
            product_t(grad_attend, W.output[...]) + product_t(grad_output, W.o_in[l])
        )
        probs = probs_s[l]
        grad_probs = product_t(grad_mixed, v_s[l])
        delta = jnp.sum(grad_probs * probs, axis=-1, keepdims=True)
        grad_scores = low(probs * (grad_probs - delta))
        grad_query = low(spin(dot(grad_scores, k_s[l]) * scale, -1.0))
        q_ref[0, rows, :] = grad_query
        q_ref[1, rows, :] = mixed_s[l]

        def fill_normed(at, n):
            if at == columns_of(width + rank + 2 * head)[0][0]:
                part[:, width + rank : width + rank + head] = spin(
                    product_tn(grad_scores, q_s[l]) * scale, -1.0
                )
                part[:, width + rank + head :] = product_tn(low(probs), grad_mixed)
            cut = min(n, max(0, width - at))
            if cut:
                part[:, at : at + cut] = product_t(grad_query, W.query[at : at + cut])
            end = min(at + n, width + rank)
            if at + cut < end:
                start = at + cut - width
                part[:, at + cut : end] = product_t(
                    grad_query, W.q_out[l, start : end - width]
                )

        sum_over_mp(width + rank + 2 * head, fill_normed, 1)
        grad_rank = low(total[:, width : width + rank])
        grad_pair = low(total[:, width + rank : width + rank + 2 * head])
        grad_pair_rank = low(
            jnp.concatenate(
                [
                    product_t(grad_pair[:, :head], W.kv_out[l, 0]),
                    product_t(grad_pair[:, head:], W.kv_out[l, 1]),
                ],
                axis=1,
            )
        )
        grad_normed = (
            total[:, :width]
            + product_t(grad_rank, W.q_in[l])
            + product_t(grad_pair, W.pair[...])
            + product_t(grad_pair_rank, W.kv_in[l])
        )
        h = h_s[l]
        factor = factor_of(h)
        unit = h * factor
        scaled = grad_normed * mixer
        g_s[...] += factor * (scaled - unit * jnp.mean(scaled * unit, axis=-1, keepdims=True))
        gain_s[0:1] += jnp.sum(grad_normed * unit, axis=0, keepdims=True)

        keep_t(0, fed_s[l])
        keep_t(1, grad_feed)
        keep_t(2, normed_s[l])
        keep_t(3, grad_attend)
        keep_rank(0, er_s[l, :, :rank])
        keep_rank(1, er_s[l, :, rank:])
        keep_rank(2, grad_shrink)
        keep_rank(3, qr_s[l])
        keep_rank(4, grad_output)

        def put(start, size, stride, value, add=False):
            for b in range(blocks):
                piece = value[b * stride : b * stride + size]
                at = pl.ds(start, size)
                if add:
                    raw_ref[b % 2, b // 2, at] += piece
                else:
                    raw_ref[b % 2, b // 2, at] = piece

        tall = raw_rows.tall
        normed_own = low(product_t(select[...], normed_s[l]))
        pair_weight = dot(normed_own, grad_pair)

        @pl.when(step == 0)
        def _():
            for j in range(2):
                put(j * tall, tall, padded_quarter, pair_weight[:, j * head : (j + 1) * head])

        @pl.when(step > 0)
        def _():
            for j in range(2):
                put(j * tall, tall, padded_quarter, pair_weight[:, j * head : (j + 1) * head], True)

        base = 2 * tall + l * raw_rows.loop

        def put_loop(i, value):
            put(pl.multiple_of(base + i * tall, 8), tall, padded_quarter, value)

        put_loop(0, dot(normed_own, grad_rank))
        for j in range(2):
            put_loop(1 + j, dot(normed_own, grad_pair_rank[:, j * rank : (j + 1) * rank]))
        fed_own = low(product_t(select[...], fed_s[l]))
        for j in range(2):
            put_loop(3 + j, dot(fed_own, grad_widen[:, j * rank : (j + 1) * rank]))
        attend_own = low(product_t(select[...], grad_attend))
        put_loop(5, sum(dot(attend_own, piece) for piece in split3(or_s[l])))
        feed_own = low(product_t(select[...], grad_feed))
        put_loop(6, sum(dot(feed_own, piece) for piece in split3(sr_s[l])))
        for j in range(2):
            rank_own = low(product_t(rank_select, kvr_s[l, :, j * rank : (j + 1) * rank]))
            put(
                pl.multiple_of(base + 7 * tall + j * rank_quarter, 8), rank_quarter, rank_quarter,
                dot(rank_own, grad_pair[:, j * head : (j + 1) * head]),
            )
        return carry

    lax.fori_loop(0, loops, back, 0)
    grad_ref[...] = g_s[...]
    for b in range(blocks):
        ends = jnp.zeros((8, head), jnp.float32)
        raw_ref[b % 2, b // 2, raw_rows.gains :] = ends
        raw_ref[b % 2, b // 2, raw_rows.gains : raw_rows.gains + 2, :block] = gain_s[
            :2, b * block : (b + 1) * block
        ]


def raw_layout(quarter, rank_quarter, loops):
    tall = -(-quarter // 8) * 8
    loop = 7 * tall + 2 * rank_quarter
    gains = 2 * tall + loops * loop
    return SimpleNamespace(tall=tall, loop=loop, gains=gains, all=gains + 8)


def block_and_factors(block_input, cotangent, segments, shared, stacked, dp_size):
    (mixer_gain, feed_gain, query, pair, output, widen, down) = shared
    (q_in, q_out, kv_in, kv_out, o_in, o_out, w_in, w_out, d_in, d_out) = stacked
    tokens, width = block_input.shape
    head = query.shape[1]
    loops, _, rank = q_in.shape
    hidden = down.shape[0]
    cosine, sine, allowed = rotary_tables(segments[0], head)
    weights = (
        q_in, query, q_out, kv_in.reshape(loops, width, 2 * rank), pair, kv_out, output, o_in, o_out,
        w_in.reshape(loops, width, 2 * rank), widen[:, 0], widen[:, 1], w_out, down, d_in, d_out,
    )
    layout = raw_layout(width // (4 * dp_size), rank // (4 * dp_size), loops)
    line = dp_size // 2
    f32, bf16 = jnp.float32, jnp.bfloat16
    shape = jax.ShapeDtypeStruct
    out_shape = (
        shape((tokens, width), bf16),
        shape((tokens, width), f32),
        shape((4, 2, line, width // dp_size, loops * tokens), bf16),
        shape((5, 2, line, rank // dp_size, loops * tokens), bf16),
        shape((6, loops * tokens, WIDE), bf16),
        shape((2, loops * tokens, head), bf16),
        shape((2, line, layout.all, head), f32),
    )
    vmem = pl.BlockSpec(memory_space=pltpu.VMEM)
    hbm = pl.BlockSpec(memory_space=pl.ANY)
    widest = width + rank + 2 * head
    pieces = -(-widest // SUM_STEP)
    dma = pltpu.SemaphoreType.DMA

    def kept(columns, dtype, count=loops):
        return pltpu.VMEM((count, tokens, columns), dtype)

    scratch = [pltpu.VMEM(w.shape, bf16) for w in weights] + [
        kept(width, f32, loops + 1), kept(width, f32), kept(width, bf16), kept(rank, bf16),
        kept(2 * rank, bf16), kept(head, bf16), kept(head, bf16), kept(head, bf16), kept(tokens, f32),
        kept(head, bf16), kept(rank, f32), kept(width, bf16), kept(2 * rank, bf16),
        kept(hidden, f32), kept(hidden, f32), pltpu.VMEM((tokens, hidden), bf16), kept(rank, f32),
        pltpu.VMEM((tokens, hidden), bf16), pltpu.VMEM((tokens, hidden), bf16),
        pltpu.VMEM((tokens, width), f32), pltpu.VMEM((8, width), f32),
        pltpu.VMEM((dp_size * 48, width), bf16),
        pltpu.VMEM((tokens, widest), f32), pltpu.VMEM((tokens, widest), f32),
        pltpu.VMEM((tokens // 2, widest), f32), pltpu.VMEM((tokens // 2, widest), f32),
        pltpu.VMEM((2, tokens // 2, widest), f32),
        dma((len(weights),)), dma((pieces,)), dma((pieces,)), dma((2, pieces)), dma((2, pieces)),
        dma((pieces,)), dma((pieces,)),
    ]
    return pl.pallas_call(
        block_kernel,
        out_shape=out_shape,
        in_specs=[vmem] * 7 + [hbm] * len(weights),
        out_specs=(vmem,) * len(out_shape),
        scratch_shapes=scratch,
        compiler_params=pltpu.CompilerParams(
            collective_id=21, has_side_effects=True, vmem_limit_bytes=60 << 20
        ),
    )(
        block_input, cotangent, cosine, sine, allowed.astype(f32), mixer_gain[None], feed_gain[None],
        *weights,
    )


def line_kernel(
    x_all, r_all, b_own, q_own, raw_all,
    main_out, side_out, raw_out,
    x_send, r_send, b_send, q_send, x_far, r_far, b_far, q_far, raw_own, raw_far,
    main_right, main_left, side_right, side_left, raw_right, raw_left,
    x_s, x_r, r_s, r_r, b_s, b_r, q_s, q_r, w_s, w_r, own_sem,
    mr_s, mr_r, ml_s, ml_r, sr_s, sr_r, sl_s, sl_r, rr_s, rr_r, rl_s, rl_r,
    credit_right, credit_left,
):
    dp, mp = lax.axis_index("dp"), lax.axis_index("mp")
    x = lax.rem(dp, 2)
    z = dp // 2
    last = 3
    pair = (dp + 1 - 2 * x, mp)
    up, down = (dp + 2, mp), (dp - 2, mp)

    barrier = pltpu.get_barrier_semaphore()
    pl.semaphore_signal(barrier, inc=1, device_id=pair, device_id_type=MESH)

    @pl.when(z > 0)
    def _():
        pl.semaphore_signal(barrier, inc=1, device_id=down, device_id_type=MESH)

    @pl.when(z < last)
    def _():
        pl.semaphore_signal(barrier, inc=1, device_id=up, device_id_type=MESH)

    pl.semaphore_wait(barrier, 1 + jnp.minimum(z, 1) + jnp.minimum(last - z, 1))

    def across(source, target, send, recv):
        return pltpu.make_async_remote_copy(
            source, target, send, recv, device_id=pair, device_id_type=MESH
        )

    def x_copy(i):
        return across(x_send.at[i], x_far.at[i], x_s.at[i], x_r.at[i])

    def r_copy(i):
        return across(r_send.at[i], r_far.at[i], r_s.at[i], r_r.at[i])

    def b_copy(i):
        return across(b_send.at[i], b_far.at[i], b_s.at[i], b_r.at[i])

    def send_x(i):
        x_send[i] = x_all[i, 1 - x].astype(jnp.float32)
        x_copy(i).start()

    def send_r(i):
        r_send[i] = r_all[i, 1 - x].astype(jnp.float32)
        r_copy(i).start()

    def send_b(i):
        b_send[i] = b_own[i].astype(jnp.float32)
        b_copy(i).start()

    q_copy = across(q_send, q_far, q_s, q_r)
    w_copy = across(raw_all.at[1 - x], raw_far, w_s, w_r)
    own_copy = pltpu.make_async_copy(raw_all.at[x], raw_own, own_sem)

    send_x(0)
    send_r(0)
    send_b(0)
    send_b(1)
    own_copy.start()

    def chain(target, step, slot, steps, value, out, right, left, r_s, r_r, l_s, l_r, credits):
        def move(buffer, send, recv, i, s, device):
            return pltpu.make_async_remote_copy(
                buffer.at[i, s], buffer.at[i, s], send.at[i, s], recv.at[i, s],
                device_id=device, device_id_type=MESH,
            )

        def pass_on(i, buffer, send, recv, onward, source, is_first, credit):
            if credits:

                @pl.when(step >= 1)
                def _():
                    move(buffer, send, recv, i, 1 - slot, onward).wait_send()

                    @pl.when(jnp.logical_and(jnp.logical_not(is_first), step <= steps - 2))
                    def _():
                        pl.semaphore_signal(
                            credit.at[i], inc=1, device_id=source, device_id_type=MESH
                        )

            @pl.when(is_first)
            def _():
                buffer[i, slot] = value

            @pl.when(jnp.logical_not(is_first))
            def _():
                move(buffer, send, recv, i, slot, onward).wait_recv()
                buffer[i, slot] += value

            if credits:

                @pl.when(step >= 2)
                def _():
                    pl.semaphore_wait(credit.at[i], 1)

            move(buffer, send, recv, i, slot, onward).start()

        @pl.when(target > z)
        def _():
            pass_on(target - 1, right, r_s, r_r, up, down, z == 0, credit_right)

        @pl.when(target < z)
        def _():
            pass_on(target, left, l_s, l_r, down, up, z == last, credit_left)

        @pl.when(target == z)
        def _():
            out[...] = value

            @pl.when(z > 0)
            def _():
                move(right, r_s, r_r, z - 1, slot, up).wait_recv()
                out[...] += right[z - 1, slot]
                if credits:

                    @pl.when(step <= steps - 3)
                    def _():
                        pl.semaphore_signal(
                            credit_right.at[z - 1], inc=1, device_id=down, device_id_type=MESH
                        )

            @pl.when(z < last)
            def _():
                move(left, l_s, l_r, z, slot, down).wait_recv()
                out[...] += left[z, slot]
                if credits:

                    @pl.when(step <= steps - 3)
                    def _():
                        pl.semaphore_signal(
                            credit_left.at[z], inc=1, device_id=up, device_id_type=MESH
                        )

    def settle(slot, right, left, r_s, l_s):
        for target in range(4):

            @pl.when(target > z)
            def _():
                i = target - 1
                pltpu.make_async_remote_copy(
                    right.at[i, slot], right.at[i, slot], r_s.at[i, slot], r_s.at[i, slot],
                    device_id=up, device_id_type=MESH,
                ).wait_send()

            @pl.when(target < z)
            def _():
                pltpu.make_async_remote_copy(
                    left.at[target, slot], left.at[target, slot], l_s.at[target, slot], l_s.at[target, slot],
                    device_id=down, device_id_type=MESH,
                ).wait_send()

    def order(turn):
        def near(end):
            return jnp.where(
                end == 0,
                3 - turn,
                jnp.where(turn == 0, 3, jnp.where(turn == 1, 0, 4 - turn)),
            )

        return jnp.where(z < 2, near(z), 3 - near(3 - z))

    def dot(left, right):
        return jnp.dot(
            left.astype(jnp.bfloat16), right.astype(jnp.bfloat16), preferred_element_type=jnp.float32
        )

    steps = b_own.shape[0]

    def left_times(x_index, group, target, own, far):
        half = own.shape[0] // 2
        rank_own, rank_far = r_all[group, x, target], r_far[group, target].astype(jnp.bfloat16)
        return [
            dot(x_all[x_index, x, target], own) + dot(x_far[x_index, target], far),
            dot(rank_own[:, :half], own[:half]) + dot(rank_far[:, :half], far[:half]),
            dot(rank_own[:, half:], own[half:]) + dot(rank_far[:, half:], far[half:]),
        ]

    def turn_body(at, carry):
        step, turn = at // 4, lax.rem(at, 4)
        slot = lax.rem(step, 2)
        group = step // 2
        target = order(turn)

        @pl.when(turn == 0)
        def _():
            b_copy(step).wait_recv()

            @pl.when(slot == 0)
            def _():
                r_copy(group).wait_recv()

            @pl.when(step == 0)
            def _():
                x_copy(0).wait_recv()

            @pl.when(step == 4)
            def _():
                x_copy(1).wait_recv()

            @pl.when(step + 2 < steps)
            def _():
                @pl.when(slot == 0)
                def _():
                    send_r(group + 1)

                @pl.when(step == 2)
                def _():
                    send_x(1)

                send_b(step + 2)

            @pl.when(step == steps - 2)
            def _():
                send_x(2)
                send_x(3)
                send_r(3)
                send_r(4)
                q_send[...] = q_own[...].astype(jnp.float32)
                q_copy.start()

            @pl.when(step == steps - 1)
            def _():
                w_copy.start()

        value = jnp.concatenate(
            left_times(
                group // 2, group, target, b_own[step], b_far[step].astype(jnp.bfloat16)
            ),
            axis=0,
        )
        chain(
            target, step, slot, steps, value, main_out.at[step], main_right, main_left,
            mr_s, mr_r, ml_s, ml_r, True,
        )
        return carry

    lax.fori_loop(0, 4 * steps, turn_body, 0)

    for i in (2, 3):
        x_copy(i).wait_recv()
    for i in (3, 4):
        r_copy(i).wait_recv()
    q_copy.wait_recv()

    def side_body(turn, carry):
        target = order(turn)
        value = jnp.concatenate(
            [
                jnp.concatenate(
                    left_times(
                        2 + i, 3 + i, target, q_own[i], q_far[i].astype(jnp.bfloat16)
                    ),
                    axis=0,
                )
                for i in range(2)
            ],
            axis=1,
        )
        chain(
            target, 0, 0, 1, value, side_out, side_right, side_left,
            sr_s, sr_r, sl_s, sl_r, False,
        )
        return carry

    lax.fori_loop(0, 4, side_body, 0)

    w_copy.wait_recv()
    own_copy.wait()

    def raw_body(turn, carry):
        target = order(turn)
        chain(
            target, 0, 0, 1, raw_own[target] + raw_far[target], raw_out, raw_right, raw_left,
            rr_s, rr_r, rl_s, rl_r, False,
        )
        return carry

    lax.fori_loop(0, 4, raw_body, 0)

    settle((steps - 1) % 2, main_right, main_left, mr_s, ml_s)
    settle(0, side_right, side_left, sr_s, sl_s)
    settle(0, raw_right, raw_left, rr_s, rl_s)
    for i in range(4):
        x_copy(i).wait_send()
    for i in range(5):
        r_copy(i).wait_send()
    for i in range(steps):
        b_copy(i).wait_send()
    q_copy.wait_send()
    w_copy.wait_send()


def line_gradients(factors, loops, dp_size, mp_size, hidden):
    x_all, r_all, b_own, q_own, raw = factors
    block, rank_block, head = x_all.shape[3], r_all.shape[3], q_own.shape[2]
    quarter, rank_quarter = block // mp_size, rank_block // mp_size
    layout = raw_layout(quarter, rank_quarter, loops)
    rows = block + loops * rank_block
    steps = b_own.shape[0]
    vmem = pl.BlockSpec(memory_space=pltpu.VMEM)
    hbm = pl.BlockSpec(memory_space=pl.ANY)
    dma = pltpu.SemaphoreType.DMA
    f32 = jnp.float32
    line = dp_size // 2 - 1
    half_x = pltpu.VMEM((x_all.shape[0], *x_all.shape[2:]), f32)
    half_r = pltpu.VMEM((r_all.shape[0], *r_all.shape[2:]), f32)
    whole_b, whole_q = pltpu.VMEM(b_own.shape, f32), pltpu.VMEM(q_own.shape, f32)
    main, side, rest = pl.pallas_call(
        line_kernel,
        out_shape=(
            jax.ShapeDtypeStruct((steps, rows, WIDE), f32),
            jax.ShapeDtypeStruct((rows, 2 * head), f32),
            jax.ShapeDtypeStruct((layout.all, head), f32),
        ),
        in_specs=[vmem] * 4 + [hbm],
        out_specs=(vmem, vmem, vmem),
        scratch_shapes=[half_x, half_r, whole_b, whole_q] * 2
        + [pltpu.VMEM(raw.shape[1:], f32)] * 2
        + [pltpu.VMEM((line, 2, rows, WIDE), f32)] * 2
        + [pltpu.VMEM((line, 1, rows, 2 * head), f32)] * 2
        + [pltpu.VMEM((line, 1, layout.all, head), f32)] * 2
        + [dma((4,))] * 2 + [dma((5,))] * 2 + [dma((steps,))] * 2 + [dma] * 5
        + [dma((line, 2))] * 4 + [dma((line, 1))] * 8
        + [pltpu.SemaphoreType.REGULAR((line,))] * 2,
        compiler_params=pltpu.CompilerParams(
            collective_id=20, has_side_effects=True, vmem_limit_bytes=60 << 20
        ),
    )(x_all, r_all, b_own, q_own, raw)

    wide = [
        jnp.concatenate([main[2 * i], main[2 * i + 1][:, : hidden - WIDE]], axis=1) for i in range(3)
    ]
    narrow = [side[:, :head], side[:, head:]]

    def shared_rows(value):
        return value[:block]

    def loop_rows(value, i):
        return value[block + i * rank_block : block + (i + 1) * rank_block]

    tall = layout.tall

    def raw_rows(start, size):
        return rest[start : start + size]

    pair_weight = jnp.concatenate([raw_rows(0, quarter), raw_rows(tall, quarter)], axis=1)
    query_inner, pair_inner, expand_inner, pair_outer, outers = [], [], [], [], []
    for i in range(loops):
        base = 2 * tall + i * layout.loop
        own = [raw_rows(base + j * tall, quarter) for j in range(7)]
        query_inner.append(own[0])
        pair_inner.append(jnp.stack(own[1:3], axis=1))
        expand_inner.append(jnp.stack(own[3:5], axis=1))
        outers += own[5:7]
        pair_outer.append(
            jnp.stack([raw_rows(base + 7 * tall + j * rank_quarter, rank_quarter) for j in range(2)])
        )
    outers = lax.all_gather(jnp.stack(outers), "mp")
    outers = jnp.swapaxes(outers, 0, 1).reshape(2 * loops, block, -1).swapaxes(1, 2)
    gains = rest[layout.gains : layout.gains + 2, :block]
    stack = jnp.stack
    return (
        gains[0],
        gains[1],
        shared_rows(narrow[0]),
        pair_weight,
        shared_rows(narrow[1]).T,
        stack([shared_rows(wide[0]), shared_rows(wide[1])], axis=1),
        shared_rows(wide[2]).T,
        stack(query_inner),
        stack([loop_rows(narrow[0], i) for i in range(loops)]),
        stack(pair_inner),
        stack(pair_outer),
        stack([loop_rows(narrow[1], i).T for i in range(loops)]),
        outers[0::2],
        stack(expand_inner),
        stack([stack([loop_rows(wide[j], i) for j in range(2)]) for i in range(loops)]),
        stack([loop_rows(wide[2], i).T for i in range(loops)]),
        outers[1::2],
    )


def per_device(dp_size, mp_size, block_input, cotangent, segments, *parameters):
    shared, stacked = parameters[:7], parameters[7:]
    loops = stacked[0].shape[0]
    if dp_size == 8 and mp_size == 4 and loops == 2:
        output, input_grad, *factors = block_and_factors(
            block_input, cotangent, segments, shared, stacked, dp_size
        )
        gradients = line_gradients(factors, loops, dp_size, mp_size, shared[6].shape[0])
        return (output, input_grad, *gradients)
    tables = rotary_tables(segments[0], shared[3].shape[1] // 2)
    total = mp_total(mp_size)
    state = block_input.astype(jnp.float32)
    kept_all = []
    for i in range(loops):
        state, kept = forward_loop(state, shared, [v[i] for v in stacked], tables, total, 1)
        kept_all.append(kept)
    upstream = cotangent.astype(jnp.float32)
    for i in reversed(range(loops)):
        upstream = reverse_loop(
            upstream, kept_all[i], shared, [v[i] for v in stacked], tables, total, 3
        )
    return (state.astype(jnp.bfloat16), upstream, *scattered_gradients(kept_all, dp_size, mp_size))


def solution(mesh):
    in_specs = (
        P("dp", None),
        P("dp", None),
        P("dp", None),
        P(),
        P(),
        P(None, "mp"),
        P(),
        P("mp", None),
        P(None, None, "mp"),
        P("mp", None),
        P(),
        P(None, None, "mp"),
        P(),
        P(),
        P(None, "mp", None),
        P(),
        P(),
        P(None, None, None, "mp"),
        P(None, "mp", None),
        P(),
    )
    out_specs = (
        P("dp", None),
        P("dp", None),
        P("dp"),
        P("dp"),
        P("dp", "mp"),
        P(("dp", "mp"), None),
        P("mp", "dp"),
        P("dp", None, "mp"),
        P("mp", "dp"),
        P(None, ("dp", "mp"), None),
        P(None, "dp", "mp"),
        P(None, ("dp", "mp"), None, None),
        P(None, None, ("dp", "mp"), None),
        P(None, "mp", "dp"),
        P(None, None, "dp"),
        P(None, ("dp", "mp"), None, None),
        P(None, None, "dp", "mp"),
        P(None, "mp", "dp"),
        P(None, None, "dp"),
    )
    return jax.shard_map(
        functools.partial(per_device, mesh.shape["dp"], mesh.shape["mp"]),
        mesh=mesh, in_specs=in_specs, out_specs=out_specs, check_vma=False
    )
```

time: 1890 us -> 634 us (0.34)
  waiting for transfers between devices: 1450 us -> 0 us
  Pallas kernels: 0 us -> 548 us
  matrix products: 121 us -> 0 us
  blocking collectives: 124 us -> 8.12 us
  local copies, waits for them, and re-layouts: 122 us -> 65.6 us
  other arithmetic: 39.8 us -> 9.86 us
    reduce_scatter x6 -> x0, waiting for transfers between devices: 752 us -> none  [the longest x1 272 us: per_device(): lax.psum_scatter(shared_total[5], 'dp', scatter_dimension=0, tiled=True)]
    pallas_call x0 -> x2, Pallas kernels: none -> 548 us  [the longest x1 407 us: line_gradients(): pl.pallas_call(line_kernel, out_shape=(jax.ShapeDtypeStruct((steps, rows,...]
    unnamed x21 -> x0, waiting for transfers between devices: 532 us -> none
    psum x7 -> x0, waiting for transfers between devices: 166 us -> none  [the longest x2 64.3 us: forward_loop_pass(): summed, output_rank = lax.psum((head_part, rank_part), 'mp')]
    unnamed x2 -> x0, blocking collectives: 124 us -> none
    dot_general x102 -> x0, matrix products: 121 us -> none  [the longest x22 38.8 us: product_tn(): lax.dot_general(left, right, (((0,), (0,)), ((), ())), preferred_element_...]
    another operation x8 -> x3, local copies, waits for them, and re-layouts: 57.6 us -> 0.06 us  [the longest x1 0.04 us: line_gradients(): expand_inner.append(jnp.stack(own[3:5], axis=1))]
    unnamed x422 -> x27, local copies, waits for them, and re-layouts: 50.6 us -> 26.9 us
  transfers between devices with their start and end apart: 19 -> 0, of which waited for: 15 -> 0; matrix products, arithmetic and copies ran while one was open for 14% -> 0% of each run, Pallas kernels for 0% -> 0%
where the time goes in v1:
time: 634 us; the launch traced here: 632 us
  Pallas kernels  548 us (86%)
  local copies, waits for them, and re-layouts  65.6 us (10%)
  other arithmetic  9.86 us (2%)
  blocking collectives  8.12 us (1%)
    pallas_call x1, Pallas kernels, line_gradients(): pl.pallas_call(line_kernel, out_shape=(jax.ShapeDtypeStruct((steps, rows,...  407 us
    pallas_call x1, Pallas kernels, block_and_factors(): pl.pallas_call(block_kernel, out_shape=out_shape, in_specs=[vmem] * 7 + [...  141 us
    unnamed x27, local copies, waits for them, and re-layouts  26.9 us

profile of v1, /device:TPU:0, one launch (start us, length us, event | category | flops | bytes accessed | tf_op | source)
XLA Modules:
  0.0 632.2 jit_solution(3379499282341334622)
XLA Ops:
  0.7 0.9 convert_reduce_fusion
  1.6 1.3 broadcast_in_dim.4.refs_5_
  2.9 1.3 broadcast_in_dim.5.refs_6_
  4.2 1.4 fusion.16.refs_4_
  5.6 1.0 multiply_sine_fusion
  6.6 6.4 %reshape.60.refs_10_ = bf16[2,1152,512]{2,1,0:T(8,128)(2,1)} reshape(bf16[2,1152,2,256]{3,2,1,0:T(2,128)(2,1)} %param.32) | data formatting | bytes 4718592 | tf_op jit(solution)/shard_map/reshape | solution.py:797
  13.0 6.6 %reshape.61.refs_16_ = bf16[2,1152,512]{2,1,0:T(8,128)(2,1)} reshape(bf16[2,1152,2,256]{3,2,1,0:T(2,128)(2,1)} %param.36) | data formatting | bytes 4718592 | tf_op jit(solution)/shard_map/reshape | solution.py:798
  19.6 3.8 copy.59.refs_19_
  23.4 5.7 fusion.17
  29.0 6.5 %copy.68 = bf16[1152,1,1728]{2,0,1:T(8,128)(2,1)} copy(bf16[1152,1,1728]{0,2,1:T(8,128)(2,1)} %get-tuple-element.96) | data formatting | bytes 7962624
  35.5 6.4 %copy.67 = bf16[1152,1,1728]{2,0,1:T(8,128)(2,1)} copy(bf16[1152,1,1728]{0,2,1:T(8,128)(2,1)} %get-tuple-element.97) | data formatting | bytes 7962624
  41.9 141.0 %shard_map.339 = (bf16[128,1152]{1,0:T(8,128)(2,1)}, f32[128,1152]{1,0:T(8,128)}, bf16[4,2,4,144,256]{4,3,2,1,0:T(8,128)(2,1)}, bf16[5,2,4,32,256]{4,3,2,1,0:T(8...) custom-call(bf16[128,1152]{1,0:T(8,128)(2,1)} %refs_0_.1, ...), custom_call_target="tpu_custom_call" | custom-call | tf_op jit(solution)/shard_map/pallas_call | solution.py:836
  182.9 406.9 %shard_map.340 = (f32[6,208,896]{2,1,0:T(8,128)}, f32[208,512]{1,0:T(8,128)}, f32[680,256]{1,0:T(8,128)}) custom-call(bf16[4,2,4,144,256]{4,3,2,1,0:T(8,128)(2,1)} %get-tuple-element.31.x_all, bf16[5,2,4,32,256]{4,3,2,1,0:T(8,128)(2,1)} %get-tuple-element.32.r_all, bf16[6,256,896]{2,1,0:T(8,128)(2,1)} %get-tuple-element.33.b_own, ...), custom_call_target="tpu_custom_call" | custom-call | tf_op jit(solution)/shard_map/pallas_call | solution.py:1163
  589.8 3.7 slice_bitcast_fusion
  594.8 0.7 copy.65
  595.5 0.7 copy.62
  596.9 0.7 slice_bitcast_fusion.6
  598.9 0.7 copy.63
  599.7 0.7 fusion.11
  600.4 8.1 %all-gather = f32[16,36,256]{2,1,0:T(8,128)S(1)} all-gather(f32[4,36,256]{2,1,0:T(8,128)S(1)} %pad_maximum_fusion.7), channel_id=2, replica_groups=mesh['dp'=8,'mp'=4] {'mp'}, dimensions={0}, use_global_device_ids=true | all-gather | bytes 737280 | tf_op jit(solution)/shard_map/all_gather | solution.py:1213
  608.5 1.0 copy.60
  609.5 5.3 slice.210
  614.8 6.0 slice.199
  620.9 1.7 copy.64
  622.6 0.7 copy.66
  623.4 1.0 copy-done
  624.7 1.0 fusion.1
  625.7 0.8 pad_maximum_fusion.2
  626.7 2.9 copy.61
  629.7 1.0 pad_maximum_fusion.1
  630.7 0.7 copy.71
  631.4 0.8 copy.72
  (37 shorter events, 3.9 us)
Async XLA Ops:
  13.0 6.6 %copy-start.2 = (bf16[2,2,256,1728]{2,3,1,0:T(8,128)(2,1)S(1)}, bf16[2,2,256,1728]{2,3,1,0:T(8,128)(2,1)}, u32[]{:S(2)}) copy-start(bf16[2,2,256,1728]{2,3,1,0:T(8,128)(2,1)} %param.37) | copy-start | bytes 10616836
  589.8 3.7 copy-start.4
  593.5 3.4 copy-start.6
  623.3 1.1 copy-start
  623.3 1.3 copy-start.1
  626.7 2.9 copy-start.3
  629.6 1.1 copy-start.7
  629.6 1.8 copy-start.5

commit v2 on v1

--- a/solution.py
+++ b/solution.py
@@ -376,13 +376,16 @@
     (h_in, cot, cosine_ref, sine_ref, mask_ref, mixer_gain, feed_gain), refs = refs[:7], refs[7:]
     count = len(WEIGHTS)
     sources, refs = refs[:count], refs[count:]
-    (out_ref, grad_ref, xt_ref, rt_ref, b_ref, q_ref, raw_ref), refs = refs[:7], refs[7:]
+    (
+        out_ref, grad_ref, raw_ref, x_all, r_all, b_all, q_all, x_got, r_got, b_got, x_end, r_end, b_end,
+    ), refs = refs[:13], refs[13:]
     weights, refs = refs[:count], refs[count:]
     (
         h_s, mid_s, normed_s, qr_s, kvr_s, q_s, k_s, v_s, probs_s, mixed_s, or_s, fed_s, er_s,
         gate_s, up_s, act_s, sr_s, gg_s, gu_s, g_s, gain_s, select,
-        part, total, near, mine, far,
+        part, total, near, mine, far, xs, rs, bs, qs,
         load_sems, c_s, c_r, y_s, y_r, e_s, e_r,
+        xl, rl, bl, ql, x_s, x_r, r_s, r_r, b_s, b_r, xe_s, xe_r, re_s, re_r, be_s, be_r,
     ) = refs
     W = SimpleNamespace(**dict(zip(WEIGHTS, weights)))
     dp, mp = lax.axis_index("dp"), lax.axis_index("mp")
@@ -396,36 +399,188 @@
     load = SimpleNamespace(**dict(zip(WEIGHTS, loads)))
     for copy in loads:
         copy.start()
+    x = lax.rem(dp, 2)
+    z = dp // 2
+    pair = (dp + 1 - 2 * x, mp)
+    near_end = (dp + 2 - 4 * lax.rem(z, 2), mp)
+    is_end = jnp.logical_or(z == 0, z == 3)
     barrier = pltpu.get_barrier_semaphore()
-    for device in (core, other):
+    for device in (core, other, pair, near_end):
         pl.semaphore_signal(barrier, inc=1, device_id=device, device_id_type=MESH)
-    pl.semaphore_wait(barrier, 2)
+    pl.semaphore_wait(barrier, 4)
 
     tokens, width = h_in.shape
     half = tokens // 2
     head = W.query.shape[1]
     rank = W.q_in.shape[2]
     hidden = W.down.shape[0]
+    loops = W.q_in.shape[0]
     scale = 1.0 / math.sqrt(head)
     own = pl.ds(pl.multiple_of(side * half, half), half)
     theirs = pl.ds(pl.multiple_of((1 - side) * half, half), half)
-    blocks = xt_ref.shape[1] * xt_ref.shape[2]
+    blocks = x_all.shape[1] * x_all.shape[2]
     block = width // blocks
     quarter = block // 4
     rank_quarter = rank // (4 * blocks)
     chunks = [(0, WIDE), (WIDE, hidden - WIDE)]
 
+    def remote(source, target, send, recv, device):
+        return pltpu.make_async_remote_copy(
+            source, target, send, recv, device_id=device, device_id_type=MESH
+        )
+
+    def span(l):
+        return pl.ds(pl.multiple_of(l * tokens, tokens), tokens)
+
+    def end_span(l, is_far):
+        return pl.ds(pl.multiple_of((2 * l + is_far) * tokens, tokens), tokens)
+
+    def x_copies(i, l):
+        across = onward = None
+        if i < 2:
+            across = remote(
+                xs.at[i, 1 - x], x_got.at[i, :, :, span(l)], x_s.at[i, l], x_r.at[i, l], pair
+            )
+        if i == 1:
+            onward = remote(
+                xs.at[i, x], x_end.at[:, :, end_span(l, 0)], xe_s.at[0, l], xe_r.at[0, l], near_end
+            )
+        return pltpu.make_async_copy(xs.at[i], x_all.at[i, :, :, :, span(l)], xl.at[i, l]), across, onward
+
+    def r_copies(i, l):
+        across = onward = None
+        if i < 3:
+            across = remote(
+                rs.at[i, 1 - x], r_got.at[i, :, :, span(l)], r_s.at[i, l], r_r.at[i, l], pair
+            )
+        if i == 2:
+            onward = remote(
+                rs.at[i, x], r_end.at[:, :, end_span(l, 0)], re_s.at[0, l], re_r.at[0, l], near_end
+            )
+        return pltpu.make_async_copy(rs.at[i], r_all.at[i, :, :, :, span(l)], rl.at[i, l]), across, onward
+
+    def b_copies(i, l):
+        across = onward = None
+        if i in (0, 4, 5):
+            k = max(0, i - 3)
+            across = remote(bs.at[i], b_got.at[k, span(l)], b_s.at[k, l], b_r.at[k, l], pair)
+        if i >= 4:
+            onward = remote(
+                bs.at[i], b_end.at[i - 4, end_span(l, 0)],
+                be_s.at[i - 4, 0, l], be_r.at[i - 4, 0, l], near_end,
+            )
+        return pltpu.make_async_copy(bs.at[i], b_all.at[i, span(l)], bl.at[i, l]), across, onward
+
+    def q_copies(i, l):
+        return pltpu.make_async_copy(qs.at[i], q_all.at[i, span(l)], ql.at[i, l]), None, None
+
+    def launch(copies):
+        local, across, onward = copies
+        local.start()
+        if across is not None:
+            across.start()
+        if onward is not None:
+
+            @pl.when(is_end)
+            def _():
+                onward.start()
+
+    def finish(copies):
+        local, across, onward = copies
+        local.wait()
+        if across is not None:
+            across.wait_send()
+        if onward is not None:
+
+            @pl.when(is_end)
+            def _():
+                onward.wait_send()
+
+    def far_feed(l):
+        return [
+            remote(
+                x_got.at[1, :, :, span(l)], x_end.at[:, :, end_span(l, 1)],
+                xe_s.at[1, l], xe_r.at[1, l], near_end,
+            ),
+            remote(
+                r_got.at[2, :, :, span(l)], r_end.at[:, :, end_span(l, 1)],
+                re_s.at[1, l], re_r.at[1, l], near_end,
+            ),
+        ]
+
+    def far_act(l):
+        return [
+            remote(
+                b_got.at[1 + k, span(l)], b_end.at[k, end_span(l, 1)],
+                be_s.at[k, 1, l], be_r.at[k, 1, l], near_end,
+            )
+            for k in range(2)
+        ]
+
+    def pass_act(l):
+        for i in (4, 5):
+            b_copies(i, l)[1].wait_recv()
+
+        @pl.when(is_end)
+        def _():
+            for copy in far_act(l):
+                copy.start()
+
+    def pass_feed(l):
+        x_copies(1, l)[1].wait_recv()
+        r_copies(2, l)[1].wait_recv()
+
+        @pl.when(is_end)
+        def _():
+            for copy in far_feed(l):
+                copy.start()
+
+    def ship_x(i, l, value, again, before):
+        @pl.when(again)
+        def _():
+            finish(x_copies(i, before))
+
+        turned = value.astype(jnp.float32).T
+        for b in range(blocks):
+            xs[i, b % 2, b // 2] = turned[b * block : (b + 1) * block]
+        launch(x_copies(i, l))
+
+    def ship_r(i, l, value, again, before):
+        @pl.when(again)
+        def _():
+            finish(r_copies(i, before))
+
+        turned = value.astype(jnp.float32).T
+        size = rank // blocks
+        for b in range(blocks):
+            rs[i, b % 2, b // 2] = turned[b * size : (b + 1) * size]
+        launch(r_copies(i, l))
+
+    def ship_b(i, l, value, again, before):
+        @pl.when(again)
+        def _():
+            finish(b_copies(i, before))
+
+        n = value.shape[1]
+        bs[i, :, :n] = value.astype(jnp.float32)
+        if n < WIDE:
+            bs[i, :, n:] = jnp.zeros((tokens, WIDE - n), jnp.float32)
+        launch(b_copies(i, l))
+
+    def ship_q(i, l, value, again, before):
+        @pl.when(again)
+        def _():
+            finish(q_copies(i, before))
+
+        qs[i] = value.astype(jnp.float32)
+        launch(q_copies(i, l))
+
     def columns_of(size):
         return [(at, min(SUM_STEP, size - at)) for at in range(0, size, SUM_STEP)]
 
-    def sum_over_mp(size, fill, turn):
+    def sum_over_mp(size, fill, turn, idle):
         def pieces_of(make):
             return [make(i, pl.ds(at, n)) for i, (at, n) in enumerate(columns_of(size))]
-
-        def remote(source, target, send, recv, device):
-            return pltpu.make_async_remote_copy(
-                source, target, send, recv, device_id=device, device_id_type=MESH
-            )
 
         first = pieces_of(
             lambda i, c: remote(part.at[theirs, c], near.at[:, c], c_s.at[i], c_r.at[i], core)
@@ -451,6 +606,7 @@
             if i:
                 middle(i - 1)
         middle(len(first) - 1)
+        idle()
         for i, (at, n) in enumerate(columns_of(size)):
             second[i].wait_recv()
             total[own, at : at + n] = mine[:, at : at + n] + far[turn, :, at : at + n]
@@ -523,7 +679,14 @@
                 start = at + cut - width
                 part[:, at + cut : at + n] = dot(mixed, W.o_in[l, :, start : start + n - cut])
 
-        sum_over_mp(width + rank, fill_attend, 0)
+        again = l > 0
+
+        def idle_attend():
+            ship_x(2, l, normed, again, 0)
+            ship_r(3, l, query_rank, again, 0)
+            ship_q(1, l, mixed, again, 0)
+
+        sum_over_mp(width + rank, fill_attend, 0, idle_attend)
         output_rank = total[:, width : width + rank]
         or_s[l] = output_rank
         middle = h_s[l] + total[:, :width]
@@ -545,11 +708,7 @@
             )
             up_s[l, :, at : at + n] = up
             act_s[:, at : at + n] = low(gelu_parts(gate)[0] * up)
-        rows = pl.ds(pl.multiple_of(l * tokens, tokens), tokens)
-        for i, (at, n) in enumerate(chunks):
-            b_ref[4 + i, rows, :n] = act_s[:, at : at + n]
-            if n < WIDE:
-                b_ref[4 + i, rows, n:] = jnp.zeros((tokens, WIDE - n), jnp.bfloat16)
+            ship_b(4 + at // WIDE, l, act_s[:, at : at + n], again, 0)
         need(load.down, load.d_in, load.d_out)
 
         def fill_feed(at, n):
@@ -560,7 +719,16 @@
                 start = at + cut - width
                 part[:, at + cut : at + n] = dot(act_s[...], W.d_in[l, :, start : start + n - cut])
 
-        sum_over_mp(width + rank, fill_feed, 1)
+        def idle_feed():
+            ship_x(0, l, fed, again, 0)
+            ship_r(0, l, widen_rank[:, :rank], again, 0)
+            ship_r(1, l, widen_rank[:, rank:], again, 0)
+
+            @pl.when(again)
+            def _():
+                pass_act(0)
+
+        sum_over_mp(width + rank, fill_feed, 1, idle_feed)
         shrink_rank = total[:, width : width + rank]
         sr_s[l] = shrink_rank
         result = mid_s[l] + total[:, :width]
@@ -569,7 +737,6 @@
         h_s[l + 1] = result
         return carry
 
-    loops = W.q_in.shape[0]
     lax.fori_loop(0, loops, forward, 0)
     out_ref[...] = low(h_s[loops])
 
@@ -598,19 +765,8 @@
 
     def back(step, carry):
         l = loops - 1 - step
-        lanes = pl.ds(pl.multiple_of(l * tokens, tokens), tokens)
-        rows = lanes
-
-        def keep_t(i, value):
-            turned = low(value.astype(jnp.float32).T)
-            for b in range(blocks):
-                xt_ref[i, b % 2, b // 2, :, lanes] = turned[b * block : (b + 1) * block]
-
-        def keep_rank(i, value):
-            turned = low(value.astype(jnp.float32).T)
-            size = rank // blocks
-            for b in range(blocks):
-                rt_ref[i, b % 2, b // 2, :, lanes] = turned[b * size : (b + 1) * size]
+        again = step > 0
+        before = loops - 1
 
         upstream = g_s[...]
         grad_feed = low(upstream)
@@ -624,11 +780,8 @@
             grad_up = low(grad_act * gelu)
             gg_s[:, at : at + n] = grad_gate
             gu_s[:, at : at + n] = grad_up
-            b_ref[i, rows, :n] = grad_gate
-            b_ref[2 + i, rows, :n] = grad_up
-            if n < WIDE:
-                b_ref[i, rows, n:] = jnp.zeros((tokens, WIDE - n), jnp.bfloat16)
-                b_ref[2 + i, rows, n:] = jnp.zeros((tokens, WIDE - n), jnp.bfloat16)
+            ship_b(i, l, grad_gate, again, before)
+            ship_b(2 + i, l, grad_up, again, before)
 
         def fill_fed(at, n):
             cut = min(n, max(0, width - at))
@@ -646,7 +799,15 @@
                 )
                 cut += size
 
-        sum_over_mp(width + 2 * rank, fill_fed, 0)
+        def idle_fed():
+            ship_x(1, l, grad_feed, again, before)
+            ship_r(2, l, grad_shrink, again, before)
+
+            @pl.when(step == 0)
+            def _():
+                pass_act(loops - 1)
+
+        sum_over_mp(width + 2 * rank, fill_fed, 0, idle_fed)
         grad_widen = low(total[:, width : width + 2 * rank])
         grad_fed = total[:, :width] + product_t(grad_widen, W.w_in[l])
         middle = mid_s[l]
@@ -668,8 +829,6 @@
         delta = jnp.sum(grad_probs * probs, axis=-1, keepdims=True)
         grad_scores = low(probs * (grad_probs - delta))
         grad_query = low(spin(dot(grad_scores, k_s[l]) * scale, -1.0))
-        q_ref[0, rows, :] = grad_query
-        q_ref[1, rows, :] = mixed_s[l]
 
         def fill_normed(at, n):
             if at == columns_of(width + rank + 2 * head)[0][0]:
@@ -687,7 +846,13 @@
                     grad_query, W.q_out[l, start : end - width]
                 )
 
-        sum_over_mp(width + rank + 2 * head, fill_normed, 1)
+        def idle_normed():
+            ship_q(0, l, grad_query, again, before)
+            ship_x(3, l, grad_attend, again, before)
+            ship_r(4, l, grad_output, again, before)
+            pass_feed(l)
+
+        sum_over_mp(width + rank + 2 * head, fill_normed, 1, idle_normed)
         grad_rank = low(total[:, width : width + rank])
         grad_pair = low(total[:, width + rank : width + rank + 2 * head])
         grad_pair_rank = low(
@@ -711,16 +876,6 @@
         scaled = grad_normed * mixer
         g_s[...] += factor * (scaled - unit * jnp.mean(scaled * unit, axis=-1, keepdims=True))
         gain_s[0:1] += jnp.sum(grad_normed * unit, axis=0, keepdims=True)
-
-        keep_t(0, fed_s[l])
-        keep_t(1, grad_feed)
-        keep_t(2, normed_s[l])
-        keep_t(3, grad_attend)
-        keep_rank(0, er_s[l, :, :rank])
-        keep_rank(1, er_s[l, :, rank:])
-        keep_rank(2, grad_shrink)
-        keep_rank(3, qr_s[l])
-        keep_rank(4, grad_output)
 
         def put(start, size, stride, value, add=False):
             for b in range(blocks):
@@ -769,6 +924,29 @@
         return carry
 
     lax.fori_loop(0, loops, back, 0)
+    last = loops - 1
+    for copies in (
+        x_copies(0, last), x_copies(2, last), r_copies(0, last), r_copies(1, last), r_copies(3, last),
+        b_copies(4, last), b_copies(5, last), q_copies(1, last),
+        x_copies(1, 0), x_copies(3, 0), r_copies(2, 0), r_copies(4, 0),
+        b_copies(0, 0), b_copies(1, 0), b_copies(2, 0), b_copies(3, 0), q_copies(0, 0),
+    ):
+        finish(copies)
+    for l in range(loops):
+        for copies in (x_copies(0, l), r_copies(0, l), r_copies(1, l), b_copies(0, l)):
+            copies[1].wait_recv()
+
+        @pl.when(is_end)
+        def _():
+            for copy in far_feed(l) + far_act(l):
+                copy.wait_send()
+
+        @pl.when(jnp.logical_not(is_end))
+        def _():
+            onward = [x_copies(1, l)[2], r_copies(2, l)[2], b_copies(4, l)[2], b_copies(5, l)[2]]
+            for copy in onward + far_feed(l) + far_act(l):
+                copy.wait_recv()
+
     grad_ref[...] = g_s[...]
     for b in range(blocks):
         ends = jnp.zeros((8, head), jnp.float32)
@@ -801,14 +979,21 @@
     line = dp_size // 2
     f32, bf16 = jnp.float32, jnp.bfloat16
     shape = jax.ShapeDtypeStruct
+    block, rank_block, both = width // dp_size, rank // dp_size, loops * tokens
     out_shape = (
         shape((tokens, width), bf16),
         shape((tokens, width), f32),
-        shape((4, 2, line, width // dp_size, loops * tokens), bf16),
-        shape((5, 2, line, rank // dp_size, loops * tokens), bf16),
-        shape((6, loops * tokens, WIDE), bf16),
-        shape((2, loops * tokens, head), bf16),
         shape((2, line, layout.all, head), f32),
+        shape((4, 2, line, block, both), f32),
+        shape((5, 2, line, rank_block, both), f32),
+        shape((6, both, WIDE), f32),
+        shape((2, both, head), f32),
+        shape((2, line, block, both), f32),
+        shape((3, line, rank_block, both), f32),
+        shape((3, both, WIDE), f32),
+        shape((line, block, 2 * both), f32),
+        shape((line, rank_block, 2 * both), f32),
+        shape((2, 2 * both, WIDE), f32),
     )
     vmem = pl.BlockSpec(memory_space=pltpu.VMEM)
     hbm = pl.BlockSpec(memory_space=pl.ANY)
@@ -830,14 +1015,19 @@
         pltpu.VMEM((tokens, widest), f32), pltpu.VMEM((tokens, widest), f32),
         pltpu.VMEM((tokens // 2, widest), f32), pltpu.VMEM((tokens // 2, widest), f32),
         pltpu.VMEM((2, tokens // 2, widest), f32),
+        pltpu.VMEM((4, 2, line, block, tokens), f32), pltpu.VMEM((5, 2, line, rank_block, tokens), f32),
+        pltpu.VMEM((6, tokens, WIDE), f32), pltpu.VMEM((2, tokens, head), f32),
         dma((len(weights),)), dma((pieces,)), dma((pieces,)), dma((2, pieces)), dma((2, pieces)),
         dma((pieces,)), dma((pieces,)),
+        dma((4, loops)), dma((5, loops)), dma((6, loops)), dma((2, loops)),
     ]
+    scratch += [dma((2, loops))] * 2 + [dma((3, loops))] * 4
+    scratch += [dma((2, loops))] * 4 + [dma((2, 2, loops))] * 2
     return pl.pallas_call(
         block_kernel,
         out_shape=out_shape,
         in_specs=[vmem] * 7 + [hbm] * len(weights),
-        out_specs=(vmem,) * len(out_shape),
+        out_specs=(vmem,) * 3 + (hbm,) * 10,
         scratch_shapes=scratch,
         compiler_params=pltpu.CompilerParams(
             collective_id=21, has_side_effects=True, vmem_limit_bytes=60 << 20
@@ -849,11 +1039,11 @@
 
 
 def line_kernel(
-    x_all, r_all, b_own, q_own, raw_all,
+    raw_all, x_all, r_all, b_all, q_all, x_got, r_got, b_got, x_end_all, r_end_all, b_end_all,
     main_out, side_out, raw_out,
-    x_send, r_send, b_send, q_send, x_far, r_far, b_far, q_far, raw_own, raw_far,
+    x_own, r_own, b_own, q_own, x_far, r_far, b_far, q_far, x_end, r_end, b_end, raw_own, raw_far, product_ref,
     main_right, main_left, side_right, side_left, raw_right, raw_left,
-    x_s, x_r, r_s, r_r, b_s, b_r, q_s, q_r, w_s, w_r, own_sem,
+    x_s, x_r, r_s, r_r, b_s, b_r, q_s, q_r, w_s, w_r, local_sems, step_sems,
     mr_s, mr_r, ml_s, ml_r, sr_s, sr_r, sl_s, sl_r, rr_s, rr_r, rl_s, rl_r,
     credit_right, credit_left,
 ):
@@ -883,35 +1073,58 @@
         )
 
     def x_copy(i):
-        return across(x_send.at[i], x_far.at[i], x_s.at[i], x_r.at[i])
+        return across(x_all.at[i, 1 - x], x_far.at[i], x_s.at[i - 2], x_r.at[i - 2])
 
     def r_copy(i):
-        return across(r_send.at[i], r_far.at[i], r_s.at[i], r_r.at[i])
+        return across(r_all.at[i, 1 - x], r_far.at[i], r_s.at[i - 3], r_r.at[i - 3])
 
     def b_copy(i):
-        return across(b_send.at[i], b_far.at[i], b_s.at[i], b_r.at[i])
-
-    def send_x(i):
-        x_send[i] = x_all[i, 1 - x].astype(jnp.float32)
-        x_copy(i).start()
-
-    def send_r(i):
-        r_send[i] = r_all[i, 1 - x].astype(jnp.float32)
-        r_copy(i).start()
-
-    def send_b(i):
-        b_send[i] = b_own[i].astype(jnp.float32)
-        b_copy(i).start()
-
-    q_copy = across(q_send, q_far, q_s, q_r)
+        return across(b_all.at[i], b_far.at[i], b_s.at[i], b_r.at[i])
+
+    q_copy = across(q_all, q_far, q_s, q_r)
     w_copy = across(raw_all.at[1 - x], raw_far, w_s, w_r)
-    own_copy = pltpu.make_async_copy(raw_all.at[x], raw_own, own_sem)
-
-    send_x(0)
-    send_r(0)
-    send_b(0)
-    send_b(1)
+
+    def here(source, target, i):
+        return pltpu.make_async_copy(source, target, local_sems.at[i])
+
+    at_start = [
+        here(x_all.at[:, x], x_own, 0),
+        here(r_all.at[:, x], r_own, 1),
+        here(x_got, x_far.at[0:2], 2),
+        here(r_got, r_far.at[0:3], 3),
+        here(b_got.at[0], b_far.at[0], 4),
+        here(b_got.at[1:3], b_far.at[4:6], 5),
+        here(q_all, q_own, 6),
+    ]
+    for_ends = [here(x_end_all, x_end, 7), here(r_end_all, r_end, 8), here(b_end_all, b_end, 9)]
+    own_copy = here(raw_all.at[x], raw_own, 10)
+    inner = jnp.logical_and(z > 0, z < last)
+
+    def chunk_of(step):
+        return jnp.where(lax.rem(step, 3) == 1, 4 + step // 3, step - (step + 1) // 3)
+
+    def b_load(step):
+        slot = lax.rem(step, 2)
+        return pltpu.make_async_copy(b_all.at[chunk_of(step)], b_own.at[slot], step_sems.at[slot])
+
+    b_copy(1).start()
+    b_load(0).start()
+    for copy in at_start:
+        copy.start()
+
+    @pl.when(inner)
+    def _():
+        for copy in for_ends:
+            copy.start()
+
     own_copy.start()
+    for copy in at_start:
+        copy.wait()
+
+    @pl.when(inner)
+    def _():
+        for copy in for_ends:
+            copy.wait()
 
     def chain(target, step, slot, steps, value, out, right, left, r_s, r_r, l_s, l_r, credits):
         def move(buffer, send, recv, i, s, device):
@@ -920,71 +1133,87 @@
                 device_id=device, device_id_type=MESH,
             )
 
-        def pass_on(i, buffer, send, recv, onward, source, is_first, credit):
-            if credits:
-
-                @pl.when(step >= 1)
+        def inside(at):
+            return lax.rem(at, 3) == 1 if credits else at < 0
+
+        def free(credit, i, source, at, from_end):
+            @pl.when(
+                jnp.logical_and(
+                    at <= steps - 1,
+                    jnp.logical_not(jnp.logical_and(from_end, inside(at))),
+                )
+            )
+            def _():
+                pl.semaphore_signal(credit.at[i], inc=1, device_id=source, device_id_type=MESH)
+
+        def pass_on(i, buffer, send, recv, onward, source, at_end, next_to_end, credit):
+            has_source = jnp.logical_not(
+                jnp.logical_or(at_end, jnp.logical_and(next_to_end, inside(step)))
+            )
+
+            @pl.when(jnp.logical_not(jnp.logical_and(at_end, inside(step))))
+            def _():
+                if credits:
+
+                    @pl.when(step >= 1)
+                    def _():
+                        skipped = jnp.logical_and(at_end, inside(step - 1))
+                        before = jnp.where(skipped, slot, 1 - slot)
+                        move(buffer, send, recv, i, before, onward).wait_send()
+
+                        @pl.when(jnp.logical_not(at_end))
+                        def _():
+                            free(credit, i, source, step + 1, next_to_end)
+
+                @pl.when(jnp.logical_not(has_source))
                 def _():
-                    move(buffer, send, recv, i, 1 - slot, onward).wait_send()
-
-                    @pl.when(jnp.logical_and(jnp.logical_not(is_first), step <= steps - 2))
+                    buffer[i, slot] = value()
+
+                @pl.when(has_source)
+                def _():
+                    product = value()
+                    move(buffer, send, recv, i, slot, onward).wait_recv()
+                    buffer[i, slot] += product
+
+                if credits:
+
+                    @pl.when(step >= 2)
                     def _():
-                        pl.semaphore_signal(
-                            credit.at[i], inc=1, device_id=source, device_id_type=MESH
-                        )
-
-            @pl.when(is_first)
-            def _():
-                buffer[i, slot] = value
-
-            @pl.when(jnp.logical_not(is_first))
-            def _():
-                move(buffer, send, recv, i, slot, onward).wait_recv()
-                buffer[i, slot] += value
-
-            if credits:
-
-                @pl.when(step >= 2)
-                def _():
-                    pl.semaphore_wait(credit.at[i], 1)
-
-            move(buffer, send, recv, i, slot, onward).start()
+                        pl.semaphore_wait(credit.at[i], 1)
+
+                move(buffer, send, recv, i, slot, onward).start()
 
         @pl.when(target > z)
         def _():
-            pass_on(target - 1, right, r_s, r_r, up, down, z == 0, credit_right)
+            pass_on(target - 1, right, r_s, r_r, up, down, z == 0, z == 1, credit_right)
 
         @pl.when(target < z)
         def _():
-            pass_on(target, left, l_s, l_r, down, up, z == last, credit_left)
+            pass_on(target, left, l_s, l_r, down, up, z == last, z == last - 1, credit_left)
 
         @pl.when(target == z)
         def _():
-            out[...] = value
+            out[...] = value()
 
             @pl.when(z > 0)
             def _():
-                move(right, r_s, r_r, z - 1, slot, up).wait_recv()
-                out[...] += right[z - 1, slot]
+                @pl.when(jnp.logical_not(jnp.logical_and(z == 1, inside(step))))
+                def _():
+                    move(right, r_s, r_r, z - 1, slot, up).wait_recv()
+                    out[...] += right[z - 1, slot]
+
                 if credits:
-
-                    @pl.when(step <= steps - 3)
-                    def _():
-                        pl.semaphore_signal(
-                            credit_right.at[z - 1], inc=1, device_id=down, device_id_type=MESH
-                        )
+                    free(credit_right, z - 1, down, step + 2, z == 1)
 
             @pl.when(z < last)
             def _():
-                move(left, l_s, l_r, z, slot, down).wait_recv()
-                out[...] += left[z, slot]
+                @pl.when(jnp.logical_not(jnp.logical_and(z == last - 1, inside(step))))
+                def _():
+                    move(left, l_s, l_r, z, slot, down).wait_recv()
+                    out[...] += left[z, slot]
+
                 if credits:
-
-                    @pl.when(step <= steps - 3)
-                    def _():
-                        pl.semaphore_signal(
-                            credit_left.at[z], inc=1, device_id=up, device_id_type=MESH
-                        )
+                    free(credit_left, z, up, step + 2, z == last - 1)
 
     def settle(slot, right, left, r_s, l_s):
         for target in range(4):
@@ -1019,13 +1248,13 @@
             left.astype(jnp.bfloat16), right.astype(jnp.bfloat16), preferred_element_type=jnp.float32
         )
 
-    steps = b_own.shape[0]
+    steps = b_all.shape[0]
 
     def left_times(x_index, group, target, own, far):
         half = own.shape[0] // 2
-        rank_own, rank_far = r_all[group, x, target], r_far[group, target].astype(jnp.bfloat16)
+        rank_own, rank_far = r_own[group, target], r_far[group, target]
         return [
-            dot(x_all[x_index, x, target], own) + dot(x_far[x_index, target], far),
+            dot(x_own[x_index, target], own) + dot(x_far[x_index, target], far),
             dot(rank_own[:, :half], own[:half]) + dot(rank_far[:, :half], far[:half]),
             dot(rank_own[:, half:], own[half:]) + dot(rank_far[:, half:], far[half:]),
         ]
@@ -1033,58 +1262,70 @@
     def turn_body(at, carry):
         step, turn = at // 4, lax.rem(at, 4)
         slot = lax.rem(step, 2)
-        group = step // 2
+        chunk = chunk_of(step)
+        group = chunk // 2
         target = order(turn)
 
         @pl.when(turn == 0)
         def _():
-            b_copy(step).wait_recv()
-
-            @pl.when(slot == 0)
-            def _():
-                r_copy(group).wait_recv()
-
-            @pl.when(step == 0)
-            def _():
-                x_copy(0).wait_recv()
+            b_load(step).wait()
+
+            @pl.when(step < steps - 1)
+            def _():
+                b_load(step + 1).start()
+
+            @pl.when(jnp.logical_and(chunk >= 1, chunk <= 3))
+            def _():
+                b_copy(chunk).wait_recv()
+
+            @pl.when(step == 1)
+            def _():
+                b_copy(2).start()
+
+            @pl.when(step == 2)
+            def _():
+                b_copy(3).start()
+
+            @pl.when(step == 3)
+            def _():
+                x_copy(2).start()
+                x_copy(3).start()
+                r_copy(3).start()
+                r_copy(4).start()
+                q_copy.start()
 
             @pl.when(step == 4)
             def _():
-                x_copy(1).wait_recv()
-
-            @pl.when(step + 2 < steps)
-            def _():
-                @pl.when(slot == 0)
-                def _():
-                    send_r(group + 1)
-
-                @pl.when(step == 2)
-                def _():
-                    send_x(1)
-
-                send_b(step + 2)
-
-            @pl.when(step == steps - 2)
-            def _():
-                send_x(2)
-                send_x(3)
-                send_r(3)
-                send_r(4)
-                q_send[...] = q_own[...].astype(jnp.float32)
-                q_copy.start()
-
-            @pl.when(step == steps - 1)
-            def _():
                 w_copy.start()
 
-        value = jnp.concatenate(
-            left_times(
-                group // 2, group, target, b_own[step], b_far[step].astype(jnp.bfloat16)
-            ),
-            axis=0,
-        )
+        def value():
+            parts = left_times(
+                group // 2, group, target,
+                b_own[slot].astype(jnp.bfloat16), b_far[chunk].astype(jnp.bfloat16),
+            )
+            product_ref[...] = jnp.concatenate(parts, axis=0)
+            beyond = jnp.logical_or(
+                jnp.logical_and(z == 1, target >= 1),
+                jnp.logical_and(z == last - 1, target <= last - 1),
+            )
+
+            @pl.when(jnp.logical_and(beyond, chunk >= 4))
+            def _():
+                end = b_end[jnp.maximum(chunk - 4, 0)].astype(jnp.bfloat16)
+                middle = end.shape[0] // 2
+                product_ref[...] += jnp.concatenate(
+                    [
+                        dot(x_end[target], end),
+                        dot(r_end[target, :, :middle], end[:middle]),
+                        dot(r_end[target, :, middle:], end[middle:]),
+                    ],
+                    axis=0,
+                )
+
+            return product_ref[...]
+
         chain(
-            target, step, slot, steps, value, main_out.at[step], main_right, main_left,
+            target, step, slot, steps, value, main_out.at[chunk], main_right, main_left,
             mr_s, mr_r, ml_s, ml_r, True,
         )
         return carry
@@ -1099,18 +1340,16 @@
 
     def side_body(turn, carry):
         target = order(turn)
-        value = jnp.concatenate(
-            [
-                jnp.concatenate(
-                    left_times(
-                        2 + i, 3 + i, target, q_own[i], q_far[i].astype(jnp.bfloat16)
-                    ),
-                    axis=0,
+
+        def value():
+            parts = [
+                left_times(
+                    2 + i, 3 + i, target, q_own[i].astype(jnp.bfloat16), q_far[i].astype(jnp.bfloat16)
                 )
                 for i in range(2)
-            ],
-            axis=1,
-        )
+            ]
+            return jnp.concatenate([jnp.concatenate(p, axis=0) for p in parts], axis=1)
+
         chain(
             target, 0, 0, 1, value, side_out, side_right, side_left,
             sr_s, sr_r, sl_s, sl_r, False,
@@ -1125,7 +1364,7 @@
     def raw_body(turn, carry):
         target = order(turn)
         chain(
-            target, 0, 0, 1, raw_own[target] + raw_far[target], raw_out, raw_right, raw_left,
+            target, 0, 0, 1, lambda: raw_own[target] + raw_far[target], raw_out, raw_right, raw_left,
             rr_s, rr_r, rl_s, rl_r, False,
         )
         return carry
@@ -1135,23 +1374,19 @@
     settle((steps - 1) % 2, main_right, main_left, mr_s, ml_s)
     settle(0, side_right, side_left, sr_s, sl_s)
     settle(0, raw_right, raw_left, rr_s, rl_s)
-    for i in range(4):
-        x_copy(i).wait_send()
-    for i in range(5):
-        r_copy(i).wait_send()
-    for i in range(steps):
-        b_copy(i).wait_send()
+    for copy in (x_copy(2), x_copy(3), r_copy(3), r_copy(4), b_copy(1), b_copy(2), b_copy(3)):
+        copy.wait_send()
     q_copy.wait_send()
     w_copy.wait_send()
 
 
 def line_gradients(factors, loops, dp_size, mp_size, hidden):
-    x_all, r_all, b_own, q_own, raw = factors
-    block, rank_block, head = x_all.shape[3], r_all.shape[3], q_own.shape[2]
+    raw, x_all, r_all, b_all, q_all, x_got, r_got, b_got, x_end, r_end, b_end = factors
+    block, rank_block, head = x_all.shape[3], r_all.shape[3], q_all.shape[2]
     quarter, rank_quarter = block // mp_size, rank_block // mp_size
     layout = raw_layout(quarter, rank_quarter, loops)
     rows = block + loops * rank_block
-    steps = b_own.shape[0]
+    steps = b_all.shape[0]
     vmem = pl.BlockSpec(memory_space=pltpu.VMEM)
     hbm = pl.BlockSpec(memory_space=pl.ANY)
     dma = pltpu.SemaphoreType.DMA
@@ -1159,7 +1394,7 @@
     line = dp_size // 2 - 1
     half_x = pltpu.VMEM((x_all.shape[0], *x_all.shape[2:]), f32)
     half_r = pltpu.VMEM((r_all.shape[0], *r_all.shape[2:]), f32)
-    whole_b, whole_q = pltpu.VMEM(b_own.shape, f32), pltpu.VMEM(q_own.shape, f32)
+    whole_b, whole_q = pltpu.VMEM(b_all.shape, f32), pltpu.VMEM(q_all.shape, f32)
     main, side, rest = pl.pallas_call(
         line_kernel,
         out_shape=(
@@ -1167,20 +1402,23 @@
             jax.ShapeDtypeStruct((rows, 2 * head), f32),
             jax.ShapeDtypeStruct((layout.all, head), f32),
         ),
-        in_specs=[vmem] * 4 + [hbm],
+        in_specs=[hbm] * 11,
         out_specs=(vmem, vmem, vmem),
-        scratch_shapes=[half_x, half_r, whole_b, whole_q] * 2
+        scratch_shapes=[half_x, half_r, pltpu.VMEM((2, *b_all.shape[1:]), f32), whole_q]
+        + [half_x, half_r, whole_b, whole_q]
+        + [pltpu.VMEM(v.shape, f32) for v in (x_end, r_end, b_end)]
         + [pltpu.VMEM(raw.shape[1:], f32)] * 2
+        + [pltpu.VMEM((rows, WIDE), f32)]
         + [pltpu.VMEM((line, 2, rows, WIDE), f32)] * 2
         + [pltpu.VMEM((line, 1, rows, 2 * head), f32)] * 2
         + [pltpu.VMEM((line, 1, layout.all, head), f32)] * 2
-        + [dma((4,))] * 2 + [dma((5,))] * 2 + [dma((steps,))] * 2 + [dma] * 5
+        + [dma((2,))] * 4 + [dma((steps,))] * 2 + [dma] * 4 + [dma((11,)), dma((2,))]
         + [dma((line, 2))] * 4 + [dma((line, 1))] * 8
         + [pltpu.SemaphoreType.REGULAR((line,))] * 2,
         compiler_params=pltpu.CompilerParams(
             collective_id=20, has_side_effects=True, vmem_limit_bytes=60 << 20
         ),
-    )(x_all, r_all, b_own, q_own, raw)
+    )(*factors)
 
     wide = [
         jnp.concatenate([main[2 * i], main[2 * i + 1][:, : hidden - WIDE]], axis=1) for i in range(3)

time: 634 us -> 570 us (0.90)
  Pallas kernels: 548 us -> 483 us
    pallas_call x1, Pallas kernels: 407 us -> 335 us  [line_gradients(): pl.pallas_call(line_kernel, out_shape=(jax.ShapeDtypeStruct((steps, rows,...]
where the time goes in v2:
time: 570 us; the launch traced here: 565 us
  Pallas kernels  483 us (85%)
  local copies, waits for them, and re-layouts  65.4 us (11%)
  other arithmetic  9.86 us (2%)
  blocking collectives  6.86 us (1%)
    pallas_call x1, Pallas kernels, line_gradients(): pl.pallas_call(line_kernel, out_shape=(jax.ShapeDtypeStruct((steps, rows,...  335 us
    pallas_call x1, Pallas kernels, block_and_factors(): pl.pallas_call(block_kernel, out_shape=out_shape, in_specs=[vmem] * 7 + [...  147 us
    unnamed x27, local copies, waits for them, and re-layouts  26.9 us

profile of v2, /device:TPU:0, one launch (start us, length us, event | category | flops | bytes accessed | tf_op | source)
XLA Modules:
  0.0 565.5 jit_solution(51893253526882949)
XLA Ops:
  0.7 0.9 convert_reduce_fusion
  1.6 1.3 broadcast_in_dim.4.refs_5_
  2.9 1.3 broadcast_in_dim.5.refs_6_
  4.2 1.4 fusion.16.refs_4_
  5.6 1.0 multiply_sine_fusion
  6.6 6.4 %reshape.60.refs_10_ = bf16[2,1152,512]{2,1,0:T(8,128)(2,1)} reshape(bf16[2,1152,2,256]{3,2,1,0:T(2,128)(2,1)} %param.32) | data formatting | bytes 4718592 | tf_op jit(solution)/shard_map/reshape | solution.py:975
  13.0 6.6 %reshape.61.refs_16_ = bf16[2,1152,512]{2,1,0:T(8,128)(2,1)} reshape(bf16[2,1152,2,256]{3,2,1,0:T(2,128)(2,1)} %param.36) | data formatting | bytes 4718592 | tf_op jit(solution)/shard_map/reshape | solution.py:976
  19.5 3.8 copy.59.refs_19_
  23.4 5.5 fusion.17
  28.9 6.4 %copy.68 = bf16[1152,1,1728]{2,0,1:T(8,128)(2,1)} copy(bf16[1152,1,1728]{0,2,1:T(8,128)(2,1)} %get-tuple-element.108) | data formatting | bytes 7962624
  35.3 6.5 %copy.67 = bf16[1152,1,1728]{2,0,1:T(8,128)(2,1)} copy(bf16[1152,1,1728]{0,2,1:T(8,128)(2,1)} %get-tuple-element.109) | data formatting | bytes 7962624
  41.8 147.2 %shard_map.339 = (bf16[128,1152]{1,0:T(8,128)(2,1)}, f32[128,1152]{1,0:T(8,128)}, f32[2,4,680,256]{3,2,1,0:T(8,128)}, f32[4,2,4,144,256]{4,3,2,1,0:T(8,128)}, f3...) custom-call(bf16[128,1152]{1,0:T(8,128)(2,1)} %refs_0_.1, ...), custom_call_target="tpu_custom_call" | custom-call | tf_op jit(solution)/shard_map/pallas_call | solution.py:1026
  189.0 335.3 %shard_map.340 = (f32[6,208,896]{2,1,0:T(8,128)}, f32[208,512]{1,0:T(8,128)}, f32[680,256]{1,0:T(8,128)}) custom-call(f32[2,4,680,256]{3,2,1,0:T(8,128)} %get-tuple-element.37.raw_all, f32[4,2,4,144,256]{4,3,2,1,0:T(8,128)} %get-tuple-element.38.x_all, f32[5,2,4,32,256]{4,3,2,1,0:T(8,128)} %get-tuple-element.39.r_all, ...), custom_call_target="tpu_custom_call" | custom-call | tf_op jit(solution)/shard_map/pallas_call | solution.py:1398
  524.3 3.7 slice_bitcast_fusion
  529.3 0.7 copy.65
  530.1 0.7 copy.62
  531.4 0.7 slice_bitcast_fusion.6
  533.5 0.7 copy.63
  534.2 0.7 fusion.11
  534.9 6.9 %all-gather = f32[16,36,256]{2,1,0:T(8,128)S(1)} all-gather(f32[4,36,256]{2,1,0:T(8,128)S(1)} %pad_maximum_fusion.7), channel_id=2, replica_groups=mesh['dp'=8,'mp'=4] {'mp'}, dimensions={0}, use_global_device_ids=true | all-gather | bytes 737280 | tf_op jit(solution)/shard_map/all_gather | solution.py:1451
  541.8 1.0 copy.60
  542.8 5.3 slice.210
  548.1 6.0 %slice.199 = f32[2,256,144]{1,0,2:T(2,128)} slice(f32[4,256,144]{1,0,2:T(4,128)} %bitcast.124), slice={[0:4:2], [0:256:1], [0:144:1]} | slice | bytes 589824 | tf_op jit(solution)/shard_map/slice | solution.py:1468
  554.2 1.7 copy.64
  555.9 0.7 copy.66
  556.7 1.0 copy-done
  558.0 1.0 fusion.1
  559.0 0.8 pad_maximum_fusion.2
  560.0 2.9 copy.61
  563.0 1.0 pad_maximum_fusion.1
  564.0 0.7 copy.71
  564.7 0.8 copy.72
  (37 shorter events, 3.9 us)
Async XLA Ops:
  13.0 6.6 %copy-start.2 = (bf16[2,2,256,1728]{2,3,1,0:T(8,128)(2,1)S(1)}, bf16[2,2,256,1728]{2,3,1,0:T(8,128)(2,1)}, u32[]{:S(2)}) copy-start(bf16[2,2,256,1728]{2,3,1,0:T(8,128)(2,1)} %param.37) | copy-start | bytes 10616836
  524.3 3.7 copy-start.4
  528.0 3.4 copy-start.6
  556.6 1.1 copy-start
  556.6 1.3 copy-start.1
  560.0 2.9 copy-start.3
  562.9 1.1 copy-start.7
  562.9 1.8 copy-start.5

commit v3 on v2

--- a/solution.py
+++ b/solution.py
@@ -367,13 +367,13 @@
 
 WEIGHTS = (
     "q_in", "query", "q_out", "kv_in", "pair", "kv_out", "output", "o_in", "o_out",
-    "w_in", "gate", "up", "w_out", "down", "d_in", "d_out",
+    "w_in", "wide", "w_out", "down", "d_in", "d_out",
 )
 SUM_STEP = 384
 
 
 def block_kernel(*refs):
-    (h_in, cot, cosine_ref, sine_ref, mask_ref, mixer_gain, feed_gain), refs = refs[:7], refs[7:]
+    (h_in, cot, segments, mixer_gain, feed_gain), refs = refs[:5], refs[5:]
     count = len(WEIGHTS)
     sources, refs = refs[:count], refs[count:]
     (
@@ -383,7 +383,7 @@
     (
         h_s, mid_s, normed_s, qr_s, kvr_s, q_s, k_s, v_s, probs_s, mixed_s, or_s, fed_s, er_s,
         gate_s, up_s, act_s, sr_s, gg_s, gu_s, g_s, gain_s, select,
-        part, total, near, mine, far, xs, rs, bs, qs,
+        part, total, near, mine, far, xs, rs, bs, qs, kv_flat, w_flat, cosine_ref, sine_ref, mask_ref,
         load_sems, c_s, c_r, y_s, y_r, e_s, e_r,
         xl, rl, bl, ql, x_s, x_r, r_s, r_r, b_s, b_r, xe_s, xe_r, re_s, re_r, be_s, be_r,
     ) = refs
@@ -638,6 +638,19 @@
         slope = 0.5 * (1.0 + t) + 0.5 * value * (1.0 - t * t) * c * (1.0 + 3 * 0.044715 * square)
         return gelu, slope
 
+    across_row = jnp.broadcast_to(segments[...].astype(jnp.float32), (tokens, tokens))
+    down_row = across_row.T
+    at_row = lax.broadcasted_iota(jnp.int32, (tokens, tokens), 0)
+    at_column = lax.broadcasted_iota(jnp.int32, (tokens, tokens), 1)
+    earlier = jnp.sum(jnp.where(across_row < down_row, 1.0, 0.0), axis=1, keepdims=True)
+    position = at_row[:, : head // 2].astype(jnp.float32) - earlier
+    exponent = at_column[:, : head // 2].astype(jnp.float32) * (-2.0 / head)
+    angles = position * jnp.exp(exponent * math.log(10000.0))
+    cosine_ref[...] = jnp.cos(angles)
+    sine_ref[...] = jnp.sin(angles)
+    mask_ref[...] = jnp.where(
+        jnp.logical_and(across_row == down_row, at_row >= at_column), 1.0, 0.0
+    )
     h_s[0] = h_in[...].astype(jnp.float32)
     mixer, feed = mixer_gain[...], feed_gain[...]
 
@@ -652,11 +665,16 @@
         normed = low(h * factor_of(h) * mixer)
         normed_s[l] = normed
         need(load.q_in, load.query, load.q_out, load.kv_in, load.pair, load.kv_out)
+
+        @pl.when(l == 0)
+        def _():
+            kv_flat[0] = W.kv_in[0].reshape(width, 2 * rank)
+
         query_rank = low(dot(normed, W.q_in[l]))
         qr_s[l] = query_rank
         queries = dot(normed, W.query[...]) + dot(query_rank, W.q_out[l])
         q_s[l] = low(spin(queries, 1.0))
-        pair_rank = low(dot(normed, W.kv_in[l]))
+        pair_rank = low(dot(normed, kv_flat[l]))
         kvr_s[l] = pair_rank
         keys = dot(normed, W.pair[:, :head]) + dot(pair_rank[:, :rank], W.kv_out[l, 0])
         k_s[l] = low(spin(keys, 1.0))
@@ -686,6 +704,14 @@
             ship_r(3, l, query_rank, again, 0)
             ship_q(1, l, mixed, again, 0)
 
+            @pl.when(l == 0)
+            def _():
+                load.w_in.wait()
+                for i in range(loops):
+                    w_flat[i] = W.w_in[i].reshape(width, 2 * rank)
+                for i in range(1, loops):
+                    kv_flat[i] = W.kv_in[i].reshape(width, 2 * rank)
+
         sum_over_mp(width + rank, fill_attend, 0, idle_attend)
         output_rank = total[:, width : width + rank]
         or_s[l] = output_rank
@@ -695,16 +721,16 @@
         mid_s[l] = middle
         fed = low(middle * factor_of(middle) * feed)
         fed_s[l] = fed
-        need(load.w_in, load.gate, load.up, load.w_out)
-        widen_rank = low(dot(fed, W.w_in[l]))
+        need(load.wide, load.w_out)
+        widen_rank = low(dot(fed, w_flat[l]))
         er_s[l] = widen_rank
         for at, n in chunks:
-            gate = dot(fed, W.gate[:, at : at + n]) + dot(
-                widen_rank[:, :rank], W.w_out[l, 0, :, at : at + n]
+            gate = product_t(fed, W.wide[0, at : at + n]) + product_t(
+                widen_rank[:, :rank], W.w_out[l, 0, at : at + n]
             )
             gate_s[l, :, at : at + n] = gate
-            up = dot(fed, W.up[:, at : at + n]) + dot(
-                widen_rank[:, rank:], W.w_out[l, 1, :, at : at + n]
+            up = product_t(fed, W.wide[1, at : at + n]) + product_t(
+                widen_rank[:, rank:], W.w_out[l, 1, at : at + n]
             )
             up_s[l, :, at : at + n] = up
             act_s[:, at : at + n] = low(gelu_parts(gate)[0] * up)
@@ -786,16 +812,16 @@
         def fill_fed(at, n):
             cut = min(n, max(0, width - at))
             if cut:
-                part[:, at : at + cut] = product_t(
-                    gg_s[...], W.gate[at : at + cut]
-                ) + product_t(gu_s[...], W.up[at : at + cut])
+                part[:, at : at + cut] = dot(gg_s[...], W.wide[0, :, at : at + cut]) + dot(
+                    gu_s[...], W.wide[1, :, at : at + cut]
+                )
             while cut < n:
                 start = at + cut - width
                 j, offset = divmod(start, rank)
                 size = min(n - cut, rank - offset)
                 value = (gg_s, gu_s)[j][...]
-                part[:, at + cut : at + cut + size] = product_t(
-                    value, W.w_out[l, j, offset : offset + size]
+                part[:, at + cut : at + cut + size] = dot(
+                    value, W.w_out[l, j, :, offset : offset + size]
                 )
                 cut += size
 
@@ -809,7 +835,7 @@
 
         sum_over_mp(width + 2 * rank, fill_fed, 0, idle_fed)
         grad_widen = low(total[:, width : width + 2 * rank])
-        grad_fed = total[:, :width] + product_t(grad_widen, W.w_in[l])
+        grad_fed = total[:, :width] + product_t(grad_widen, w_flat[l])
         middle = mid_s[l]
         factor = factor_of(middle)
         unit = middle * factor
@@ -868,7 +894,7 @@
             total[:, :width]
             + product_t(grad_rank, W.q_in[l])
             + product_t(grad_pair, W.pair[...])
-            + product_t(grad_pair_rank, W.kv_in[l])
+            + product_t(grad_pair_rank, kv_flat[l])
         )
         h = h_s[l]
         factor = factor_of(h)
@@ -970,10 +996,9 @@
     head = query.shape[1]
     loops, _, rank = q_in.shape
     hidden = down.shape[0]
-    cosine, sine, allowed = rotary_tables(segments[0], head)
     weights = (
-        q_in, query, q_out, kv_in.reshape(loops, width, 2 * rank), pair, kv_out, output, o_in, o_out,
-        w_in.reshape(loops, width, 2 * rank), widen[:, 0], widen[:, 1], w_out, down, d_in, d_out,
+        q_in, query, q_out, kv_in, pair, kv_out, output, o_in, o_out,
+        w_in, widen.transpose(1, 2, 0), w_out.swapaxes(2, 3), down, d_in, d_out,
     )
     layout = raw_layout(width // (4 * dp_size), rank // (4 * dp_size), loops)
     line = dp_size // 2
@@ -1017,6 +1042,9 @@
         pltpu.VMEM((2, tokens // 2, widest), f32),
         pltpu.VMEM((4, 2, line, block, tokens), f32), pltpu.VMEM((5, 2, line, rank_block, tokens), f32),
         pltpu.VMEM((6, tokens, WIDE), f32), pltpu.VMEM((2, tokens, head), f32),
+        pltpu.VMEM((loops, width, 2 * rank), bf16), pltpu.VMEM((loops, width, 2 * rank), bf16),
+        pltpu.VMEM((tokens, head // 2), f32), pltpu.VMEM((tokens, head // 2), f32),
+        pltpu.VMEM((tokens, tokens), f32),
         dma((len(weights),)), dma((pieces,)), dma((pieces,)), dma((2, pieces)), dma((2, pieces)),
         dma((pieces,)), dma((pieces,)),
         dma((4, loops)), dma((5, loops)), dma((6, loops)), dma((2, loops)),
@@ -1026,24 +1054,25 @@
     return pl.pallas_call(
         block_kernel,
         out_shape=out_shape,
-        in_specs=[vmem] * 7 + [hbm] * len(weights),
+        in_specs=[vmem] * 5 + [hbm] * len(weights),
         out_specs=(vmem,) * 3 + (hbm,) * 10,
         scratch_shapes=scratch,
         compiler_params=pltpu.CompilerParams(
-            collective_id=21, has_side_effects=True, vmem_limit_bytes=60 << 20
+            collective_id=21, has_side_effects=True, vmem_limit_bytes=63 << 20
         ),
     )(
-        block_input, cotangent, cosine, sine, allowed.astype(f32), mixer_gain[None], feed_gain[None],
+        block_input, cotangent, segments, mixer_gain[None], feed_gain[None],
         *weights,
     )
 
 
 def line_kernel(
     raw_all, x_all, r_all, b_all, q_all, x_got, r_got, b_got, x_end_all, r_end_all, b_end_all,
-    main_out, side_out, raw_out,
+    gains_out, q_w, pair_w, o_w, e_w, s_w, q_i, q_o, p_i, p_o, o_i, o_o, e_i, e_o, s_i, s_o,
+    main_out, side_out, raw_out, around,
     x_own, r_own, b_own, q_own, x_far, r_far, b_far, q_far, x_end, r_end, b_end, raw_own, raw_far, product_ref,
     main_right, main_left, side_right, side_left, raw_right, raw_left,
-    x_s, x_r, r_s, r_r, b_s, b_r, q_s, q_r, w_s, w_r, local_sems, step_sems,
+    x_s, x_r, r_s, r_r, b_s, b_r, q_s, q_r, w_s, w_r, local_sems, step_sems, around_s, around_r,
     mr_s, mr_r, ml_s, ml_r, sr_s, sr_r, sl_s, sl_r, rr_s, rr_r, rl_s, rl_r,
     credit_right, credit_left,
 ):
@@ -1054,8 +1083,16 @@
     pair = (dp + 1 - 2 * x, mp)
     up, down = (dp + 2, mp), (dp - 2, mp)
 
+    core, other = (dp, mp + 1 - 2 * lax.rem(mp, 2)), (dp, lax.rem(mp + 2, 4))
+    hidden = s_w.shape[1]
+    block, rank_block, quarter = s_w.shape[0], s_i.shape[1], pair_w.shape[0]
+    loops, head = s_i.shape[0], q_w.shape[1]
+    layout = raw_layout(quarter, rank_block // 4, loops)
+    tall = layout.tall
+
     barrier = pltpu.get_barrier_semaphore()
-    pl.semaphore_signal(barrier, inc=1, device_id=pair, device_id_type=MESH)
+    for device in (pair, core, other):
+        pl.semaphore_signal(barrier, inc=1, device_id=device, device_id_type=MESH)
 
     @pl.when(z > 0)
     def _():
@@ -1065,7 +1102,7 @@
     def _():
         pl.semaphore_signal(barrier, inc=1, device_id=up, device_id_type=MESH)
 
-    pl.semaphore_wait(barrier, 1 + jnp.minimum(z, 1) + jnp.minimum(last - z, 1))
+    pl.semaphore_wait(barrier, 3 + jnp.minimum(z, 1) + jnp.minimum(last - z, 1))
 
     def across(source, target, send, recv):
         return pltpu.make_async_remote_copy(
@@ -1146,24 +1183,49 @@
             def _():
                 pl.semaphore_signal(credit.at[i], inc=1, device_id=source, device_id_type=MESH)
 
-        def pass_on(i, buffer, send, recv, onward, source, at_end, next_to_end, credit):
-            has_source = jnp.logical_not(
-                jnp.logical_or(at_end, jnp.logical_and(next_to_end, inside(step)))
-            )
-
-            @pl.when(jnp.logical_not(jnp.logical_and(at_end, inside(step))))
+        def pass_on(i, place, buffer, send, recv, onward, source, at_end, next_to_end, credit):
+            def here(i, s):
+                return move(buffer, send, recv, i, s, onward)
+
+            def begin():
+                if credits:
+
+                    @pl.when(step >= 3)
+                    def _():
+                        pl.semaphore_wait(credit.at[i], 1)
+
+                here(i, slot).start()
+
+            @pl.when(jnp.logical_and(at_end, jnp.logical_not(inside(step))))
+            def _():
+                buffer[i, slot] = value()
+                if credits:
+                    before = lax.rem(step + 2 - inside(step - 1).astype(jnp.int32), 3)
+                    after = jnp.where(onward[0] > dp, i - 1, i + 1)
+
+                    @pl.when(jnp.logical_and(place < 2, step >= 1))
+                    def _():
+                        here(after, before).wait_send()
+
+                    @pl.when(place == 2)
+                    def _():
+                        here(2 - i, slot).wait_send()
+
+                    begin()
+                else:
+                    begin()
+                    here(i, slot).wait_send()
+
+            @pl.when(jnp.logical_not(at_end))
             def _():
                 if credits:
 
                     @pl.when(step >= 1)
                     def _():
-                        skipped = jnp.logical_and(at_end, inside(step - 1))
-                        before = jnp.where(skipped, slot, 1 - slot)
-                        move(buffer, send, recv, i, before, onward).wait_send()
-
-                        @pl.when(jnp.logical_not(at_end))
-                        def _():
-                            free(credit, i, source, step + 1, next_to_end)
+                        here(i, lax.rem(step + 2, 3)).wait_send()
+                        free(credit, i, source, step + 2, next_to_end)
+
+                has_source = jnp.logical_not(jnp.logical_and(next_to_end, inside(step)))
 
                 @pl.when(jnp.logical_not(has_source))
                 def _():
@@ -1172,74 +1234,75 @@
                 @pl.when(has_source)
                 def _():
                     product = value()
-                    move(buffer, send, recv, i, slot, onward).wait_recv()
+                    here(i, slot).wait_recv()
                     buffer[i, slot] += product
 
-                if credits:
-
-                    @pl.when(step >= 2)
-                    def _():
-                        pl.semaphore_wait(credit.at[i], 1)
-
-                move(buffer, send, recv, i, slot, onward).start()
+                begin()
 
         @pl.when(target > z)
         def _():
-            pass_on(target - 1, right, r_s, r_r, up, down, z == 0, z == 1, credit_right)
+            pass_on(target - 1, 3 - target, right, r_s, r_r, up, down, z == 0, z == 1, credit_right)
 
         @pl.when(target < z)
         def _():
-            pass_on(target, left, l_s, l_r, down, up, z == last, z == last - 1, credit_left)
+            pass_on(target, target, left, l_s, l_r, down, up, z == last, z == last - 1, credit_left)
 
         @pl.when(target == z)
         def _():
             out[...] = value()
 
-            @pl.when(z > 0)
-            def _():
-                @pl.when(jnp.logical_not(jnp.logical_and(z == 1, inside(step))))
+    def arrive(step, slot, steps, out, right, left, r_s, r_r, l_s, l_r, credits):
+        def came(buffer, send, recv, i):
+            return pltpu.make_async_remote_copy(
+                buffer.at[i, slot], buffer.at[i, slot], send.at[i, slot], recv.at[i, slot],
+                device_id=pair, device_id_type=MESH,
+            )
+
+        started_inside = lax.rem(step, 3) == 1 if credits else step < 0
+
+        def side_of(there, from_end, buffer, send, recv, i, credit, source):
+            @pl.when(there)
+            def _():
+                quiet = jnp.logical_and(from_end, started_inside)
+
+                @pl.when(jnp.logical_not(quiet))
                 def _():
-                    move(right, r_s, r_r, z - 1, slot, up).wait_recv()
-                    out[...] += right[z - 1, slot]
+                    came(buffer, send, recv, i).wait_recv()
+                    out[...] += buffer[i, slot]
 
                 if credits:
-                    free(credit_right, z - 1, down, step + 2, z == 1)
-
-            @pl.when(z < last)
-            def _():
-                @pl.when(jnp.logical_not(jnp.logical_and(z == last - 1, inside(step))))
-                def _():
-                    move(left, l_s, l_r, z, slot, down).wait_recv()
-                    out[...] += left[z, slot]
-
-                if credits:
-                    free(credit_left, z, up, step + 2, z == last - 1)
-
-    def settle(slot, right, left, r_s, l_s):
+                    skip = jnp.logical_and(from_end, lax.rem(step + 3, 3) == 1)
+
+                    @pl.when(jnp.logical_and(step + 3 <= steps - 1, jnp.logical_not(skip)))
+                    def _():
+                        pl.semaphore_signal(
+                            credit.at[i], inc=1, device_id=source, device_id_type=MESH
+                        )
+
+        side_of(z > 0, z == 1, right, r_s, r_r, jnp.maximum(z - 1, 0), credit_right, down)
+        side_of(z < last, z == last - 1, left, l_s, l_r, jnp.minimum(z, last - 1), credit_left, up)
+
+    def settle(slot, right, left, r_s, l_s, main):
+        def wait(buffer, send, i, device):
+            pltpu.make_async_remote_copy(
+                buffer.at[i, slot], buffer.at[i, slot], send.at[i, slot], send.at[i, slot],
+                device_id=device, device_id_type=MESH,
+            ).wait_send()
+
         for target in range(4):
-
-            @pl.when(target > z)
-            def _():
-                i = target - 1
-                pltpu.make_async_remote_copy(
-                    right.at[i, slot], right.at[i, slot], r_s.at[i, slot], r_s.at[i, slot],
-                    device_id=up, device_id_type=MESH,
-                ).wait_send()
-
-            @pl.when(target < z)
-            def _():
-                pltpu.make_async_remote_copy(
-                    left.at[target, slot], left.at[target, slot], l_s.at[target, slot], l_s.at[target, slot],
-                    device_id=down, device_id_type=MESH,
-                ).wait_send()
+            rightmost, leftmost = target == 3, target == 0
+
+            @pl.when(jnp.logical_and(target > z, jnp.logical_or(z > 0, main and not rightmost)))
+            def _():
+                wait(right, r_s, target - 1, up)
+
+            @pl.when(jnp.logical_and(target < z, jnp.logical_or(z < last, main and not leftmost)))
+            def _():
+                wait(left, l_s, target, down)
 
     def order(turn):
         def near(end):
-            return jnp.where(
-                end == 0,
-                3 - turn,
-                jnp.where(turn == 0, 3, jnp.where(turn == 1, 0, 4 - turn)),
-            )
+            return jnp.where(end == 0, 3 - turn, jnp.where(turn < 2, 3 - turn, turn - 2))
 
         return jnp.where(z < 2, near(z), 3 - near(3 - z))
 
@@ -1259,9 +1322,32 @@
             dot(rank_own[:, half:], own[half:]) + dot(rank_far[:, half:], far[half:]),
         ]
 
+    def main_arrive(step):
+        slot = lax.rem(step, 3)
+        chunk = chunk_of(step)
+        arrive(
+            step, slot, steps, main_out.at[slot], main_right, main_left, mr_s, mr_r, ml_s, ml_r, True,
+        )
+        for part, (at, n) in enumerate(((0, WIDE), (WIDE, hidden - WIDE))):
+            for j in range(2):
+
+                @pl.when(chunk == 2 * j + part)
+                def _():
+                    e_w[:, j, at : at + n] = main_out[slot, :block, :n]
+                    for l in range(loops):
+                        start = block + l * rank_block
+                        e_o[l, j, :, at : at + n] = main_out[slot, start : start + rank_block, :n]
+
+            @pl.when(chunk == 4 + part)
+            def _():
+                s_w[:, at : at + n] = main_out[slot, :block, :n]
+                for l in range(loops):
+                    start = block + l * rank_block
+                    s_i[l, :, at : at + n] = main_out[slot, start : start + rank_block, :n]
+
     def turn_body(at, carry):
         step, turn = at // 4, lax.rem(at, 4)
-        slot = lax.rem(step, 2)
+        slot = lax.rem(step, 3)
         chunk = chunk_of(step)
         group = chunk // 2
         target = order(turn)
@@ -1287,6 +1373,10 @@
                 b_copy(3).start()
 
             @pl.when(step == 3)
+            def _():
+                w_copy.start()
+
+            @pl.when(step == 4)
             def _():
                 x_copy(2).start()
                 x_copy(3).start()
@@ -1294,14 +1384,10 @@
                 r_copy(4).start()
                 q_copy.start()
 
-            @pl.when(step == 4)
-            def _():
-                w_copy.start()
-
         def value():
             parts = left_times(
                 group // 2, group, target,
-                b_own[slot].astype(jnp.bfloat16), b_far[chunk].astype(jnp.bfloat16),
+                b_own[lax.rem(step, 2)].astype(jnp.bfloat16), b_far[chunk].astype(jnp.bfloat16),
             )
             product_ref[...] = jnp.concatenate(parts, axis=0)
             beyond = jnp.logical_or(
@@ -1325,12 +1411,31 @@
             return product_ref[...]
 
         chain(
-            target, step, slot, steps, value, main_out.at[chunk], main_right, main_left,
+            target, step, slot, steps, value, main_out.at[slot], main_right, main_left,
             mr_s, mr_r, ml_s, ml_r, True,
         )
+
+        @pl.when(jnp.logical_and(turn == 3, step >= 2))
+        def _():
+            main_arrive(step - 2)
+
         return carry
 
     lax.fori_loop(0, 4 * steps, turn_body, 0)
+
+    w_copy.wait_recv()
+    own_copy.wait()
+
+    def raw_body(turn, carry):
+        target = order(turn)
+        chain(
+            target, 0, 0, 1, lambda: raw_own[target] + raw_far[target], raw_out, raw_right, raw_left,
+            rr_s, rr_r, rl_s, rl_r, False,
+        )
+        return carry
+
+    lax.fori_loop(0, 4, raw_body, 0)
+    main_arrive(jnp.int32(steps - 2))
 
     for i in (2, 3):
         x_copy(i).wait_recv()
@@ -1357,23 +1462,55 @@
         return carry
 
     lax.fori_loop(0, 4, side_body, 0)
-
-    w_copy.wait_recv()
-    own_copy.wait()
-
-    def raw_body(turn, carry):
-        target = order(turn)
-        chain(
-            target, 0, 0, 1, lambda: raw_own[target] + raw_far[target], raw_out, raw_right, raw_left,
-            rr_s, rr_r, rl_s, rl_r, False,
-        )
-        return carry
-
-    lax.fori_loop(0, 4, raw_body, 0)
-
-    settle((steps - 1) % 2, main_right, main_left, mr_s, ml_s)
-    settle(0, side_right, side_left, sr_s, sl_s)
-    settle(0, raw_right, raw_left, rr_s, rl_s)
+    main_arrive(jnp.int32(steps - 1))
+    arrive(0, 0, 1, raw_out, raw_right, raw_left, rr_s, rr_r, rl_s, rl_r, False)
+
+    def share(device, owner, i):
+        return pltpu.make_async_remote_copy(
+            around.at[owner], around.at[owner], around_s.at[i], around_r.at[i],
+            device_id=device, device_id_type=MESH,
+        )
+
+    far_owner = lax.rem(mp + 2, 4)
+    for l in range(loops):
+        start = 2 * tall + l * layout.loop + 5 * tall
+        around[mp, l] = raw_out[start : start + 2 * tall]
+    along, same, passed = share(other, mp, 0), share(core, mp, 1), share(core, far_owner, 2)
+    along.start()
+    same.start()
+    arrive(0, 0, 1, side_out, side_right, side_left, sr_s, sr_r, sl_s, sl_r, False)
+    along.wait_recv()
+    passed.start()
+    q_w[...] = side_out[:block, :head]
+    o_w[...] = side_out[:block, head:]
+    for l in range(loops):
+        start = block + l * rank_block
+        q_o[l] = side_out[start : start + rank_block, :head]
+        o_i[l] = side_out[start : start + rank_block, head:]
+    gains_out[...] = raw_out[layout.gains : layout.gains + 2, :block]
+    for j in range(2):
+        pair_w[:, j * head : (j + 1) * head] = raw_out[j * tall : j * tall + quarter]
+    for l in range(loops):
+        base = 2 * tall + l * layout.loop
+        q_i[:, l] = raw_out[base : base + quarter]
+        for j in range(2):
+            start = base + (1 + j) * tall
+            p_i[l, :, j] = raw_out[start : start + quarter]
+            e_i[l, :, j] = raw_out[start + 2 * tall : start + 2 * tall + quarter]
+            start = base + 7 * tall + j * (rank_block // 4)
+            p_o[l, j] = raw_out[start : start + rank_block // 4]
+    same.wait_recv()
+    passed.wait_recv()
+    for l in range(loops):
+        for m in range(4):
+            o_o[l, m * quarter : (m + 1) * quarter] = around[m, l, :quarter]
+            s_o[l, m * quarter : (m + 1) * quarter] = around[m, l, tall : tall + quarter]
+    for copy in (along, same, passed):
+        copy.wait_send()
+
+    settle((steps - 1) % 3, main_right, main_left, mr_s, ml_s, True)
+    settle(0, side_right, side_left, sr_s, sl_s, False)
+    settle(0, raw_right, raw_left, rr_s, rl_s, False)
     for copy in (x_copy(2), x_copy(3), r_copy(3), r_copy(4), b_copy(1), b_copy(2), b_copy(3)):
         copy.wait_send()
     q_copy.wait_send()
@@ -1395,81 +1532,41 @@
     half_x = pltpu.VMEM((x_all.shape[0], *x_all.shape[2:]), f32)
     half_r = pltpu.VMEM((r_all.shape[0], *r_all.shape[2:]), f32)
     whole_b, whole_q = pltpu.VMEM(b_all.shape, f32), pltpu.VMEM(q_all.shape, f32)
-    main, side, rest = pl.pallas_call(
+    shapes = (
+        (2, block), (block, head), (quarter, 2 * head), (block, head), (block, 2, hidden),
+        (block, hidden), (quarter, loops, head), (loops, rank_block, head), (loops, quarter, 2, head),
+        (loops, 2, rank_quarter, head), (loops, rank_block, head), (loops, block, head),
+        (loops, quarter, 2, head), (loops, 2, rank_block, hidden), (loops, rank_block, hidden),
+        (loops, block, head),
+    )
+    gains, q_w, pair_w, o_w, e_w, s_w, q_i, q_o, p_i, p_o, o_i, o_o, e_i, e_o, s_i, s_o = pl.pallas_call(
         line_kernel,
-        out_shape=(
-            jax.ShapeDtypeStruct((steps, rows, WIDE), f32),
-            jax.ShapeDtypeStruct((rows, 2 * head), f32),
-            jax.ShapeDtypeStruct((layout.all, head), f32),
-        ),
+        out_shape=tuple(jax.ShapeDtypeStruct(v, f32) for v in shapes),
         in_specs=[hbm] * 11,
-        out_specs=(vmem, vmem, vmem),
-        scratch_shapes=[half_x, half_r, pltpu.VMEM((2, *b_all.shape[1:]), f32), whole_q]
+        out_specs=(vmem,) * len(shapes),
+        scratch_shapes=[
+            pltpu.VMEM((3, rows, WIDE), f32), pltpu.VMEM((rows, 2 * head), f32),
+            pltpu.VMEM((layout.all, head), f32), pltpu.VMEM((4, loops, 2 * layout.tall, head), f32),
+        ]
+        + [half_x, half_r, pltpu.VMEM((2, *b_all.shape[1:]), f32), whole_q]
         + [half_x, half_r, whole_b, whole_q]
         + [pltpu.VMEM(v.shape, f32) for v in (x_end, r_end, b_end)]
         + [pltpu.VMEM(raw.shape[1:], f32)] * 2
         + [pltpu.VMEM((rows, WIDE), f32)]
-        + [pltpu.VMEM((line, 2, rows, WIDE), f32)] * 2
+        + [pltpu.VMEM((line, 3, rows, WIDE), f32)] * 2
         + [pltpu.VMEM((line, 1, rows, 2 * head), f32)] * 2
         + [pltpu.VMEM((line, 1, layout.all, head), f32)] * 2
-        + [dma((2,))] * 4 + [dma((steps,))] * 2 + [dma] * 4 + [dma((11,)), dma((2,))]
-        + [dma((line, 2))] * 4 + [dma((line, 1))] * 8
+        + [dma((2,))] * 4 + [dma((steps,))] * 2 + [dma] * 4 + [dma((11,)), dma((2,)), dma((3,)), dma((3,))]
+        + [dma((line, 3))] * 4 + [dma((line, 1))] * 8
         + [pltpu.SemaphoreType.REGULAR((line,))] * 2,
         compiler_params=pltpu.CompilerParams(
-            collective_id=20, has_side_effects=True, vmem_limit_bytes=60 << 20
+            collective_id=20, has_side_effects=True, vmem_limit_bytes=63 << 20
         ),
     )(*factors)
 
-    wide = [
-        jnp.concatenate([main[2 * i], main[2 * i + 1][:, : hidden - WIDE]], axis=1) for i in range(3)
-    ]
-    narrow = [side[:, :head], side[:, head:]]
-
-    def shared_rows(value):
-        return value[:block]
-
-    def loop_rows(value, i):
-        return value[block + i * rank_block : block + (i + 1) * rank_block]
-
-    tall = layout.tall
-
-    def raw_rows(start, size):
-        return rest[start : start + size]
-
-    pair_weight = jnp.concatenate([raw_rows(0, quarter), raw_rows(tall, quarter)], axis=1)
-    query_inner, pair_inner, expand_inner, pair_outer, outers = [], [], [], [], []
-    for i in range(loops):
-        base = 2 * tall + i * layout.loop
-        own = [raw_rows(base + j * tall, quarter) for j in range(7)]
-        query_inner.append(own[0])
-        pair_inner.append(jnp.stack(own[1:3], axis=1))
-        expand_inner.append(jnp.stack(own[3:5], axis=1))
-        outers += own[5:7]
-        pair_outer.append(
-            jnp.stack([raw_rows(base + 7 * tall + j * rank_quarter, rank_quarter) for j in range(2)])
-        )
-    outers = lax.all_gather(jnp.stack(outers), "mp")
-    outers = jnp.swapaxes(outers, 0, 1).reshape(2 * loops, block, -1).swapaxes(1, 2)
-    gains = rest[layout.gains : layout.gains + 2, :block]
-    stack = jnp.stack
     return (
-        gains[0],
-        gains[1],
-        shared_rows(narrow[0]),
-        pair_weight,
-        shared_rows(narrow[1]).T,
-        stack([shared_rows(wide[0]), shared_rows(wide[1])], axis=1),
-        shared_rows(wide[2]).T,
-        stack(query_inner),
-        stack([loop_rows(narrow[0], i) for i in range(loops)]),
-        stack(pair_inner),
-        stack(pair_outer),
-        stack([loop_rows(narrow[1], i).T for i in range(loops)]),
-        outers[0::2],
-        stack(expand_inner),
-        stack([stack([loop_rows(wide[j], i) for j in range(2)]) for i in range(loops)]),
-        stack([loop_rows(wide[2], i).T for i in range(loops)]),
-        outers[1::2],
+        gains[0], gains[1], q_w, pair_w, o_w.T, e_w, s_w.T, q_i.swapaxes(0, 1), q_o, p_i, p_o,
+        o_i.swapaxes(1, 2), o_o.swapaxes(1, 2), e_i, e_o, s_i.swapaxes(1, 2), s_o.swapaxes(1, 2),
     )
 
 

time: 570 us -> 448 us (0.79)
  Pallas kernels: 483 us -> 429 us
  local copies, waits for them, and re-layouts: 65.4 us -> 18.6 us
  other arithmetic: 9.86 us -> 0 us
  blocking collectives: 6.86 us -> 0 us
    pallas_call x2, Pallas kernels: 483 us -> 429 us  [the longest x1 279 us: line_gradients(): pl.pallas_call(line_kernel, out_shape=tuple((jax.ShapeDtypeStruct(v, f32)...]
    slice x3 -> x0, local copies, waits for them, and re-layouts: 16.8 us -> none  [the longest x1 6.04 us: line_gradients(): outers[0::2]]
    reshape x2 -> x0, local copies, waits for them, and re-layouts: 13 us -> none  [the longest x1 6.56 us: block_and_factors(): w_in.reshape(loops, width, 2 * rank)]
    unnamed x27 -> x47, local copies, waits for them, and re-layouts: 26.9 us -> 14.7 us
    all_gather x1 -> x0, blocking collectives: 6.86 us -> none  [line_gradients(): outers = lax.all_gather(jnp.stack(outers), 'mp')]
where the time goes in v3:
time: 448 us
  Pallas kernels  429 us (96%)
  local copies, waits for them, and re-layouts  18.6 us (4%)
    pallas_call x1, Pallas kernels, line_gradients(): pl.pallas_call(line_kernel, out_shape=tuple((jax.ShapeDtypeStruct(v, f32)...  279 us
    pallas_call x1, Pallas kernels, block_and_factors(): pl.pallas_call(block_kernel, out_shape=out_shape, in_specs=[vmem] * 5 + [...  150 us
    unnamed x47, local copies, waits for them, and re-layouts  14.7 us

profile of v3, /device:TPU:0, one launch (start us, length us, event | category | flops | bytes accessed | tf_op | source)
XLA Modules:
  0.0 448.1 jit_solution(5550248863415721163)
XLA Ops:
  0.7 1.3 broadcast_in_dim.6.refs_3_
  1.9 1.3 broadcast_in_dim.7.refs_4_
  3.2 149.8 %shard_map.339 = (bf16[128,1152]{1,0:T(8,128)(2,1)}, f32[128,1152]{1,0:T(8,128)}, f32[2,4,680,256]{3,2,1,0:T(8,128)}, f32[4,2,4,144,256]{4,3,2,1,0:T(8,128)}, f3...) custom-call(bf16[128,1152]{1,0:T(8,128)(2,1)} %refs_0_.1, ...), custom_call_target="tpu_custom_call" | custom-call | tf_op jit(solution)/shard_map/pallas_call | solution.py:1054
  153.0 0.0 copy-start.7
  153.0 0.0 copy-start.3
  153.0 279.0 %shard_map.340 = (f32[2,144]{1,0:T(2,128)}, f32[144,256]{1,0:T(8,128)}, f32[36,512]{1,0:T(8,128)}, f32[144,256]{1,0:T(8,128)}, f32[144,2,1728]{2,1,0:T(2,128)}, ...) custom-call(f32[2,4,680,256]{3,2,1,0:T(8,128)} %get-tuple-element.50, ...), custom_call_target="tpu_custom_call" | custom-call | tf_op jit(solution)/shard_map/pallas_call | solution.py:1542
  432.0 0.0 copy-start.10
  432.0 0.0 copy-start
  432.0 1.4 fusion
  433.4 0.0 copy-done.7
  433.4 0.7 copy.56
  434.1 0.0 copy-done.3
  434.1 0.8 copy.57
  434.9 1.6 copy.58
  436.5 1.6 copy.59
  438.1 0.0 copy-done.10
  438.1 0.7 copy.60
  438.8 0.0 copy-done
  438.8 1.3 copy.61
  440.2 1.0 copy.62
  441.1 0.0 copy-done.11
  441.1 0.6 copy.63
  441.8 0.6 copy.64
  442.4 0.7 copy.65
  443.1 0.6 copy.66
  443.7 0.6 copy.67
  444.3 0.0 copy-done.6
  444.3 0.7 copy.68
  445.0 0.7 copy.69
  445.7 0.9 copy.70
  446.6 0.8 copy.71
  447.4 0.7 copy.72
  (20 shorter events, 0.0 us)
Async XLA Ops:
  153.0 280.4 %copy-start.7 = (bf16[128,1152]{1,0:T(8,128)(2,1)S(1)}, bf16[128,1152]{1,0:T(8,128)(2,1)}, u32[]{:S(2)}) copy-start(bf16[128,1152]{1,0:T(8,128)(2,1)} %get-tuple-element.98) | copy-start | bytes 884740
  153.0 281.1 %copy-start.3 = (f32[128,1152]{1,0:T(8,128)S(1)}, f32[128,1152]{1,0:T(8,128)}, u32[]{:S(2)}) copy-start(f32[128,1152]{1,0:T(8,128)} %get-tuple-element.99) | copy-start | bytes 1769476
  432.0 6.1 %copy-start.10 = (f32[144,256]{1,0:T(8,128)S(1)}, f32[144,256]{1,0:T(8,128)}, u32[]{:S(2)}) copy-start(f32[144,256]{1,0:T(8,128)} %get-tuple-element.64) | copy-start | bytes 442372
  432.0 6.8 %copy-start = (f32[144,2,1728]{2,1,0:T(2,128)S(1)}, f32[144,2,1728]{2,1,0:T(2,128)}, u32[]{:S(2)}) copy-start(f32[144,2,1728]{2,1,0:T(2,128)} %get-tuple-element.105) | copy-start | bytes 5971972
  436.5 3.6 copy-start.1
  438.8 2.3 copy-start.11
  438.8 3.0 copy-start.13
  438.8 3.6 copy-start.9
  438.8 4.2 copy-start.14
  440.1 3.5 copy-start.12
  440.1 4.2 copy-start.6
  440.1 4.9 %copy-start.8 = (f32[2,36,2,256]{3,2,1,0:T(2,128)S(1)}, f32[2,36,2,256]{3,2,1,0:T(2,128)}, u32[]{:S(2)}) copy-start(f32[2,36,2,256]{3,2,1,0:T(2,128)} %get-tuple-element.113) | copy-start | bytes 442372
  440.1 5.6 %copy-start.2 = (f32[2,2,32,1728]{3,2,1,0:T(8,128)S(1)}, f32[2,2,32,1728]{3,2,1,0:T(8,128)}, u32[]{:S(2)}) copy-start(f32[2,2,32,1728]{3,2,1,0:T(8,128)} %get-tuple-element.114) | copy-start | bytes 2654212
  440.1 6.5 %copy-start.4 = (f32[2,32,1728]{2,1,0:T(8,128)S(1)}, f32[2,32,1728]{2,1,0:T(8,128)}, u32[]{:S(2)}) copy-start(f32[2,32,1728]{2,1,0:T(8,128)} %get-tuple-element.75) | copy-start | bytes 1327108
  441.1 6.3 %copy-start.5 = (f32[2,144,256]{2,1,0:T(8,128)S(1)}, f32[2,144,256]{2,1,0:T(8,128)}, u32[]{:S(2)}) copy-start(f32[2,144,256]{2,1,0:T(8,128)} %get-tuple-element.76) | copy-start | bytes 884740

commit v4 on v3

--- a/solution.py
+++ b/solution.py
@@ -367,7 +367,7 @@
 
 WEIGHTS = (
     "q_in", "query", "q_out", "kv_in", "pair", "kv_out", "output", "o_in", "o_out",
-    "w_in", "wide", "w_out", "down", "d_in", "d_out",
+    "wide", "w_out", "down", "d_in", "d_out", "w_in",
 )
 SUM_STEP = 384
 
@@ -379,13 +379,15 @@
     (
         out_ref, grad_ref, raw_ref, x_all, r_all, b_all, q_all, x_got, r_got, b_got, x_end, r_end, b_end,
     ), refs = refs[:13], refs[13:]
-    weights, refs = refs[:count], refs[count:]
+    weights, refs = (*refs[: count - 1], refs[WEIGHTS.index("kv_in")]), refs[count - 1 :]
     (
         h_s, mid_s, normed_s, qr_s, kvr_s, q_s, k_s, v_s, probs_s, mixed_s, or_s, fed_s, er_s,
         gate_s, up_s, act_s, sr_s, gg_s, gu_s, g_s, gain_s, select,
-        part, total, near, mine, far, xs, rs, bs, qs, kv_flat, w_flat, cosine_ref, sine_ref, mask_ref,
+        part, total, near, mine, far, side_part, side_near, side_mine, side_far, side_total,
+        late_s, er_grad_s, chosen_s, xs, rs, bs, qs, kv_flat, w_flat, cosine_ref, sine_ref, mask_ref,
         load_sems, c_s, c_r, y_s, y_r, e_s, e_r,
         xl, rl, bl, ql, x_s, x_r, r_s, r_r, b_s, b_r, xe_s, xe_r, re_s, re_r, be_s, be_r,
+        sc_s, sc_r, sy_s, sy_r, se_s, se_r, xc_s, xc_r, rc_s, rc_r,
     ) = refs
     W = SimpleNamespace(**dict(zip(WEIGHTS, weights)))
     dp, mp = lax.axis_index("dp"), lax.axis_index("mp")
@@ -397,7 +399,7 @@
         for i, (source, target) in enumerate(zip(sources, weights))
     ]
     load = SimpleNamespace(**dict(zip(WEIGHTS, loads)))
-    for copy in loads:
+    for copy in loads[:-1]:
         copy.start()
     x = lax.rem(dp, 2)
     z = dp // 2
@@ -474,25 +476,25 @@
     def q_copies(i, l):
         return pltpu.make_async_copy(qs.at[i], q_all.at[i, span(l)], ql.at[i, l]), None, None
 
-    def launch(copies):
+    def launch(copies, whole=True):
         local, across, onward = copies
         local.start()
         if across is not None:
             across.start()
         if onward is not None:
 
-            @pl.when(is_end)
+            @pl.when(is_end if whole else jnp.logical_and(is_end, side == 0))
             def _():
                 onward.start()
 
-    def finish(copies):
+    def finish(copies, whole=True):
         local, across, onward = copies
         local.wait()
         if across is not None:
             across.wait_send()
         if onward is not None:
 
-            @pl.when(is_end)
+            @pl.when(is_end if whole else jnp.logical_and(is_end, side == 0))
             def _():
                 onward.wait_send()
 
@@ -530,7 +532,7 @@
         x_copies(1, l)[1].wait_recv()
         r_copies(2, l)[1].wait_recv()
 
-        @pl.when(is_end)
+        @pl.when(jnp.logical_and(is_end, side == 1))
         def _():
             for copy in far_feed(l):
                 copy.start()
@@ -538,23 +540,23 @@
     def ship_x(i, l, value, again, before):
         @pl.when(again)
         def _():
-            finish(x_copies(i, before))
+            finish(x_copies(i, before), False)
 
         turned = value.astype(jnp.float32).T
         for b in range(blocks):
             xs[i, b % 2, b // 2] = turned[b * block : (b + 1) * block]
-        launch(x_copies(i, l))
+        launch(x_copies(i, l), False)
 
     def ship_r(i, l, value, again, before):
         @pl.when(again)
         def _():
-            finish(r_copies(i, before))
+            finish(r_copies(i, before), False)
 
         turned = value.astype(jnp.float32).T
         size = rank // blocks
         for b in range(blocks):
             rs[i, b % 2, b // 2] = turned[b * size : (b + 1) * size]
-        launch(r_copies(i, l))
+        launch(r_copies(i, l), False)
 
     def ship_b(i, l, value, again, before):
         @pl.when(again)
@@ -578,9 +580,38 @@
     def columns_of(size):
         return [(at, min(SUM_STEP, size - at)) for at in range(0, size, SUM_STEP)]
 
-    def sum_over_mp(size, fill, turn, idle):
+    def side_copies(turn, size):
+        columns = pl.ds(0, size)
+        return (
+            remote(
+                side_part.at[turn, theirs, columns], side_near.at[turn, :, columns],
+                sc_s.at[turn], sc_r.at[turn], core,
+            ),
+            remote(
+                side_mine.at[turn, :, columns], side_far.at[turn, :, columns],
+                sy_s.at[turn], sy_r.at[turn], other,
+            ),
+            remote(
+                side_total.at[turn, own, columns], side_total.at[turn, own, columns],
+                se_s.at[turn], se_r.at[turn], core,
+            ),
+        )
+
+    def finish_side(turn, size):
+        first, second, third = side_copies(turn, size)
+        second.wait_recv()
+        side_total[turn, own, :size] = side_mine[turn, :, :size] + side_far[turn, :, :size]
+        third.start()
+        third.wait_recv()
+        for copy in (first, second, third):
+            copy.wait_send()
+        return side_total[turn, :, :size]
+
+    def sum_over_mp(fill, turn, side_size, finish_previous, idle):
+        pieces = columns_of(width)
+
         def pieces_of(make):
-            return [make(i, pl.ds(at, n)) for i, (at, n) in enumerate(columns_of(size))]
+            return [make(i, pl.ds(at, n)) for i, (at, n) in enumerate(pieces)]
 
         first = pieces_of(
             lambda i, c: remote(part.at[theirs, c], near.at[:, c], c_s.at[i], c_r.at[i], core)
@@ -593,21 +624,29 @@
         third = pieces_of(
             lambda i, c: remote(total.at[own, c], total.at[own, c], e_s.at[i], e_r.at[i], core)
         )
+        side_first, side_second, _ = side_copies(turn, side_size)
 
         def middle(i):
-            at, n = columns_of(size)[i]
+            at, n = pieces[i]
             first[i].wait_recv()
             mine[:, at : at + n] = part[own, at : at + n] + near[:, at : at + n]
             second[i].start()
 
-        for i, (at, n) in enumerate(columns_of(size)):
+        for i, (at, n) in enumerate(pieces):
             fill(at, n)
             first[i].start()
             if i:
                 middle(i - 1)
+        side_first.start()
         middle(len(first) - 1)
+        side_first.wait_recv()
+        side_mine[turn, :, :side_size] = (
+            side_part[turn, own, :side_size] + side_near[turn, :, :side_size]
+        )
+        finish_previous()
+        side_second.start()
         idle()
-        for i, (at, n) in enumerate(columns_of(size)):
+        for i, (at, n) in enumerate(pieces):
             second[i].wait_recv()
             total[own, at : at + n] = mine[:, at : at + n] + far[turn, :, at : at + n]
             third[i].start()
@@ -689,13 +728,15 @@
         mixed_s[l] = mixed
         need(load.output, load.o_in, load.o_out)
 
+        output_rank = dot(mixed, W.o_in[l])
+        side_part[0, :, :rank] = output_rank
+        output_parts = split3(output_rank)
+
         def fill_attend(at, n):
-            cut = min(n, max(0, width - at))
-            if cut:
-                part[:, at : at + cut] = dot(mixed, W.output[:, at : at + cut])
-            if cut < n:
-                start = at + cut - width
-                part[:, at + cut : at + n] = dot(mixed, W.o_in[l, :, start : start + n - cut])
+            value = dot(mixed, W.output[:, at : at + n])
+            for piece in output_parts:
+                value = value + dot(piece, W.o_out[l, :, at : at + n])
+            part[:, at : at + n] = value
 
         again = l > 0
 
@@ -706,18 +747,24 @@
 
             @pl.when(l == 0)
             def _():
+                for i in range(1, loops):
+                    kv_flat[i] = W.kv_in[i].reshape(width, 2 * rank)
+                load.w_in.start()
                 load.w_in.wait()
                 for i in range(loops):
                     w_flat[i] = W.w_in[i].reshape(width, 2 * rank)
-                for i in range(1, loops):
-                    kv_flat[i] = W.kv_in[i].reshape(width, 2 * rank)
-
-        sum_over_mp(width + rank, fill_attend, 0, idle_attend)
-        output_rank = total[:, width : width + rank]
-        or_s[l] = output_rank
-        middle = h_s[l] + total[:, :width]
-        for piece in split3(output_rank):
-            middle = middle + dot(piece, W.o_out[l])
+
+            @pl.when(again)
+            def _():
+                pass_act(0)
+
+        def finish_before_attend():
+            @pl.when(again)
+            def _():
+                sr_s[jnp.maximum(l - 1, 0)] = finish_side(1, rank)
+
+        sum_over_mp(fill_attend, 0, rank, finish_before_attend, idle_attend)
+        middle = h_s[l] + total[...]
         mid_s[l] = middle
         fed = low(middle * factor_of(middle) * feed)
         fed_s[l] = fed
@@ -737,30 +784,26 @@
             ship_b(4 + at // WIDE, l, act_s[:, at : at + n], again, 0)
         need(load.down, load.d_in, load.d_out)
 
+        shrink_rank = dot(act_s[...], W.d_in[l])
+        side_part[1, :, :rank] = shrink_rank
+        shrink_parts = split3(shrink_rank)
+
         def fill_feed(at, n):
-            cut = min(n, max(0, width - at))
-            if cut:
-                part[:, at : at + cut] = dot(act_s[...], W.down[:, at : at + cut])
-            if cut < n:
-                start = at + cut - width
-                part[:, at + cut : at + n] = dot(act_s[...], W.d_in[l, :, start : start + n - cut])
+            value = dot(act_s[...], W.down[:, at : at + n])
+            for piece in shrink_parts:
+                value = value + dot(piece, W.d_out[l, :, at : at + n])
+            part[:, at : at + n] = value
 
         def idle_feed():
             ship_x(0, l, fed, again, 0)
             ship_r(0, l, widen_rank[:, :rank], again, 0)
             ship_r(1, l, widen_rank[:, rank:], again, 0)
 
-            @pl.when(again)
-            def _():
-                pass_act(0)
-
-        sum_over_mp(width + rank, fill_feed, 1, idle_feed)
-        shrink_rank = total[:, width : width + rank]
-        sr_s[l] = shrink_rank
-        result = mid_s[l] + total[:, :width]
-        for piece in split3(shrink_rank):
-            result = result + dot(piece, W.d_out[l])
-        h_s[l + 1] = result
+        def finish_before_feed():
+            or_s[l] = finish_side(0, rank)
+
+        sum_over_mp(fill_feed, 1, rank, finish_before_feed, idle_feed)
+        h_s[l + 1] = mid_s[l] + total[...]
         return carry
 
     lax.fori_loop(0, loops, forward, 0)
@@ -789,6 +832,53 @@
     )
     raw_rows = raw_layout(quarter, rank_quarter, loops)
 
+    tall = raw_rows.tall
+
+    def put(start, size, stride, value, add=False):
+        for b in range(blocks):
+            piece = value[b * stride : b * stride + size]
+            if add:
+                raw_ref[b % 2, b // 2, start : start + size] += piece
+            else:
+                raw_ref[b % 2, b // 2, start : start + size] = piece
+
+    def pair_ranks(l, grad_keys, grad_values):
+        return low(
+            jnp.concatenate(
+                [product_t(grad_keys, W.kv_out[l, 0]), product_t(grad_values, W.kv_out[l, 1])], axis=1
+            )
+        )
+
+    def raw_of(l):
+        grad_rank = late_s[l, :, :rank]
+        grad_pair = late_s[l, :, rank:]
+        grad_pair_rank = pair_ranks(l, grad_pair[:, :head], grad_pair[:, head:])
+        grad_widen = er_grad_s[l]
+        normed_own = low(product_t(select[...], normed_s[l]))
+        pair_weight = dot(normed_own, grad_pair)
+        for j in range(2):
+            value = pair_weight[:, j * head : (j + 1) * head]
+            put(j * tall, tall, padded_quarter, value, l < loops - 1)
+        base = 2 * tall + l * raw_rows.loop
+
+        def put_loop(i, value):
+            put(base + i * tall, tall, padded_quarter, value)
+
+        put_loop(0, dot(normed_own, grad_rank))
+        for j in range(2):
+            put_loop(1 + j, dot(normed_own, grad_pair_rank[:, j * rank : (j + 1) * rank]))
+        fed_own = low(product_t(select[...], fed_s[l]))
+        for j in range(2):
+            put_loop(3 + j, dot(fed_own, grad_widen[:, j * rank : (j + 1) * rank]))
+        put_loop(5, sum(dot(chosen_s[l, 1], piece) for piece in split3(or_s[l])))
+        put_loop(6, sum(dot(chosen_s[l, 0], piece) for piece in split3(sr_s[l])))
+        for j in range(2):
+            rank_own = low(product_t(rank_select, kvr_s[l, :, j * rank : (j + 1) * rank]))
+            put(
+                base + 7 * tall + j * rank_quarter, rank_quarter, rank_quarter,
+                dot(rank_own, grad_pair[:, j * head : (j + 1) * head]),
+            )
+
     def back(step, carry):
         l = loops - 1 - step
         again = step > 0
@@ -809,33 +899,37 @@
             ship_b(i, l, grad_gate, again, before)
             ship_b(2 + i, l, grad_up, again, before)
 
+        for j, value in enumerate((gg_s, gu_s)):
+            side_part[0, :, j * rank : (j + 1) * rank] = dot(value[...], W.w_out[l, j])
+        grad_widen = low(side_part[0, :, : 2 * rank])
+
         def fill_fed(at, n):
-            cut = min(n, max(0, width - at))
-            if cut:
-                part[:, at : at + cut] = dot(gg_s[...], W.wide[0, :, at : at + cut]) + dot(
-                    gu_s[...], W.wide[1, :, at : at + cut]
-                )
-            while cut < n:
-                start = at + cut - width
-                j, offset = divmod(start, rank)
-                size = min(n - cut, rank - offset)
-                value = (gg_s, gu_s)[j][...]
-                part[:, at + cut : at + cut + size] = dot(
-                    value, W.w_out[l, j, :, offset : offset + size]
-                )
-                cut += size
+            part[:, at : at + n] = (
+                dot(gg_s[...], W.wide[0, :, at : at + n])
+                + dot(gu_s[...], W.wide[1, :, at : at + n])
+                + product_t(grad_widen, w_flat[l, at : at + n])
+            )
+
+        def finish_before_fed():
+            @pl.when(step == 0)
+            def _():
+                sr_s[loops - 1] = finish_side(1, rank)
+
+            @pl.when(again)
+            def _():
+                late_s[loops - 1] = low(finish_side(1, rank + 2 * head))
 
         def idle_fed():
             ship_x(1, l, grad_feed, again, before)
             ship_r(2, l, grad_shrink, again, before)
-
-            @pl.when(step == 0)
-            def _():
-                pass_act(loops - 1)
-
-        sum_over_mp(width + 2 * rank, fill_fed, 0, idle_fed)
-        grad_widen = low(total[:, width : width + 2 * rank])
-        grad_fed = total[:, :width] + product_t(grad_widen, w_flat[l])
+            chosen_s[l, 0] = low(product_t(select[...], grad_feed))
+
+            @pl.when(again)
+            def _():
+                raw_of(loops - 1)
+
+        sum_over_mp(fill_fed, 0, 2 * rank, finish_before_fed, idle_fed)
+        grad_fed = total[...]
         middle = mid_s[l]
         factor = factor_of(middle)
         unit = middle * factor
@@ -856,46 +950,41 @@
         grad_scores = low(probs * (grad_probs - delta))
         grad_query = low(spin(dot(grad_scores, k_s[l]) * scale, -1.0))
 
+        grad_rank = product_t(grad_query, W.q_out[l])
+        grad_keys = spin(product_tn(grad_scores, q_s[l]) * scale, -1.0)
+        grad_values = product_tn(low(probs), grad_mixed)
+        side_part[1, :, :rank] = grad_rank
+        side_part[1, :, rank : rank + head] = grad_keys
+        side_part[1, :, rank + head :] = grad_values
+        grad_rank, grad_keys, grad_values = low(grad_rank), low(grad_keys), low(grad_values)
+        grad_pair = jnp.concatenate([grad_keys, grad_values], axis=1)
+        grad_pair_rank = pair_ranks(l, grad_keys, grad_values)
+
         def fill_normed(at, n):
-            if at == columns_of(width + rank + 2 * head)[0][0]:
-                part[:, width + rank : width + rank + head] = spin(
-                    product_tn(grad_scores, q_s[l]) * scale, -1.0
-                )
-                part[:, width + rank + head :] = product_tn(low(probs), grad_mixed)
-            cut = min(n, max(0, width - at))
-            if cut:
-                part[:, at : at + cut] = product_t(grad_query, W.query[at : at + cut])
-            end = min(at + n, width + rank)
-            if at + cut < end:
-                start = at + cut - width
-                part[:, at + cut : end] = product_t(
-                    grad_query, W.q_out[l, start : end - width]
-                )
+            part[:, at : at + n] = (
+                product_t(grad_query, W.query[at : at + n])
+                + product_t(grad_rank, W.q_in[l, at : at + n])
+                + product_t(grad_pair, W.pair[at : at + n])
+                + product_t(grad_pair_rank, kv_flat[l, at : at + n])
+            )
+
+        def finish_before_normed():
+            er_grad_s[l] = low(finish_side(0, 2 * rank))
 
         def idle_normed():
             ship_q(0, l, grad_query, again, before)
             ship_x(3, l, grad_attend, again, before)
             ship_r(4, l, grad_output, again, before)
+            chosen_s[l, 1] = low(product_t(select[...], grad_attend))
+
+            @pl.when(step == 0)
+            def _():
+                pass_act(loops - 1)
+
             pass_feed(l)
 
-        sum_over_mp(width + rank + 2 * head, fill_normed, 1, idle_normed)
-        grad_rank = low(total[:, width : width + rank])
-        grad_pair = low(total[:, width + rank : width + rank + 2 * head])
-        grad_pair_rank = low(
-            jnp.concatenate(
-                [
-                    product_t(grad_pair[:, :head], W.kv_out[l, 0]),
-                    product_t(grad_pair[:, head:], W.kv_out[l, 1]),
-                ],
-                axis=1,
-            )
-        )
-        grad_normed = (
-            total[:, :width]
-            + product_t(grad_rank, W.q_in[l])
-            + product_t(grad_pair, W.pair[...])
-            + product_t(grad_pair_rank, kv_flat[l])
-        )
+        sum_over_mp(fill_normed, 1, rank + 2 * head, finish_before_normed, idle_normed)
+        grad_normed = total[...]
         h = h_s[l]
         factor = factor_of(h)
         unit = h * factor
@@ -903,76 +992,11 @@
         g_s[...] += factor * (scaled - unit * jnp.mean(scaled * unit, axis=-1, keepdims=True))
         gain_s[0:1] += jnp.sum(grad_normed * unit, axis=0, keepdims=True)
 
-        def put(start, size, stride, value, add=False):
-            for b in range(blocks):
-                piece = value[b * stride : b * stride + size]
-                at = pl.ds(start, size)
-                if add:
-                    raw_ref[b % 2, b // 2, at] += piece
-                else:
-                    raw_ref[b % 2, b // 2, at] = piece
-
-        tall = raw_rows.tall
-        normed_own = low(product_t(select[...], normed_s[l]))
-        pair_weight = dot(normed_own, grad_pair)
-
-        @pl.when(step == 0)
-        def _():
-            for j in range(2):
-                put(j * tall, tall, padded_quarter, pair_weight[:, j * head : (j + 1) * head])
-
-        @pl.when(step > 0)
-        def _():
-            for j in range(2):
-                put(j * tall, tall, padded_quarter, pair_weight[:, j * head : (j + 1) * head], True)
-
-        base = 2 * tall + l * raw_rows.loop
-
-        def put_loop(i, value):
-            put(pl.multiple_of(base + i * tall, 8), tall, padded_quarter, value)
-
-        put_loop(0, dot(normed_own, grad_rank))
-        for j in range(2):
-            put_loop(1 + j, dot(normed_own, grad_pair_rank[:, j * rank : (j + 1) * rank]))
-        fed_own = low(product_t(select[...], fed_s[l]))
-        for j in range(2):
-            put_loop(3 + j, dot(fed_own, grad_widen[:, j * rank : (j + 1) * rank]))
-        attend_own = low(product_t(select[...], grad_attend))
-        put_loop(5, sum(dot(attend_own, piece) for piece in split3(or_s[l])))
-        feed_own = low(product_t(select[...], grad_feed))
-        put_loop(6, sum(dot(feed_own, piece) for piece in split3(sr_s[l])))
-        for j in range(2):
-            rank_own = low(product_t(rank_select, kvr_s[l, :, j * rank : (j + 1) * rank]))
-            put(
-                pl.multiple_of(base + 7 * tall + j * rank_quarter, 8), rank_quarter, rank_quarter,
-                dot(rank_own, grad_pair[:, j * head : (j + 1) * head]),
-            )
         return carry
 
     lax.fori_loop(0, loops, back, 0)
-    last = loops - 1
-    for copies in (
-        x_copies(0, last), x_copies(2, last), r_copies(0, last), r_copies(1, last), r_copies(3, last),
-        b_copies(4, last), b_copies(5, last), q_copies(1, last),
-        x_copies(1, 0), x_copies(3, 0), r_copies(2, 0), r_copies(4, 0),
-        b_copies(0, 0), b_copies(1, 0), b_copies(2, 0), b_copies(3, 0), q_copies(0, 0),
-    ):
-        finish(copies)
-    for l in range(loops):
-        for copies in (x_copies(0, l), r_copies(0, l), r_copies(1, l), b_copies(0, l)):
-            copies[1].wait_recv()
-
-        @pl.when(is_end)
-        def _():
-            for copy in far_feed(l) + far_act(l):
-                copy.wait_send()
-
-        @pl.when(jnp.logical_not(is_end))
-        def _():
-            onward = [x_copies(1, l)[2], r_copies(2, l)[2], b_copies(4, l)[2], b_copies(5, l)[2]]
-            for copy in onward + far_feed(l) + far_act(l):
-                copy.wait_recv()
-
+    late_s[0] = low(finish_side(1, rank + 2 * head))
+    raw_of(0)
     grad_ref[...] = g_s[...]
     for b in range(blocks):
         ends = jnp.zeros((8, head), jnp.float32)
@@ -980,6 +1004,57 @@
         raw_ref[b % 2, b // 2, raw_rows.gains : raw_rows.gains + 2, :block] = gain_s[
             :2, b * block : (b + 1) * block
         ]
+    last = loops - 1
+    for copies in (
+        x_copies(0, last), x_copies(2, last), r_copies(0, last), r_copies(1, last), r_copies(3, last),
+        q_copies(1, last), x_copies(1, 0), x_copies(3, 0), r_copies(2, 0), r_copies(4, 0),
+        q_copies(0, 0),
+    ):
+        finish(copies, False)
+    for copies in (
+        b_copies(4, last), b_copies(5, last), b_copies(0, 0), b_copies(1, 0), b_copies(2, 0),
+        b_copies(3, 0),
+    ):
+        finish(copies)
+
+    def to_core(l, half):
+        lanes = end_span(l, half)
+        return [
+            remote(x_end.at[:, :, lanes], x_end.at[:, :, lanes], xc_s.at[l], xc_r.at[l], core),
+            remote(r_end.at[:, :, lanes], r_end.at[:, :, lanes], rc_s.at[l], rc_r.at[l], core),
+        ]
+
+    for l in range(loops):
+        for copies in (x_copies(0, l), r_copies(0, l), r_copies(1, l), b_copies(0, l)):
+            copies[1].wait_recv()
+
+        @pl.when(is_end)
+        def _():
+            for copy in far_act(l):
+                copy.wait_send()
+
+        @pl.when(jnp.logical_and(is_end, side == 1))
+        def _():
+            for copy in far_feed(l):
+                copy.wait_send()
+
+        for half in range(2):
+
+            @pl.when(jnp.logical_and(jnp.logical_not(is_end), side == half))
+            def _():
+                came = far_feed(l) if half else [x_copies(1, l)[2], r_copies(2, l)[2]]
+                for copy, onward in zip(came, to_core(l, half)):
+                    copy.wait_recv()
+                    onward.start()
+
+    @pl.when(jnp.logical_not(is_end))
+    def _():
+        for l in range(loops):
+            for copy in [b_copies(4, l)[2], b_copies(5, l)[2]] + far_act(l):
+                copy.wait_recv()
+            for copy in to_core(l, 0):
+                copy.wait_send()
+                copy.wait_recv()
 
 
 def raw_layout(quarter, rank_quarter, loops):
@@ -998,7 +1073,7 @@
     hidden = down.shape[0]
     weights = (
         q_in, query, q_out, kv_in, pair, kv_out, output, o_in, o_out,
-        w_in, widen.transpose(1, 2, 0), w_out.swapaxes(2, 3), down, d_in, d_out,
+        widen.transpose(1, 2, 0), w_out.swapaxes(2, 3), down, d_in, d_out, w_in,
     )
     layout = raw_layout(width // (4 * dp_size), rank // (4 * dp_size), loops)
     line = dp_size // 2
@@ -1022,14 +1097,14 @@
     )
     vmem = pl.BlockSpec(memory_space=pltpu.VMEM)
     hbm = pl.BlockSpec(memory_space=pl.ANY)
-    widest = width + rank + 2 * head
-    pieces = -(-widest // SUM_STEP)
+    widest = rank + 2 * head
+    pieces = -(-width // SUM_STEP)
     dma = pltpu.SemaphoreType.DMA
 
     def kept(columns, dtype, count=loops):
         return pltpu.VMEM((count, tokens, columns), dtype)
 
-    scratch = [pltpu.VMEM(w.shape, bf16) for w in weights] + [
+    scratch = [pltpu.VMEM(w.shape, bf16) for w in weights[:-1]] + [
         kept(width, f32, loops + 1), kept(width, f32), kept(width, bf16), kept(rank, bf16),
         kept(2 * rank, bf16), kept(head, bf16), kept(head, bf16), kept(head, bf16), kept(tokens, f32),
         kept(head, bf16), kept(rank, f32), kept(width, bf16), kept(2 * rank, bf16),
@@ -1037,9 +1112,13 @@
         pltpu.VMEM((tokens, hidden), bf16), pltpu.VMEM((tokens, hidden), bf16),
         pltpu.VMEM((tokens, width), f32), pltpu.VMEM((8, width), f32),
         pltpu.VMEM((dp_size * 48, width), bf16),
-        pltpu.VMEM((tokens, widest), f32), pltpu.VMEM((tokens, widest), f32),
-        pltpu.VMEM((tokens // 2, widest), f32), pltpu.VMEM((tokens // 2, widest), f32),
-        pltpu.VMEM((2, tokens // 2, widest), f32),
+        pltpu.VMEM((tokens, width), f32), pltpu.VMEM((tokens, width), f32),
+        pltpu.VMEM((tokens // 2, width), f32), pltpu.VMEM((tokens // 2, width), f32),
+        pltpu.VMEM((2, tokens // 2, width), f32),
+        pltpu.VMEM((2, tokens, widest), f32), pltpu.VMEM((2, tokens // 2, widest), f32),
+        pltpu.VMEM((2, tokens // 2, widest), f32), pltpu.VMEM((2, tokens // 2, widest), f32),
+        pltpu.VMEM((2, tokens, widest), f32),
+        kept(widest, bf16), kept(2 * rank, bf16), pltpu.VMEM((loops, 2, dp_size * 48, tokens), bf16),
         pltpu.VMEM((4, 2, line, block, tokens), f32), pltpu.VMEM((5, 2, line, rank_block, tokens), f32),
         pltpu.VMEM((6, tokens, WIDE), f32), pltpu.VMEM((2, tokens, head), f32),
         pltpu.VMEM((loops, width, 2 * rank), bf16), pltpu.VMEM((loops, width, 2 * rank), bf16),
@@ -1051,6 +1130,7 @@
     ]
     scratch += [dma((2, loops))] * 2 + [dma((3, loops))] * 4
     scratch += [dma((2, loops))] * 4 + [dma((2, 2, loops))] * 2
+    scratch += [dma((2,))] * 6 + [dma((loops,))] * 4
     return pl.pallas_call(
         block_kernel,
         out_shape=out_shape,
@@ -1565,9 +1645,43 @@
     )(*factors)
 
     return (
+        gains, q_w, pair_w, o_w, e_w, s_w, q_i, q_o, p_i, p_o, o_i, o_o, e_i, e_o, s_i, s_o
+    )
+
+
+def in_place(results):
+    gains, q_w, pair_w, o_w, e_w, s_w, q_i, q_o, p_i, p_o, o_i, o_o, e_i, e_o, s_i, s_o = results
+    return (
         gains[0], gains[1], q_w, pair_w, o_w.T, e_w, s_w.T, q_i.swapaxes(0, 1), q_o, p_i, p_o,
         o_i.swapaxes(1, 2), o_o.swapaxes(1, 2), e_i, e_o, s_i.swapaxes(1, 2), s_o.swapaxes(1, 2),
     )
+
+
+def copy_kernel(*refs):
+    count = (len(refs) - 2) // 3
+    sources, targets, rooms = refs[:count], refs[count : 2 * count], refs[2 * count : 3 * count]
+    come = [pltpu.make_async_copy(v, room, refs[-2].at[i]) for i, (v, room) in enumerate(zip(sources, rooms))]
+    go = [pltpu.make_async_copy(room, v, refs[-1].at[i]) for i, (v, room) in enumerate(zip(targets, rooms))]
+    for copy in come:
+        copy.start()
+    for first, second in zip(come, go):
+        first.wait()
+        second.start()
+    for copy in go:
+        copy.wait()
+
+
+def placed(values):
+    hbm = pl.BlockSpec(memory_space=pl.ANY)
+    sems = pltpu.SemaphoreType.DMA((len(values),))
+    return pl.pallas_call(
+        copy_kernel,
+        out_shape=tuple(jax.ShapeDtypeStruct(v.shape, v.dtype) for v in values),
+        in_specs=[hbm] * len(values),
+        out_specs=(hbm,) * len(values),
+        scratch_shapes=[pltpu.VMEM(v.shape, v.dtype) for v in values] + [sems, sems],
+        compiler_params=pltpu.CompilerParams(vmem_limit_bytes=60 << 20),
+    )(*values)
 
 
 def per_device(dp_size, mp_size, block_input, cotangent, segments, *parameters):
@@ -1578,6 +1692,8 @@
             block_input, cotangent, segments, shared, stacked, dp_size
         )
         gradients = line_gradients(factors, loops, dp_size, mp_size, shared[6].shape[0])
+        output, input_grad, *gradients = placed((output, input_grad, *gradients))
+        gradients = in_place(gradients)
         return (output, input_grad, *gradients)
     tables = rotary_tables(segments[0], shared[3].shape[1] // 2)
     total = mp_total(mp_size)

time: 448 us -> 431 us (0.962)
  local copies, waits for them, and re-layouts: 18.6 us -> 3.91 us
    unnamed x47 -> x0, local copies, waits for them, and re-layouts: 14.7 us -> none
    pallas_call x1, Pallas kernels: 150 us -> 139 us  [block_and_factors(): pl.pallas_call(block_kernel, out_shape=out_shape, in_specs=[vmem] * 5 + [...]
    pallas_call x0 -> x1, Pallas kernels: none -> 5.52 us  [placed(): pl.pallas_call(copy_kernel, out_shape=tuple((jax.ShapeDtypeStruct(v.shape...]
where the time goes in v4:
time: 431 us; the launch traced here: 430 us
  Pallas kernels  426 us (99%)
    pallas_call x1, Pallas kernels, line_gradients(): pl.pallas_call(line_kernel, out_shape=tuple((jax.ShapeDtypeStruct(v, f32)...  281 us
    pallas_call x1, Pallas kernels, block_and_factors(): pl.pallas_call(block_kernel, out_shape=out_shape, in_specs=[vmem] * 5 + [...  139 us

profile of v4, /device:TPU:0, one launch (start us, length us, event | category | flops | bytes accessed | tf_op | source)
XLA Modules:
  0.0 430.5 jit_solution(17221372392920736374)
XLA Ops:
  0.7 1.3 broadcast_in_dim.6.refs_3_
  1.9 1.3 broadcast_in_dim.7.refs_4_
  3.2 139.2 %shard_map.339 = (bf16[128,1152]{1,0:T(8,128)(2,1)}, f32[128,1152]{1,0:T(8,128)}, f32[2,4,680,256]{3,2,1,0:T(8,128)}, f32[4,2,4,144,256]{4,3,2,1,0:T(8,128)}, f3...) custom-call(bf16[128,1152]{1,0:T(8,128)(2,1)} %refs_0_.1, ...), custom_call_target="tpu_custom_call" | custom-call | tf_op jit(solution)/shard_map/pallas_call | solution.py:1134
  142.5 281.1 %shard_map.340 = (f32[2,144]{1,0:T(2,128)}, f32[144,256]{1,0:T(8,128)}, f32[36,512]{1,0:T(8,128)}, f32[144,256]{1,0:T(8,128)}, f32[144,2,1728]{2,1,0:T(2,128)}, ...) custom-call(f32[2,4,680,256]{3,2,1,0:T(8,128)} %get-tuple-element.68, ...), custom_call_target="tpu_custom_call" | custom-call | tf_op jit(solution)/shard_map/pallas_call | solution.py:1622
  423.6 5.5 %shard_map.341 = (bf16[128,1152]{1,0:T(8,128)(2,1)}, f32[128,1152]{1,0:T(8,128)}, f32[2,144]{1,0:T(2,128)}, f32[144,256]{1,0:T(8,128)}, f32[36,512]{1,0:T(8,128)...) custom-call(bf16[128,1152]{1,0:T(8,128)(2,1)} %get-tuple-element.66., ...), custom_call_target="tpu_custom_call" | custom-call | tf_op jit(solution)/shard_map/pallas_call | solution.py:1677
  429.1 1.3 fusion

commit v5 on v4

--- a/solution.py
+++ b/solution.py
@@ -558,15 +558,18 @@
             rs[i, b % 2, b // 2] = turned[b * size : (b + 1) * size]
         launch(r_copies(i, l), False)
 
-    def ship_b(i, l, value, again, before):
+    def ship_b(i, l, values, again, before):
         @pl.when(again)
         def _():
             finish(b_copies(i, before))
 
-        n = value.shape[1]
-        bs[i, :, :n] = value.astype(jnp.float32)
-        if n < WIDE:
-            bs[i, :, n:] = jnp.zeros((tokens, WIDE - n), jnp.float32)
+        filled = 0
+        for value in values:
+            n = value.shape[1]
+            bs[i, :, filled : filled + n] = value.astype(jnp.float32)
+            filled += n
+        if filled < WIDE:
+            bs[i, :, filled:] = jnp.zeros((tokens, WIDE - filled), jnp.float32)
         launch(b_copies(i, l))
 
     def ship_q(i, l, value, again, before):
@@ -691,7 +694,7 @@
         jnp.logical_and(across_row == down_row, at_row >= at_column), 1.0, 0.0
     )
     h_s[0] = h_in[...].astype(jnp.float32)
-    mixer, feed = mixer_gain[...], feed_gain[...]
+    mixer, feed = mixer_gain[...].reshape(1, width), feed_gain[...].reshape(1, width)
 
     def forward(l, carry):
         def need(*copies):
@@ -781,7 +784,7 @@
             )
             up_s[l, :, at : at + n] = up
             act_s[:, at : at + n] = low(gelu_parts(gate)[0] * up)
-            ship_b(4 + at // WIDE, l, act_s[:, at : at + n], again, 0)
+            ship_b(4 + at // WIDE, l, [act_s[:, at : at + n]], again, 0)
         need(load.down, load.d_in, load.d_out)
 
         shrink_rank = dot(act_s[...], W.d_in[l])
@@ -896,8 +899,14 @@
             grad_up = low(grad_act * gelu)
             gg_s[:, at : at + n] = grad_gate
             gu_s[:, at : at + n] = grad_up
-            ship_b(i, l, grad_gate, again, before)
-            ship_b(2 + i, l, grad_up, again, before)
+            if i == 0:
+                ship_b(0, l, [grad_gate], again, before)
+                ship_b(2, l, [grad_up], again, before)
+            else:
+                ahead = WIDE - n
+                grad_up = grad_up.astype(jnp.float32)
+                ship_b(1, l, [grad_gate, grad_up[:, :ahead]], again, before)
+                ship_b(3, l, [grad_up[:, ahead:]], again, before)
 
         for j, value in enumerate((gg_s, gu_s)):
             side_part[0, :, j * rank : (j + 1) * rank] = dot(value[...], W.w_out[l, j])
@@ -926,6 +935,7 @@
 
             @pl.when(again)
             def _():
+                pass_feed(loops - 1)
                 raw_of(loops - 1)
 
         sum_over_mp(fill_fed, 0, 2 * rank, finish_before_fed, idle_fed)
@@ -981,7 +991,9 @@
             def _():
                 pass_act(loops - 1)
 
-            pass_feed(l)
+            @pl.when(again)
+            def _():
+                pass_feed(0)
 
         sum_over_mp(fill_normed, 1, rank + 2 * head, finish_before_normed, idle_normed)
         grad_normed = total[...]
@@ -1058,7 +1070,7 @@
 
 
 def raw_layout(quarter, rank_quarter, loops):
-    tall = -(-quarter // 8) * 8
+    tall = quarter
     loop = 7 * tall + 2 * rank_quarter
     gains = 2 * tall + loops * loop
     return SimpleNamespace(tall=tall, loop=loop, gains=gains, all=gains + 8)
@@ -1141,14 +1153,14 @@
             collective_id=21, has_side_effects=True, vmem_limit_bytes=63 << 20
         ),
     )(
-        block_input, cotangent, segments, mixer_gain[None], feed_gain[None],
+        block_input, cotangent, segments, mixer_gain, feed_gain,
         *weights,
     )
 
 
 def line_kernel(
     raw_all, x_all, r_all, b_all, q_all, x_got, r_got, b_got, x_end_all, r_end_all, b_end_all,
-    gains_out, q_w, pair_w, o_w, e_w, s_w, q_i, q_o, p_i, p_o, o_i, o_o, e_i, e_o, s_i, s_o,
+    mixer_out, feed_out, q_w, pair_w, o_w, e_w, s_w, q_i, q_o, p_i, p_o, o_i, o_o, e_i, e_o, s_i, s_o,
     main_out, side_out, raw_out, around,
     x_own, r_own, b_own, q_own, x_far, r_far, b_far, q_far, x_end, r_end, b_end, raw_own, raw_far, product_ref,
     main_right, main_left, side_right, side_left, raw_right, raw_left,
@@ -1169,6 +1181,8 @@
     loops, head = s_i.shape[0], q_w.shape[1]
     layout = raw_layout(quarter, rank_block // 4, loops)
     tall = layout.tall
+    tail = hidden - WIDE
+    short = 2 * hidden - 3 * WIDE
 
     barrier = pltpu.get_barrier_semaphore()
     for device in (pair, core, other):
@@ -1235,20 +1249,23 @@
             copy.start()
 
     own_copy.start()
-    for copy in at_start:
+    for copy in at_start[:5]:
         copy.wait()
 
-    @pl.when(inner)
-    def _():
-        for copy in for_ends:
-            copy.wait()
-
     def chain(target, step, slot, steps, value, out, right, left, r_s, r_r, l_s, l_r, credits):
-        def move(buffer, send, recv, i, s, device):
+        def move(buffer, send, recv, i, s, device, size):
+            piece = buffer.at[i, s, :, pl.ds(0, size)]
             return pltpu.make_async_remote_copy(
-                buffer.at[i, s], buffer.at[i, s], send.at[i, s], recv.at[i, s],
-                device_id=device, device_id_type=MESH,
-            )
+                piece, piece, send.at[i, s], recv.at[i, s], device_id=device, device_id_type=MESH
+            )
+
+        def at_size(act):
+            full = right.shape[3]
+            if credits:
+                pl.when(step < steps - 1)(lambda: act(full))
+                pl.when(step == steps - 1)(lambda: act(short))
+            else:
+                act(full)
 
         def inside(at):
             return lax.rem(at, 3) == 1 if credits else at < 0
@@ -1264,8 +1281,8 @@
                 pl.semaphore_signal(credit.at[i], inc=1, device_id=source, device_id_type=MESH)
 
         def pass_on(i, place, buffer, send, recv, onward, source, at_end, next_to_end, credit):
-            def here(i, s):
-                return move(buffer, send, recv, i, s, onward)
+            def here(i, s, size=right.shape[3]):
+                return move(buffer, send, recv, i, s, onward, size)
 
             def begin():
                 if credits:
@@ -1274,7 +1291,7 @@
                     def _():
                         pl.semaphore_wait(credit.at[i], 1)
 
-                here(i, slot).start()
+                at_size(lambda size: here(i, slot, size).start())
 
             @pl.when(jnp.logical_and(at_end, jnp.logical_not(inside(step))))
             def _():
@@ -1289,7 +1306,7 @@
 
                     @pl.when(place == 2)
                     def _():
-                        here(2 - i, slot).wait_send()
+                        at_size(lambda size: here(2 - i, slot, size).wait_send())
 
                     begin()
                 else:
@@ -1314,7 +1331,7 @@
                 @pl.when(has_source)
                 def _():
                     product = value()
-                    here(i, slot).wait_recv()
+                    at_size(lambda size: here(i, slot, size).wait_recv())
                     buffer[i, slot] += product
 
                 begin()
@@ -1332,11 +1349,12 @@
             out[...] = value()
 
     def arrive(step, slot, steps, out, right, left, r_s, r_r, l_s, l_r, credits):
-        def came(buffer, send, recv, i):
-            return pltpu.make_async_remote_copy(
-                buffer.at[i, slot], buffer.at[i, slot], send.at[i, slot], recv.at[i, slot],
-                device_id=pair, device_id_type=MESH,
-            )
+        def take(buffer, send, recv, i, size):
+            piece = buffer.at[i, slot, :, pl.ds(0, size)]
+            pltpu.make_async_remote_copy(
+                piece, piece, send.at[i, slot], recv.at[i, slot], device_id=pair, device_id_type=MESH
+            ).wait_recv()
+            out[:, :size] += buffer[i, slot, :, :size]
 
         started_inside = lax.rem(step, 3) == 1 if credits else step < 0
 
@@ -1347,8 +1365,12 @@
 
                 @pl.when(jnp.logical_not(quiet))
                 def _():
-                    came(buffer, send, recv, i).wait_recv()
-                    out[...] += buffer[i, slot]
+                    full = buffer.shape[3]
+                    if credits:
+                        pl.when(step < steps - 1)(lambda: take(buffer, send, recv, i, full))
+                        pl.when(step == steps - 1)(lambda: take(buffer, send, recv, i, short))
+                    else:
+                        take(buffer, send, recv, i, full)
 
                 if credits:
                     skip = jnp.logical_and(from_end, lax.rem(step + 3, 3) == 1)
@@ -1364,9 +1386,9 @@
 
     def settle(slot, right, left, r_s, l_s, main):
         def wait(buffer, send, i, device):
+            piece = buffer.at[i, slot, :, pl.ds(0, short if main else buffer.shape[3])]
             pltpu.make_async_remote_copy(
-                buffer.at[i, slot], buffer.at[i, slot], send.at[i, slot], send.at[i, slot],
-                device_id=device, device_id_type=MESH,
+                piece, piece, send.at[i, slot], send.at[i, slot], device_id=device, device_id_type=MESH
             ).wait_send()
 
         for target in range(4):
@@ -1394,10 +1416,13 @@
     steps = b_all.shape[0]
 
     def left_times(x_index, group, target, own, far):
+        shared = dot(x_own[x_index, target], own) + dot(x_far[x_index, target], far)
+        return [shared, *rank_times(group, target, own, far)]
+
+    def rank_times(group, target, own, far):
         half = own.shape[0] // 2
         rank_own, rank_far = r_own[group, target], r_far[group, target]
         return [
-            dot(x_own[x_index, target], own) + dot(x_far[x_index, target], far),
             dot(rank_own[:, :half], own[:half]) + dot(rank_far[:, :half], far[:half]),
             dot(rank_own[:, half:], own[half:]) + dot(rank_far[:, half:], far[half:]),
         ]
@@ -1408,22 +1433,29 @@
         arrive(
             step, slot, steps, main_out.at[slot], main_right, main_left, mr_s, mr_r, ml_s, ml_r, True,
         )
-        for part, (at, n) in enumerate(((0, WIDE), (WIDE, hidden - WIDE))):
-            for j in range(2):
-
-                @pl.when(chunk == 2 * j + part)
-                def _():
-                    e_w[:, j, at : at + n] = main_out[slot, :block, :n]
-                    for l in range(loops):
-                        start = block + l * rank_block
-                        e_o[l, j, :, at : at + n] = main_out[slot, start : start + rank_block, :n]
+        parts = (
+            (0, 0, 0, 0, WIDE), (1, 0, 0, WIDE, tail), (1, tail, 1, WIDE, WIDE - tail),
+            (2, 0, 1, 0, WIDE), (3, 0, 1, 2 * WIDE - tail, short),
+        )
+        for which, start, j, at, n in parts:
+
+            @pl.when(chunk == which)
+            def _():
+                e_w[:, j, at : at + n] = main_out[slot, :block, start : start + n]
+                for l in range(loops):
+                    first = block + l * rank_block
+                    e_o[l, j, :, at : at + n] = main_out[
+                        slot, first : first + rank_block, start : start + n
+                    ]
+
+        for part, (at, n) in enumerate(((0, WIDE), (WIDE, tail))):
 
             @pl.when(chunk == 4 + part)
             def _():
                 s_w[:, at : at + n] = main_out[slot, :block, :n]
                 for l in range(loops):
-                    start = block + l * rank_block
-                    s_i[l, :, at : at + n] = main_out[slot, start : start + rank_block, :n]
+                    first = block + l * rank_block
+                    s_i[l, :, at : at + n] = main_out[slot, first : first + rank_block, :n]
 
     def turn_body(at, carry):
         step, turn = at // 4, lax.rem(at, 4)
@@ -1447,6 +1479,13 @@
             @pl.when(step == 1)
             def _():
                 b_copy(2).start()
+                for copy in at_start[5:]:
+                    copy.wait()
+
+                @pl.when(inner)
+                def _():
+                    for copy in for_ends:
+                        copy.wait()
 
             @pl.when(step == 2)
             def _():
@@ -1470,6 +1509,19 @@
                 b_own[lax.rem(step, 2)].astype(jnp.bfloat16), b_far[chunk].astype(jnp.bfloat16),
             )
             product_ref[...] = jnp.concatenate(parts, axis=0)
+
+            @pl.when(chunk == 1)
+            def _():
+                other_rank = rank_times(
+                    1, target, b_own[lax.rem(step, 2)].astype(jnp.bfloat16),
+                    b_far[1].astype(jnp.bfloat16),
+                )
+                kept = product_ref[block:]
+                column = lax.broadcasted_iota(jnp.int32, kept.shape, 1)
+                product_ref[block:] = jnp.where(
+                    column < tail, kept, jnp.concatenate(other_rank, axis=0)
+                )
+
             beyond = jnp.logical_or(
                 jnp.logical_and(z == 1, target >= 1),
                 jnp.logical_and(z == last - 1, target <= last - 1),
@@ -1567,7 +1619,8 @@
         start = block + l * rank_block
         q_o[l] = side_out[start : start + rank_block, :head]
         o_i[l] = side_out[start : start + rank_block, head:]
-    gains_out[...] = raw_out[layout.gains : layout.gains + 2, :block]
+    mixer_out[...] = raw_out[layout.gains, :block]
+    feed_out[...] = raw_out[layout.gains + 1, :block]
     for j in range(2):
         pair_w[:, j * head : (j + 1) * head] = raw_out[j * tall : j * tall + quarter]
     for l in range(loops):
@@ -1613,13 +1666,13 @@
     half_r = pltpu.VMEM((r_all.shape[0], *r_all.shape[2:]), f32)
     whole_b, whole_q = pltpu.VMEM(b_all.shape, f32), pltpu.VMEM(q_all.shape, f32)
     shapes = (
-        (2, block), (block, head), (quarter, 2 * head), (block, head), (block, 2, hidden),
+        (block,), (block,), (block, head), (quarter, 2 * head), (block, head), (block, 2, hidden),
         (block, hidden), (quarter, loops, head), (loops, rank_block, head), (loops, quarter, 2, head),
         (loops, 2, rank_quarter, head), (loops, rank_block, head), (loops, block, head),
         (loops, quarter, 2, head), (loops, 2, rank_block, hidden), (loops, rank_block, hidden),
         (loops, block, head),
     )
-    gains, q_w, pair_w, o_w, e_w, s_w, q_i, q_o, p_i, p_o, o_i, o_o, e_i, e_o, s_i, s_o = pl.pallas_call(
+    return pl.pallas_call(
         line_kernel,
         out_shape=tuple(jax.ShapeDtypeStruct(v, f32) for v in shapes),
         in_specs=[hbm] * 11,
@@ -1644,15 +1697,11 @@
         ),
     )(*factors)
 
+
+def in_place(results):
+    mixer, feed, q_w, pair_w, o_w, e_w, s_w, q_i, q_o, p_i, p_o, o_i, o_o, e_i, e_o, s_i, s_o = results
     return (
-        gains, q_w, pair_w, o_w, e_w, s_w, q_i, q_o, p_i, p_o, o_i, o_o, e_i, e_o, s_i, s_o
-    )
-
-
-def in_place(results):
-    gains, q_w, pair_w, o_w, e_w, s_w, q_i, q_o, p_i, p_o, o_i, o_o, e_i, e_o, s_i, s_o = results
-    return (
-        gains[0], gains[1], q_w, pair_w, o_w.T, e_w, s_w.T, q_i.swapaxes(0, 1), q_o, p_i, p_o,
+        mixer, feed, q_w, pair_w, o_w.T, e_w, s_w.T, q_i.swapaxes(0, 1), q_o, p_i, p_o,
         o_i.swapaxes(1, 2), o_o.swapaxes(1, 2), e_i, e_o, s_i.swapaxes(1, 2), s_o.swapaxes(1, 2),
     )
 

time: 431 us -> 408 us (0.947)
  Pallas kernels: 426 us -> 407 us
    pallas_call x1, Pallas kernels: 281 us -> 272 us  [line_gradients(): pl.pallas_call(line_kernel, out_shape=tuple((jax.ShapeDtypeStruct(v, f32)...]
    pallas_call x1, Pallas kernels: 139 us -> 130 us  [block_and_factors(): pl.pallas_call(block_kernel, out_shape=out_shape, in_specs=[vmem] * 5 + [...]
where the time goes in v5:
time: 408 us
  Pallas kernels  407 us (100%)
    pallas_call x1, Pallas kernels, line_gradients(): pl.pallas_call(line_kernel, out_shape=tuple((jax.ShapeDtypeStruct(v, f32)...  272 us
    pallas_call x1, Pallas kernels, block_and_factors(): pl.pallas_call(block_kernel, out_shape=out_shape, in_specs=[vmem] * 5 + [...  130 us

profile of v5, /device:TPU:0, one launch (start us, length us, event | category | flops | bytes accessed | tf_op | source)
XLA Modules:
  0.0 407.9 jit_solution(6366136097410443789)
XLA Ops:
  0.7 129.9 %shard_map.339 = (bf16[128,1152]{1,0:T(8,128)(2,1)}, f32[128,1152]{1,0:T(8,128)}, f32[2,4,616,256]{3,2,1,0:T(8,128)}, f32[4,2,4,144,256]{4,3,2,1,0:T(8,128)}, f3...) custom-call(bf16[128,1152]{1,0:T(8,128)(2,1)} %refs_0_.1, ...), custom_call_target="tpu_custom_call" | custom-call | tf_op jit(solution)/shard_map/pallas_call | solution.py:1146
  130.6 271.6 %shard_map.340 = (f32[144]{0:T(256)}, f32[144]{0:T(256)}, f32[144,256]{1,0:T(8,128)}, f32[36,512]{1,0:T(8,128)}, f32[144,256]{1,0:T(8,128)}, /*index=5*/f32[144,...) custom-call(f32[2,4,616,256]{3,2,1,0:T(8,128)} %get-tuple-element.70, ...), custom_call_target="tpu_custom_call" | custom-call | tf_op jit(solution)/shard_map/pallas_call | solution.py:1675
  402.2 5.5 %shard_map.341 = (bf16[128,1152]{1,0:T(8,128)(2,1)}, f32[128,1152]{1,0:T(8,128)}, f32[144]{0:T(256)}, f32[144]{0:T(256)}, f32[144,256]{1,0:T(8,128)}, /*index=5*...) custom-call(bf16[128,1152]{1,0:T(8,128)(2,1)} %get-tuple-element.68., ...), custom_call_target="tpu_custom_call" | custom-call | tf_op jit(solution)/shard_map/pallas_call | solution.py:1726

commit v6 on v5

--- a/solution.py
+++ b/solution.py
@@ -386,7 +386,7 @@
         part, total, near, mine, far, side_part, side_near, side_mine, side_far, side_total,
         late_s, er_grad_s, chosen_s, xs, rs, bs, qs, kv_flat, w_flat, cosine_ref, sine_ref, mask_ref,
         load_sems, c_s, c_r, y_s, y_r, e_s, e_r,
-        xl, rl, bl, ql, x_s, x_r, r_s, r_r, b_s, b_r, xe_s, xe_r, re_s, re_r, be_s, be_r,
+        xl, rl, bl, ql, x_s, x_r, r_s, r_r, b_s, b_r, xe_s, xe_r, re_s, re_r, be_s, be_r, bf_s, bf_r,
         sc_s, sc_r, sy_s, sy_r, se_s, se_r, xc_s, xc_r, rc_s, rc_r,
     ) = refs
     W = SimpleNamespace(**dict(zip(WEIGHTS, weights)))
@@ -443,9 +443,9 @@
             across = remote(
                 xs.at[i, 1 - x], x_got.at[i, :, :, span(l)], x_s.at[i, l], x_r.at[i, l], pair
             )
-        if i == 1:
             onward = remote(
-                xs.at[i, x], x_end.at[:, :, end_span(l, 0)], xe_s.at[0, l], xe_r.at[0, l], near_end
+                xs.at[i, x], x_end.at[i, :, :, end_span(l, 0)],
+                xe_s.at[0, i, l], xe_r.at[0, i, l], near_end,
             )
         return pltpu.make_async_copy(xs.at[i], x_all.at[i, :, :, :, span(l)], xl.at[i, l]), across, onward
 
@@ -455,9 +455,10 @@
             across = remote(
                 rs.at[i, 1 - x], r_got.at[i, :, :, span(l)], r_s.at[i, l], r_r.at[i, l], pair
             )
-        if i == 2:
+        if i in (1, 2):
             onward = remote(
-                rs.at[i, x], r_end.at[:, :, end_span(l, 0)], re_s.at[0, l], re_r.at[0, l], near_end
+                rs.at[i, x], r_end.at[i - 1, :, :, end_span(l, 0)],
+                re_s.at[0, i - 1, l], re_r.at[0, i - 1, l], near_end,
             )
         return pltpu.make_async_copy(rs.at[i], r_all.at[i, :, :, :, span(l)], rl.at[i, l]), across, onward
 
@@ -466,10 +467,10 @@
         if i in (0, 4, 5):
             k = max(0, i - 3)
             across = remote(bs.at[i], b_got.at[k, span(l)], b_s.at[k, l], b_r.at[k, l], pair)
-        if i >= 4:
+        if i >= 3:
+            k = (i - 4) % 3
             onward = remote(
-                bs.at[i], b_end.at[i - 4, end_span(l, 0)],
-                be_s.at[i - 4, 0, l], be_r.at[i - 4, 0, l], near_end,
+                bs.at[i], b_end.at[k, end_span(l, 0)], be_s.at[k, l], be_r.at[k, l], near_end
             )
         return pltpu.make_async_copy(bs.at[i], b_all.at[i, span(l)], bl.at[i, l]), across, onward
 
@@ -498,26 +499,22 @@
             def _():
                 onward.wait_send()
 
-    def far_feed(l):
+    def far_rows(i, l):
         return [
             remote(
-                x_got.at[1, :, :, span(l)], x_end.at[:, :, end_span(l, 1)],
-                xe_s.at[1, l], xe_r.at[1, l], near_end,
+                x_got.at[i, :, :, span(l)], x_end.at[i, :, :, end_span(l, 1)],
+                xe_s.at[1, i, l], xe_r.at[1, i, l], near_end,
             ),
             remote(
-                r_got.at[2, :, :, span(l)], r_end.at[:, :, end_span(l, 1)],
-                re_s.at[1, l], re_r.at[1, l], near_end,
+                r_got.at[i + 1, :, :, span(l)], r_end.at[i, :, :, end_span(l, 1)],
+                re_s.at[1, i, l], re_r.at[1, i, l], near_end,
             ),
         ]
 
     def far_act(l):
-        return [
-            remote(
-                b_got.at[1 + k, span(l)], b_end.at[k, end_span(l, 1)],
-                be_s.at[k, 1, l], be_r.at[k, 1, l], near_end,
-            )
-            for k in range(2)
-        ]
+        return remote(
+            b_got.at[1, span(l)], b_end.at[0, end_span(l, 1)], bf_s.at[l], bf_r.at[l], near_end
+        )
 
     def pass_act(l):
         for i in (4, 5):
@@ -525,16 +522,15 @@
 
         @pl.when(is_end)
         def _():
-            for copy in far_act(l):
-                copy.start()
-
-    def pass_feed(l):
-        x_copies(1, l)[1].wait_recv()
-        r_copies(2, l)[1].wait_recv()
+            far_act(l).start()
+
+    def pass_rows(i, l):
+        x_copies(i, l)[1].wait_recv()
+        r_copies(i + 1, l)[1].wait_recv()
 
         @pl.when(jnp.logical_and(is_end, side == 1))
         def _():
-            for copy in far_feed(l):
+            for copy in far_rows(i, l):
                 copy.start()
 
     def ship_x(i, l, value, again, before):
@@ -760,6 +756,14 @@
             @pl.when(again)
             def _():
                 pass_act(0)
+                pass_rows(1, loops - 1)
+
+            @pl.when(l == 0)
+            def _():
+                load.d_out.wait()
+                shrink = product_t(cot[...], W.d_out[loops - 1])
+                ship_x(1, loops - 1, cot[...], False, 0)
+                ship_r(2, loops - 1, low(shrink), False, 0)
 
         def finish_before_attend():
             @pl.when(again)
@@ -785,7 +789,7 @@
             up_s[l, :, at : at + n] = up
             act_s[:, at : at + n] = low(gelu_parts(gate)[0] * up)
             ship_b(4 + at // WIDE, l, [act_s[:, at : at + n]], again, 0)
-        need(load.down, load.d_in, load.d_out)
+        need(load.down, load.d_in)
 
         shrink_rank = dot(act_s[...], W.d_in[l])
         side_part[1, :, :rank] = shrink_rank
@@ -801,6 +805,10 @@
             ship_x(0, l, fed, again, 0)
             ship_r(0, l, widen_rank[:, :rank], again, 0)
             ship_r(1, l, widen_rank[:, rank:], again, 0)
+
+            @pl.when(again)
+            def _():
+                pass_rows(0, 0)
 
         def finish_before_feed():
             or_s[l] = finish_side(0, rank)
@@ -929,13 +937,15 @@
                 late_s[loops - 1] = low(finish_side(1, rank + 2 * head))
 
         def idle_fed():
-            ship_x(1, l, grad_feed, again, before)
-            ship_r(2, l, grad_shrink, again, before)
+            @pl.when(again)
+            def _():
+                ship_x(1, l, grad_feed, True, before)
+                ship_r(2, l, grad_shrink, True, before)
+
             chosen_s[l, 0] = low(product_t(select[...], grad_feed))
 
             @pl.when(again)
             def _():
-                pass_feed(loops - 1)
                 raw_of(loops - 1)
 
         sum_over_mp(fill_fed, 0, 2 * rank, finish_before_fed, idle_fed)
@@ -990,10 +1000,11 @@
             @pl.when(step == 0)
             def _():
                 pass_act(loops - 1)
+                pass_rows(0, loops - 1)
 
             @pl.when(again)
             def _():
-                pass_feed(0)
+                pass_rows(1, 0)
 
         sum_over_mp(fill_normed, 1, rank + 2 * head, finish_before_normed, idle_normed)
         grad_normed = total[...]
@@ -1029,42 +1040,47 @@
     ):
         finish(copies)
 
-    def to_core(l, half):
+    def to_core(i, l, half):
         lanes = end_span(l, half)
+        x_part, r_part = x_end.at[i, :, :, lanes], r_end.at[i, :, :, lanes]
         return [
-            remote(x_end.at[:, :, lanes], x_end.at[:, :, lanes], xc_s.at[l], xc_r.at[l], core),
-            remote(r_end.at[:, :, lanes], r_end.at[:, :, lanes], rc_s.at[l], rc_r.at[l], core),
+            remote(x_part, x_part, xc_s.at[i, l], xc_r.at[i, l], core),
+            remote(r_part, r_part, rc_s.at[i, l], rc_r.at[i, l], core),
         ]
 
+    both = [(i, l) for l in range(loops) for i in range(2)]
     for l in range(loops):
-        for copies in (x_copies(0, l), r_copies(0, l), r_copies(1, l), b_copies(0, l)):
+        for copies in (r_copies(0, l), b_copies(0, l)):
             copies[1].wait_recv()
 
-        @pl.when(is_end)
+    @pl.when(is_end)
+    def _():
+        for l in range(loops):
+            far_act(l).wait_send()
+
+    @pl.when(jnp.logical_and(is_end, side == 1))
+    def _():
+        for i, l in both:
+            for copy in far_rows(i, l):
+                copy.wait_send()
+
+    for half in range(2):
+
+        @pl.when(jnp.logical_and(jnp.logical_not(is_end), side == half))
         def _():
-            for copy in far_act(l):
-                copy.wait_send()
-
-        @pl.when(jnp.logical_and(is_end, side == 1))
-        def _():
-            for copy in far_feed(l):
-                copy.wait_send()
-
-        for half in range(2):
-
-            @pl.when(jnp.logical_and(jnp.logical_not(is_end), side == half))
-            def _():
-                came = far_feed(l) if half else [x_copies(1, l)[2], r_copies(2, l)[2]]
-                for copy, onward in zip(came, to_core(l, half)):
+            for i, l in both:
+                came = far_rows(i, l) if half else [x_copies(i, l)[2], r_copies(i + 1, l)[2]]
+                for copy, onward in zip(came, to_core(i, l, half)):
                     copy.wait_recv()
                     onward.start()
 
     @pl.when(jnp.logical_not(is_end))
     def _():
         for l in range(loops):
-            for copy in [b_copies(4, l)[2], b_copies(5, l)[2]] + far_act(l):
+            for copy in [b_copies(i, l)[2] for i in (3, 4, 5)] + [far_act(l)]:
                 copy.wait_recv()
-            for copy in to_core(l, 0):
+        for i, l in both:
+            for copy in to_core(i, l, 0):
                 copy.wait_send()
                 copy.wait_recv()
 
@@ -1103,9 +1119,9 @@
         shape((2, line, block, both), f32),
         shape((3, line, rank_block, both), f32),
         shape((3, both, WIDE), f32),
-        shape((line, block, 2 * both), f32),
-        shape((line, rank_block, 2 * both), f32),
-        shape((2, 2 * both, WIDE), f32),
+        shape((2, line, block, 2 * both), f32),
+        shape((2, line, rank_block, 2 * both), f32),
+        shape((3, 2 * both, WIDE), f32),
     )
     vmem = pl.BlockSpec(memory_space=pltpu.VMEM)
     hbm = pl.BlockSpec(memory_space=pl.ANY)
@@ -1141,8 +1157,8 @@
         dma((4, loops)), dma((5, loops)), dma((6, loops)), dma((2, loops)),
     ]
     scratch += [dma((2, loops))] * 2 + [dma((3, loops))] * 4
-    scratch += [dma((2, loops))] * 4 + [dma((2, 2, loops))] * 2
-    scratch += [dma((2,))] * 6 + [dma((loops,))] * 4
+    scratch += [dma((2, 2, loops))] * 4 + [dma((3, loops))] * 2 + [dma((loops,))] * 2
+    scratch += [dma((2,))] * 6 + [dma((2, loops))] * 4
     return pl.pallas_call(
         block_kernel,
         out_shape=out_shape,
@@ -1164,7 +1180,7 @@
     main_out, side_out, raw_out, around,
     x_own, r_own, b_own, q_own, x_far, r_far, b_far, q_far, x_end, r_end, b_end, raw_own, raw_far, product_ref,
     main_right, main_left, side_right, side_left, raw_right, raw_left,
-    x_s, x_r, r_s, r_r, b_s, b_r, q_s, q_r, w_s, w_r, local_sems, step_sems, around_s, around_r,
+    x_s, x_r, r_s, r_r, b_s, b_r, q_s, q_r, w_s, w_r, local_sems, step_sems, around_s, around_r, ee_s, ee_r,
     mr_s, mr_r, ml_s, ml_r, sr_s, sr_r, sl_s, sl_r, rr_s, rr_r, rl_s, rl_r,
     credit_right, credit_left,
 ):
@@ -1227,12 +1243,35 @@
         here(b_got.at[1:3], b_far.at[4:6], 5),
         here(q_all, q_own, 6),
     ]
-    for_ends = [here(x_end_all, x_end, 7), here(r_end_all, r_end, 8), here(b_end_all, b_end, 9)]
+    tokens = b_end.shape[1] // 4
+
+    def end_rows(at):
+        return pl.ds(at * tokens, tokens)
+
+    for_ends = [
+        here(x_end_all, x_end, 7), here(r_end_all, r_end, 8), here(b_end_all.at[0], b_end.at[0], 9)
+    ] + [
+        here(b_end_all.at[k, end_rows(2 * l)], b_end.at[k, end_rows(2 * l)], 9 + 2 * k + l)
+        for k in (1, 2) for l in range(loops)
+    ]
+
+    def end_copies(k):
+        return [
+            across(
+                b_end_all.at[k, end_rows(2 * l)], b_end.at[k, end_rows(2 * l + 1)],
+                ee_s.at[k - 1, l], ee_r.at[k - 1, l],
+            )
+            for l in range(loops)
+        ]
+
     own_copy = here(raw_all.at[x], raw_own, 10)
     inner = jnp.logical_and(z > 0, z < last)
 
     def chunk_of(step):
-        return jnp.where(lax.rem(step, 3) == 1, 4 + step // 3, step - (step + 1) // 3)
+        return jnp.where(lax.rem(step, 3) == 0, 4 + step // 3, step - 1 - step // 3)
+
+    def begins_inside(step):
+        return jnp.logical_or(lax.rem(step, 3) == 0, step == 5)
 
     def b_load(step):
         slot = lax.rem(step, 2)
@@ -1249,8 +1288,13 @@
             copy.start()
 
     own_copy.start()
-    for copy in at_start[:5]:
+    for copy in at_start[:-1]:
         copy.wait()
+
+    @pl.when(inner)
+    def _():
+        for copy in for_ends:
+            copy.wait()
 
     def chain(target, step, slot, steps, value, out, right, left, r_s, r_r, l_s, l_r, credits):
         def move(buffer, send, recv, i, s, device, size):
@@ -1268,7 +1312,7 @@
                 act(full)
 
         def inside(at):
-            return lax.rem(at, 3) == 1 if credits else at < 0
+            return begins_inside(at) if credits else at < 0
 
         def free(credit, i, source, at, from_end):
             @pl.when(
@@ -1300,7 +1344,7 @@
                     before = lax.rem(step + 2 - inside(step - 1).astype(jnp.int32), 3)
                     after = jnp.where(onward[0] > dp, i - 1, i + 1)
 
-                    @pl.when(jnp.logical_and(place < 2, step >= 1))
+                    @pl.when(jnp.logical_and(place < 2, step >= 2))
                     def _():
                         here(after, before).wait_send()
 
@@ -1356,7 +1400,7 @@
             ).wait_recv()
             out[:, :size] += buffer[i, slot, :, :size]
 
-        started_inside = lax.rem(step, 3) == 1 if credits else step < 0
+        started_inside = begins_inside(step) if credits else step < 0
 
         def side_of(there, from_end, buffer, send, recv, i, credit, source):
             @pl.when(there)
@@ -1373,7 +1417,7 @@
                         take(buffer, send, recv, i, full)
 
                 if credits:
-                    skip = jnp.logical_and(from_end, lax.rem(step + 3, 3) == 1)
+                    skip = jnp.logical_and(from_end, begins_inside(step + 3))
 
                     @pl.when(jnp.logical_and(step + 3 <= steps - 1, jnp.logical_not(skip)))
                     def _():
@@ -1384,23 +1428,38 @@
         side_of(z > 0, z == 1, right, r_s, r_r, jnp.maximum(z - 1, 0), credit_right, down)
         side_of(z < last, z == last - 1, left, l_s, l_r, jnp.minimum(z, last - 1), credit_left, up)
 
-    def settle(slot, right, left, r_s, l_s, main):
-        def wait(buffer, send, i, device):
-            piece = buffer.at[i, slot, :, pl.ds(0, short if main else buffer.shape[3])]
+    def settle(right, left, r_s, l_s, main):
+        def wait(buffer, send, i, slot, size, device):
+            piece = buffer.at[i, slot, :, pl.ds(0, size)]
             pltpu.make_async_remote_copy(
                 piece, piece, send.at[i, slot], send.at[i, slot], device_id=device, device_id_type=MESH
             ).wait_send()
 
-        for target in range(4):
-            rightmost, leftmost = target == 3, target == 0
-
-            @pl.when(jnp.logical_and(target > z, jnp.logical_or(z > 0, main and not rightmost)))
-            def _():
-                wait(right, r_s, target - 1, up)
-
-            @pl.when(jnp.logical_and(target < z, jnp.logical_or(z < last, main and not leftmost)))
-            def _():
-                wait(left, l_s, target, down)
+        full = right.shape[3]
+        slot, size = (2, short) if main else (0, full)
+        for target in range(1, 4):
+
+            @pl.when(jnp.logical_and(target > z, z > 0))
+            def _():
+                wait(right, r_s, target - 1, slot, size, up)
+
+        for target in range(3):
+
+            @pl.when(jnp.logical_and(target < z, z < last))
+            def _():
+                wait(left, l_s, target, slot, size, down)
+
+        if main:
+
+            @pl.when(z == 0)
+            def _():
+                for i in (0, 1):
+                    wait(right, r_s, i, 1, full, up)
+
+            @pl.when(z == last)
+            def _():
+                for i in (1, 2):
+                    wait(left, l_s, i, 1, full, down)
 
     def order(turn):
         def near(end):
@@ -1478,22 +1537,30 @@
 
             @pl.when(step == 1)
             def _():
-                b_copy(2).start()
-                for copy in at_start[5:]:
-                    copy.wait()
-
                 @pl.when(inner)
                 def _():
-                    for copy in for_ends:
-                        copy.wait()
+                    for copy in end_copies(1):
+                        copy.start()
+
+                b_copy(2).start()
 
             @pl.when(step == 2)
             def _():
+                @pl.when(inner)
+                def _():
+                    for copy in end_copies(2):
+                        copy.start()
+
                 b_copy(3).start()
 
             @pl.when(step == 3)
             def _():
                 w_copy.start()
+
+                @pl.when(inner)
+                def _():
+                    for copy in end_copies(1):
+                        copy.wait_recv()
 
             @pl.when(step == 4)
             def _():
@@ -1502,6 +1569,11 @@
                 r_copy(3).start()
                 r_copy(4).start()
                 q_copy.start()
+
+            @pl.when(jnp.logical_and(step == 5, inner))
+            def _():
+                for copy in end_copies(2):
+                    copy.wait_recv()
 
         def value():
             parts = left_times(
@@ -1527,15 +1599,16 @@
                 jnp.logical_and(z == last - 1, target <= last - 1),
             )
 
-            @pl.when(jnp.logical_and(beyond, chunk >= 4))
-            def _():
-                end = b_end[jnp.maximum(chunk - 4, 0)].astype(jnp.bfloat16)
+            @pl.when(jnp.logical_and(beyond, chunk >= 3))
+            def _():
+                end = b_end[jnp.where(chunk == 3, 2, jnp.maximum(chunk - 4, 0))].astype(jnp.bfloat16)
+                shared = jnp.where(chunk == 3, 0, 1)
                 middle = end.shape[0] // 2
                 product_ref[...] += jnp.concatenate(
                     [
-                        dot(x_end[target], end),
-                        dot(r_end[target, :, :middle], end[:middle]),
-                        dot(r_end[target, :, middle:], end[middle:]),
+                        dot(x_end[shared, target], end),
+                        dot(r_end[shared, target, :, :middle], end[:middle]),
+                        dot(r_end[shared, target, :, middle:], end[middle:]),
                     ],
                     axis=0,
                 )
@@ -1557,6 +1630,7 @@
 
     w_copy.wait_recv()
     own_copy.wait()
+    at_start[-1].wait()
 
     def raw_body(turn, carry):
         target = order(turn)
@@ -1641,9 +1715,14 @@
     for copy in (along, same, passed):
         copy.wait_send()
 
-    settle((steps - 1) % 3, main_right, main_left, mr_s, ml_s, True)
-    settle(0, side_right, side_left, sr_s, sl_s, False)
-    settle(0, raw_right, raw_left, rr_s, rl_s, False)
+    settle(main_right, main_left, mr_s, ml_s, True)
+    settle(side_right, side_left, sr_s, sl_s, False)
+    settle(raw_right, raw_left, rr_s, rl_s, False)
+    @pl.when(inner)
+    def _():
+        for copy in end_copies(1) + end_copies(2):
+            copy.wait_send()
+
     for copy in (x_copy(2), x_copy(3), r_copy(3), r_copy(4), b_copy(1), b_copy(2), b_copy(3)):
         copy.wait_send()
     q_copy.wait_send()
@@ -1689,7 +1768,8 @@
         + [pltpu.VMEM((line, 3, rows, WIDE), f32)] * 2
         + [pltpu.VMEM((line, 1, rows, 2 * head), f32)] * 2
         + [pltpu.VMEM((line, 1, layout.all, head), f32)] * 2
-        + [dma((2,))] * 4 + [dma((steps,))] * 2 + [dma] * 4 + [dma((11,)), dma((2,)), dma((3,)), dma((3,))]
+        + [dma((2,))] * 4 + [dma((steps,))] * 2 + [dma] * 4 + [dma((15,)), dma((2,)), dma((3,)), dma((3,))]
+        + [dma((2, loops))] * 2
         + [dma((line, 3))] * 4 + [dma((line, 1))] * 8
         + [pltpu.SemaphoreType.REGULAR((line,))] * 2,
         compiler_params=pltpu.CompilerParams(

time: 408 us -> 390 us (0.956)
  Pallas kernels: 407 us -> 389 us
    pallas_call x1, Pallas kernels: 272 us -> 249 us  [line_gradients(): pl.pallas_call(line_kernel, out_shape=tuple((jax.ShapeDtypeStruct(v, f32)...]
    pallas_call x1, Pallas kernels: 130 us -> 134 us  [block_and_factors(): pl.pallas_call(block_kernel, out_shape=out_shape, in_specs=[vmem] * 5 + [...]
where the time goes in v6:
time: 390 us
  Pallas kernels  389 us (100%)
    pallas_call x1, Pallas kernels, line_gradients(): pl.pallas_call(line_kernel, out_shape=tuple((jax.ShapeDtypeStruct(v, f32)...  249 us
    pallas_call x1, Pallas kernels, block_and_factors(): pl.pallas_call(block_kernel, out_shape=out_shape, in_specs=[vmem] * 5 + [...  134 us

profile of v6, /device:TPU:0, one launch (start us, length us, event | category | flops | bytes accessed | tf_op | source)
XLA Modules:
  0.0 390.1 jit_solution(7140850370457652333)
XLA Ops:
  0.7 134.3 %shard_map.339 = (bf16[128,1152]{1,0:T(8,128)(2,1)}, f32[128,1152]{1,0:T(8,128)}, f32[2,4,616,256]{3,2,1,0:T(8,128)}, f32[4,2,4,144,256]{4,3,2,1,0:T(8,128)}, f3...) custom-call(bf16[128,1152]{1,0:T(8,128)(2,1)} %refs_0_.1, ...), custom_call_target="tpu_custom_call" | custom-call | tf_op jit(solution)/shard_map/pallas_call | solution.py:1162
  135.0 249.3 %shard_map.340 = (f32[144]{0:T(256)}, f32[144]{0:T(256)}, f32[144,256]{1,0:T(8,128)}, f32[36,512]{1,0:T(8,128)}, f32[144,256]{1,0:T(8,128)}, /*index=5*/f32[144,...) custom-call(f32[2,4,616,256]{3,2,1,0:T(8,128)} %get-tuple-element.70, ...), custom_call_target="tpu_custom_call" | custom-call | tf_op jit(solution)/shard_map/pallas_call | solution.py:1754
  384.3 5.5 %shard_map.341 = (bf16[128,1152]{1,0:T(8,128)(2,1)}, f32[128,1152]{1,0:T(8,128)}, f32[144]{0:T(256)}, f32[144]{0:T(256)}, f32[144,256]{1,0:T(8,128)}, /*index=5*...) custom-call(bf16[128,1152]{1,0:T(8,128)(2,1)} %get-tuple-element.68., ...), custom_call_target="tpu_custom_call" | custom-call | tf_op jit(solution)/shard_map/pallas_call | solution.py:1806

commit v7 on v6

--- a/solution.py
+++ b/solution.py
@@ -377,7 +377,7 @@
     count = len(WEIGHTS)
     sources, refs = refs[:count], refs[count:]
     (
-        out_ref, grad_ref, raw_ref, x_all, r_all, b_all, q_all, x_got, r_got, b_got, x_end, r_end, b_end,
+        out_ref, grad_ref, raw_out, x_all, r_all, b_all, q_all, x_got, r_got, b_got, x_end, r_end, b_end,
     ), refs = refs[:13], refs[13:]
     weights, refs = (*refs[: count - 1], refs[WEIGHTS.index("kv_in")]), refs[count - 1 :]
     (
@@ -387,7 +387,7 @@
         late_s, er_grad_s, chosen_s, xs, rs, bs, qs, kv_flat, w_flat, cosine_ref, sine_ref, mask_ref,
         load_sems, c_s, c_r, y_s, y_r, e_s, e_r,
         xl, rl, bl, ql, x_s, x_r, r_s, r_r, b_s, b_r, xe_s, xe_r, re_s, re_r, be_s, be_r, bf_s, bf_r,
-        sc_s, sc_r, sy_s, sy_r, se_s, se_r, xc_s, xc_r, rc_s, rc_r,
+        sc_s, sc_r, sy_s, sy_r, se_s, se_r, xc_s, xc_r, rc_s, rc_r, raw_ref, raw_sems,
     ) = refs
     W = SimpleNamespace(**dict(zip(WEIGHTS, weights)))
     dp, mp = lax.axis_index("dp"), lax.axis_index("mp")
@@ -606,7 +606,7 @@
             copy.wait_send()
         return side_total[turn, :, :size]
 
-    def sum_over_mp(fill, turn, side_size, finish_previous, idle):
+    def sum_over_mp(fill, turn, side_size, finish_previous, idle, side_ahead=False):
         pieces = columns_of(width)
 
         def pieces_of(make):
@@ -631,19 +631,26 @@
             mine[:, at : at + n] = part[own, at : at + n] + near[:, at : at + n]
             second[i].start()
 
+        def begin_side():
+            side_first.wait_recv()
+            side_mine[turn, :, :side_size] = (
+                side_part[turn, own, :side_size] + side_near[turn, :, :side_size]
+            )
+            finish_previous()
+            side_second.start()
+
+        side_behind = jnp.logical_not(side_ahead)
+        pl.when(side_ahead)(side_first.start)
         for i, (at, n) in enumerate(pieces):
             fill(at, n)
             first[i].start()
             if i:
                 middle(i - 1)
-        side_first.start()
+            else:
+                pl.when(side_ahead)(begin_side)
+        pl.when(side_behind)(side_first.start)
         middle(len(first) - 1)
-        side_first.wait_recv()
-        side_mine[turn, :, :side_size] = (
-            side_part[turn, own, :side_size] + side_near[turn, :, :side_size]
-        )
-        finish_previous()
-        side_second.start()
+        pl.when(side_behind)(begin_side)
         idle()
         for i, (at, n) in enumerate(pieces):
             second[i].wait_recv()
@@ -890,6 +897,11 @@
                 dot(rank_own, grad_pair[:, j * head : (j + 1) * head]),
             )
 
+    raw_go = [
+        pltpu.make_async_copy(raw_ref.at[:, :, rows], raw_out.at[:, :, rows], raw_sems.at[i])
+        for i, rows in enumerate((pl.ds(0, raw_rows.gains), pl.ds(raw_rows.gains, 8)))
+    ]
+
     def back(step, carry):
         l = loops - 1 - step
         again = step > 0
@@ -1005,8 +1017,11 @@
             @pl.when(again)
             def _():
                 pass_rows(1, 0)
-
-        sum_over_mp(fill_normed, 1, rank + 2 * head, finish_before_normed, idle_normed)
+                late_s[0] = low(finish_side(1, rank + 2 * head))
+                raw_of(0)
+                raw_go[0].start()
+
+        sum_over_mp(fill_normed, 1, rank + 2 * head, finish_before_normed, idle_normed, again)
         grad_normed = total[...]
         h = h_s[l]
         factor = factor_of(h)
@@ -1018,8 +1033,6 @@
         return carry
 
     lax.fori_loop(0, loops, back, 0)
-    late_s[0] = low(finish_side(1, rank + 2 * head))
-    raw_of(0)
     grad_ref[...] = g_s[...]
     for b in range(blocks):
         ends = jnp.zeros((8, head), jnp.float32)
@@ -1027,6 +1040,9 @@
         raw_ref[b % 2, b // 2, raw_rows.gains : raw_rows.gains + 2, :block] = gain_s[
             :2, b * block : (b + 1) * block
         ]
+    raw_go[1].start()
+    for copy in raw_go:
+        copy.wait()
     last = loops - 1
     for copies in (
         x_copies(0, last), x_copies(2, last), r_copies(0, last), r_copies(1, last), r_copies(3, last),
@@ -1159,11 +1175,12 @@
     scratch += [dma((2, loops))] * 2 + [dma((3, loops))] * 4
     scratch += [dma((2, 2, loops))] * 4 + [dma((3, loops))] * 2 + [dma((loops,))] * 2
     scratch += [dma((2,))] * 6 + [dma((2, loops))] * 4
+    scratch += [pltpu.VMEM((2, line, layout.all, head), f32), dma((2,))]
     return pl.pallas_call(
         block_kernel,
         out_shape=out_shape,
         in_specs=[vmem] * 5 + [hbm] * len(weights),
-        out_specs=(vmem,) * 3 + (hbm,) * 10,
+        out_specs=(vmem,) * 2 + (hbm,) * 11,
         scratch_shapes=scratch,
         compiler_params=pltpu.CompilerParams(
             collective_id=21, has_side_effects=True, vmem_limit_bytes=63 << 20
@@ -1212,8 +1229,6 @@
     def _():
         pl.semaphore_signal(barrier, inc=1, device_id=up, device_id_type=MESH)
 
-    pl.semaphore_wait(barrier, 3 + jnp.minimum(z, 1) + jnp.minimum(last - z, 1))
-
     def across(source, target, send, recv):
         return pltpu.make_async_remote_copy(
             source, target, send, recv, device_id=pair, device_id_type=MESH
@@ -1277,7 +1292,6 @@
         slot = lax.rem(step, 2)
         return pltpu.make_async_copy(b_all.at[chunk_of(step)], b_own.at[slot], step_sems.at[slot])
 
-    b_copy(1).start()
     b_load(0).start()
     for copy in at_start:
         copy.start()
@@ -1288,6 +1302,8 @@
             copy.start()
 
     own_copy.start()
+    pl.semaphore_wait(barrier, 3 + jnp.minimum(z, 1) + jnp.minimum(last - z, 1))
+    b_copy(1).start()
     for copy in at_start[:-1]:
         copy.wait()
 

time: 390 us -> 388 us (level)
  no operation moved by 1% of the time
where the time goes in v7:
time: 388 us
  Pallas kernels  387 us (100%)
    pallas_call x1, Pallas kernels, line_gradients(): pl.pallas_call(line_kernel, out_shape=tuple((jax.ShapeDtypeStruct(v, f32)...  250 us
    pallas_call x1, Pallas kernels, block_and_factors(): pl.pallas_call(block_kernel, out_shape=out_shape, in_specs=[vmem] * 5 + [...  132 us

profile of v7, /device:TPU:0, one launch (start us, length us, event | category | flops | bytes accessed | tf_op | source)
XLA Modules:
  0.0 388.2 jit_solution(11386951983427788029)
XLA Ops:
  0.7 132.2 %shard_map.339 = (bf16[128,1152]{1,0:T(8,128)(2,1)}, f32[128,1152]{1,0:T(8,128)}, f32[2,4,616,256]{3,2,1,0:T(8,128)}, f32[4,2,4,144,256]{4,3,2,1,0:T(8,128)}, f3...) custom-call(bf16[128,1152]{1,0:T(8,128)(2,1)} %refs_0_.1, ...), custom_call_target="tpu_custom_call" | custom-call | tf_op jit(solution)/shard_map/pallas_call | solution.py:1179
  132.8 249.6 %shard_map.340 = (f32[144]{0:T(256)}, f32[144]{0:T(256)}, f32[144,256]{1,0:T(8,128)}, f32[36,512]{1,0:T(8,128)}, f32[144,256]{1,0:T(8,128)}, /*index=5*/f32[144,...) custom-call(f32[2,4,616,256]{3,2,1,0:T(8,128)} %get-tuple-element.70, ...), custom_call_target="tpu_custom_call" | custom-call | tf_op jit(solution)/shard_map/pallas_call | solution.py:1770
  382.5 5.5 %shard_map.341 = (bf16[128,1152]{1,0:T(8,128)(2,1)}, f32[128,1152]{1,0:T(8,128)}, f32[144]{0:T(256)}, f32[144]{0:T(256)}, f32[144,256]{1,0:T(8,128)}, /*index=5*...) custom-call(bf16[128,1152]{1,0:T(8,128)(2,1)} %get-tuple-element.68., ...), custom_call_target="tpu_custom_call" | custom-call | tf_op jit(solution)/shard_map/pallas_call | solution.py:1822

commit v8 on v7

--- a/solution.py
+++ b/solution.py
@@ -747,18 +747,15 @@
         again = l > 0
 
         def idle_attend():
+            @pl.when(l == 0)
+            def _():
+                for i in range(1, loops):
+                    kv_flat[i] = W.kv_in[i].reshape(width, 2 * rank)
+                load.w_in.start()
+
             ship_x(2, l, normed, again, 0)
             ship_r(3, l, query_rank, again, 0)
             ship_q(1, l, mixed, again, 0)
-
-            @pl.when(l == 0)
-            def _():
-                for i in range(1, loops):
-                    kv_flat[i] = W.kv_in[i].reshape(width, 2 * rank)
-                load.w_in.start()
-                load.w_in.wait()
-                for i in range(loops):
-                    w_flat[i] = W.w_in[i].reshape(width, 2 * rank)
 
             @pl.when(again)
             def _():
@@ -771,6 +768,8 @@
                 shrink = product_t(cot[...], W.d_out[loops - 1])
                 ship_x(1, loops - 1, cot[...], False, 0)
                 ship_r(2, loops - 1, low(shrink), False, 0)
+                load.w_in.wait()
+                w_flat[0] = W.w_in[0].reshape(width, 2 * rank)
 
         def finish_before_attend():
             @pl.when(again)
@@ -816,6 +815,11 @@
             @pl.when(again)
             def _():
                 pass_rows(0, 0)
+
+            @pl.when(l == 0)
+            def _():
+                for i in range(1, loops):
+                    w_flat[i] = W.w_in[i].reshape(width, 2 * rank)
 
         def finish_before_feed():
             or_s[l] = finish_side(0, rank)
@@ -1807,11 +1811,12 @@
     sources, targets, rooms = refs[:count], refs[count : 2 * count], refs[2 * count : 3 * count]
     come = [pltpu.make_async_copy(v, room, refs[-2].at[i]) for i, (v, room) in enumerate(zip(sources, rooms))]
     go = [pltpu.make_async_copy(room, v, refs[-1].at[i]) for i, (v, room) in enumerate(zip(targets, rooms))]
-    for copy in come:
-        copy.start()
-    for first, second in zip(come, go):
-        first.wait()
-        second.start()
+    by_size = sorted(range(count), key=lambda i: -math.prod(sources[i].shape))
+    for i in by_size:
+        come[i].start()
+    for i in by_size:
+        come[i].wait()
+        go[i].start()
     for copy in go:
         copy.wait()
 

time: 388 us -> 388 us (level)
  no operation moved by 1% of the time
where the time goes in v8:
time: 388 us
  Pallas kernels  387 us (100%)
    pallas_call x1, Pallas kernels, line_gradients(): pl.pallas_call(line_kernel, out_shape=tuple((jax.ShapeDtypeStruct(v, f32)...  250 us
    pallas_call x1, Pallas kernels, block_and_factors(): pl.pallas_call(block_kernel, out_shape=out_shape, in_specs=[vmem] * 5 + [...  132 us

profile of v8, /device:TPU:0, one launch (start us, length us, event | category | flops | bytes accessed | tf_op | source)
XLA Modules:
  0.0 388.0 jit_solution(8691656563239267862)
XLA Ops:
  0.7 131.8 %shard_map.339 = (bf16[128,1152]{1,0:T(8,128)(2,1)}, f32[128,1152]{1,0:T(8,128)}, f32[2,4,616,256]{3,2,1,0:T(8,128)}, f32[4,2,4,144,256]{4,3,2,1,0:T(8,128)}, f3...) custom-call(bf16[128,1152]{1,0:T(8,128)(2,1)} %refs_0_.1, ...), custom_call_target="tpu_custom_call" | custom-call | tf_op jit(solution)/shard_map/pallas_call | solution.py:1183
  132.5 250.3 %shard_map.340 = (f32[144]{0:T(256)}, f32[144]{0:T(256)}, f32[144,256]{1,0:T(8,128)}, f32[36,512]{1,0:T(8,128)}, f32[144,256]{1,0:T(8,128)}, /*index=5*/f32[144,...) custom-call(f32[2,4,616,256]{3,2,1,0:T(8,128)} %get-tuple-element.70, ...), custom_call_target="tpu_custom_call" | custom-call | tf_op jit(solution)/shard_map/pallas_call | solution.py:1774
  382.8 5.0 %shard_map.341 = (bf16[128,1152]{1,0:T(8,128)(2,1)}, f32[128,1152]{1,0:T(8,128)}, f32[144]{0:T(256)}, f32[144]{0:T(256)}, f32[144,256]{1,0:T(8,128)}, /*index=5*...) custom-call(bf16[128,1152]{1,0:T(8,128)(2,1)} %get-tuple-element.68., ...), custom_call_target="tpu_custom_call" | custom-call | tf_op jit(solution)/shard_map/pallas_call | solution.py:1827
